TPU v7x, 256 devices: a whole 4x4x8 slice. The times are simulated.
256 devices in a mesh: scan: 64 (over y, z, core), mode: 4 (over x).
Axes of the slice: x: 4, y: 4, z: 8, core: 2. Of those that a mesh axis runs over, the one named last changes fastest.
Arguments:
- object_tiles: bfloat16 [512, 2, 2, 128, 128], P('scan'), may hold values from -5 to 5
- tile_owner: int32 [512], replicated, may hold values from 0 to 63, as said below
- block_tiles: int32 [64, 64], replicated, may hold values from 0 to 511, as said below
- positions: int32 [1024, 2], P('scan'), may hold values from 0 to 3968, as said below
- counts: int32 [1024, 128, 128], P('scan'), may hold values from 0 to 5
- probe: float32 [4, 2, 128, 128], P('mode'), may hold values from -3 to 3
Outputs:
- object_grad: float32 [512, 2, 2, 128, 128], P('scan', None, None, 'mode')
- probe_grad: float32 [4, 2, 128, 128], P('mode')
Inputs may be any that keep to these rules, and one draw needn't show every extreme that they name: `tile_owner`: each scan index owns exactly 8 tiles, and the 64 tiles of any one row of block_tiles have 64 different owners. `block_tiles`: row b holds the tiles of a window of 2 consecutive tile rows and 32 consecutive tile columns of an object of 32 tile columns (tile t in tile row t // 32, column t % 32); slot s is the window's tile in window row s // 32 and window column s % 32. `positions`: row offsets run from 0 to 128 and column offsets from 0 to 3968, so every patch lies inside its block's window.
All inputs are finite; a program needn't handle non-finite values.
Results may differ from a plain program's by a relative error of at most 0.00055.
Values may be sent and summed in bfloat16 or wider, within the bound.
A program may use at most 128 MiB of HBM per device.

v0:
```python
import jax
import jax.numpy as jnp
from jax import lax
from jax.sharding import PartitionSpec as P

background = 0.25
fresnel_number = 1.0
highest = lax.Precision.HIGHEST


def tables(pattern_side):
    index_range = jnp.arange(pattern_side, dtype=jnp.int32)
    product = index_range[:, None] * index_range[None, :] % pattern_side
    angles = 2.0 * jnp.pi / pattern_side * product.astype(jnp.float32)
    scaling = 1.0 / jnp.sqrt(jnp.float32(pattern_side))
    four_re = jnp.cos(angles) * scaling
    four_im = -jnp.sin(angles) * scaling
    frequency = (
        jnp.where(index_range < pattern_side // 2, index_range, index_range - pattern_side).astype(
            jnp.float32
        )
        / pattern_side
    )
    phases = -jnp.pi * fresnel_number * frequency * frequency
    chirp_re = jnp.cos(phases)
    chirp_im = jnp.sin(phases)
    left_re = four_re * chirp_re[None, :] + four_im * chirp_im[None, :]
    left_im = four_re * chirp_im[None, :] - four_im * chirp_re[None, :]
    prop_re = jnp.dot(left_re, four_re, precision=highest) - jnp.dot(
        left_im, four_im, precision=highest
    )
    prop_im = jnp.dot(left_re, four_im, precision=highest) + jnp.dot(
        left_im, four_re, precision=highest
    )
    return (four_re, four_im, prop_re, prop_im)


def two_sided(matrix_re, matrix_im, field_re, field_im):
    half_re = jnp.einsum("jk,bkl->bjl", matrix_re, field_re, precision=highest) - jnp.einsum(
        "jk,bkl->bjl", matrix_im, field_im, precision=highest
    )
    half_im = jnp.einsum("jk,bkl->bjl", matrix_re, field_im, precision=highest) + jnp.einsum(
        "jk,bkl->bjl", matrix_im, field_re, precision=highest
    )
    full_re = jnp.einsum("bjk,kl->bjl", half_re, matrix_re, precision=highest) - jnp.einsum(
        "bjk,kl->bjl", half_im, matrix_im, precision=highest
    )
    full_im = jnp.einsum("bjk,kl->bjl", half_re, matrix_im, precision=highest) + jnp.einsum(
        "bjk,kl->bjl", half_im, matrix_re, precision=highest
    )
    return (full_re, full_im)


def forward(probe_re, probe_im, obj_re, obj_im, dft_tables):
    four_re, four_im, prop_re, prop_im = dft_tables
    batch_size = obj_re.shape[1]
    wave_re = jnp.broadcast_to(probe_re, (batch_size,) + probe_re.shape)
    wave_im = jnp.broadcast_to(probe_im, (batch_size,) + probe_im.shape)
    waves = []
    depth_count = obj_re.shape[0]
    for depth_index in range(depth_count):
        waves.append((wave_re, wave_im))
        exit_re = wave_re * obj_re[depth_index] - wave_im * obj_im[depth_index]
        exit_im = wave_re * obj_im[depth_index] + wave_im * obj_re[depth_index]
        if depth_index + 1 < depth_count:
            wave_re, wave_im = two_sided(prop_re, prop_im, exit_re, exit_im)
        else:
            far_re, far_im = two_sided(four_re, four_im, exit_re, exit_im)
    return (waves, far_re, far_im)


def backward(waves, far_re, far_im, weight, obj_re, obj_im, dft_tables):
    four_re, four_im, prop_re, prop_im = dft_tables
    depth_count = obj_re.shape[0]
    grad_re, grad_im = two_sided(four_re, -four_im, weight * far_re, weight * far_im)
    terms_re = [None] * depth_count
    terms_im = [None] * depth_count
    for depth_index in reversed(range(depth_count)):
        wave_re, wave_im = waves[depth_index]
        terms_re[depth_index] = wave_re * grad_re + wave_im * grad_im
        terms_im[depth_index] = wave_re * grad_im - wave_im * grad_re
        back_re = obj_re[depth_index] * grad_re + obj_im[depth_index] * grad_im
        back_im = obj_re[depth_index] * grad_im - obj_im[depth_index] * grad_re
        if depth_index > 0:
            grad_re, grad_im = two_sided(prop_re, -prop_im, back_re, back_im)
    return (
        jnp.stack(terms_re),
        jnp.stack(terms_im),
        jnp.sum(back_re, axis=0),
        jnp.sum(back_im, axis=0),
    )


def shards(object_tiles, tile_owner, block_tiles, positions, counts, probe):
    scan_count = lax.axis_size("scan")
    scan_here = lax.axis_index("scan")
    window_span = scan_count // 2
    tile_dev = object_tiles.shape[0]
    depth_count = object_tiles.shape[1]
    pattern_side = probe.shape[-1]
    batch_size = positions.shape[0]
    dft_tables = tables(pattern_side)
    anchor_zero = jnp.int32(0)
    owner_range = jnp.arange(scan_count, dtype=jnp.int32)
    owner_hot = (tile_owner[:, None] == owner_range[None, :]).astype(jnp.int32)
    rank_all = jnp.sum((jnp.cumsum(owner_hot, axis=0) - owner_hot) * owner_hot, axis=1)
    list_owner = tile_owner[block_tiles]
    wanted = jnp.sum(jnp.where(list_owner == scan_here, block_tiles, 0), axis=1)
    local_rows = rank_all[wanted]
    outgoing = object_tiles[local_rows]
    my_tiles = lax.dynamic_index_in_dim(block_tiles, scan_here, 0, keepdims=False)
    my_owners = tile_owner[my_tiles]
    incoming = lax.all_to_all(outgoing, "scan", split_axis=0, concat_axis=0, tiled=True)
    slot_tiles = incoming[my_owners]
    window = (
        slot_tiles.reshape(2, window_span, depth_count, 2, pattern_side, pattern_side)
        .transpose(2, 3, 0, 4, 1, 5)
        .reshape(depth_count, 2, 2 * pattern_side, window_span * pattern_side)
    )

    def cut_patch(offset):
        return lax.dynamic_slice(
            window,
            (anchor_zero, anchor_zero, offset[0], offset[1]),
            (depth_count, 2, pattern_side, pattern_side),
        )

    patches = jax.vmap(cut_patch)(positions).astype(jnp.float32)
    obj_re = jnp.transpose(patches[:, :, 0], (1, 0, 2, 3))
    obj_im = jnp.transpose(patches[:, :, 1], (1, 0, 2, 3))
    mode_runs = forward(probe[0, 0], probe[0, 1], obj_re, obj_im, dft_tables)
    partial_sum = mode_runs[1] * mode_runs[1] + mode_runs[2] * mode_runs[2]
    intensity = lax.psum(partial_sum, "mode") + background
    weight = 1.0 - counts.astype(jnp.float32) / intensity
    terms_re, terms_im, probe_re, probe_im = backward(
        mode_runs[0], mode_runs[1], mode_runs[2], weight, obj_re, obj_im, dft_tables
    )
    probe_parts = [jnp.stack([probe_re, probe_im])]
    probe_grad = lax.psum(jnp.stack(probe_parts), "scan") / (batch_size * scan_count)
    terms = jnp.transpose(jnp.stack([terms_re, terms_im], axis=1), (2, 0, 1, 3, 4))

    def place(position, canvas):
        start = (anchor_zero, anchor_zero, positions[position, 0], positions[position, 1])
        current = lax.dynamic_slice(canvas, start, (depth_count, 2, pattern_side, pattern_side))
        return lax.dynamic_update_slice(canvas, current + terms[position], start)

    canvas = lax.fori_loop(
        0,
        batch_size,
        place,
        jnp.zeros((depth_count, 2, 2 * pattern_side, window_span * pattern_side), jnp.float32),
    )
    slot_grads = (
        canvas.reshape(depth_count, 2, 2, pattern_side, window_span, pattern_side)
        .transpose(2, 4, 0, 1, 3, 5)
        .reshape(scan_count, depth_count, 2, pattern_side, pattern_side)
    )
    slot_of_owner = jnp.sum(
        jnp.where(my_owners[None, :] == owner_range[:, None], owner_range[None, :], 0), axis=1
    )
    returning = slot_grads[slot_of_owner]
    tile_range = jnp.arange(tile_dev, dtype=jnp.int32)
    landing = (local_rows[None, :] == tile_range[:, None]).astype(jnp.float32)
    returned = lax.all_to_all(returning, "scan", split_axis=0, concat_axis=0, tiled=True)
    flattened = returned.reshape(returned.shape[0], -1)
    summed = jnp.dot(landing, flattened, precision=highest)
    object_grad = lax.psum_scatter(
        summed.reshape((tile_dev,) + returned.shape[1:]), "mode", scatter_dimension=3, tiled=True
    )
    return (object_grad, probe_grad)


def solution(mesh):
    placed = (
        P("scan", None, None, None, None),
        P(),
        P(),
        P("scan", None),
        P("scan", None, None),
        P("mode", None, None, None),
    )
    return jax.shard_map(
        shards,
        mesh=mesh,
        in_specs=placed,
        out_specs=(P("scan", None, None, "mode", None), P("mode", None, None, None)),
        check_vma=False,
    )
```

profile of v0, /device:TPU:1, one launch (start us, length us, event | category | flops | bytes accessed | tf_op | source)
XLA Modules:
  0.0 1114.8 jit_solution(17758570615037978540)
XLA Ops:
  8.1 25.9 %gather_fusion = s32[4096]{0:T(1024)S(1)} fusion(s32[512]{0:T(512)S(1)} %copy-done.2, s32[4096]{0:T(1024)S(1)} %broadcast_clamp_fusion), kind=kCustom, calls=%fused_computation | custom fusion | bytes 49152 | tf_op jit(solution)/shard_map/gather | solution.py:107
  36.7 5.5 gather_fusion.2
  42.3 13.4 %all-to-all-start = ((bf16[64,2,2,128,128]{4,3,2,1,0:T(8,128)(2,1)}), bf16[64,2,2,128,128]{4,3,2,1,0:T(8,128)(2,1)}, u32[]{:S(2)}, u32[]{:S(2)}) async-start(bf16[64,2,2,128,128]{4,3,2,1,0:T(8,128)(2,1)} %gather_fusion.2), calls=%async_computation | async-start | bytes 16777216 | tf_op jit(solution)/shard_map/all_to_all | solution.py:113
  59.3 182.2 %all-to-all-done = bf16[64,2,2,128,128]{4,3,2,1,0:T(8,128)(2,1)} async-done(((bf16[64,2,2,128,128]{4,3,2,1,0:T(8,128)(2,1)}), bf16[64,2,2,128,128]{4,3,2,1,0:T(8,128)(2,1)}, u32[]{:S(2)}, u32[]{:S(2)}) %all-to-all-start) | async-done | bytes 8388640 | tf_op jit(solution)/shard_map/all_to_all | solution.py:113
  241.5 8.9 gather_fusion.4
  250.4 12.0 %copy.216 = bf16[2,32,2,2,128,128]{5,1,4,0,3,2:T(8,128)(2,1)} copy(bf16[2,32,2,2,128,128]{5,4,3,2,1,0:T(8,128)(2,1)} %bitcast.301) | data formatting | bytes 16777216 | tf_op jit(solution)/shard_map/reshape | solution.py:116
  262.4 13.5 %reshape.137 = bf16[2,2,256,4096]{3,2,1,0:T(8,128)(2,1)} reshape(bf16[2,2,2,128,32,128]{5,4,3,2,1,0:T(8,128)(2,1)} %bitcast.302) | data formatting | bytes 16777216 | tf_op jit(solution)/shard_map/reshape | solution.py:118
  275.9 50.3 %while.15 = (s32[]{:T(128)}, bf16[2,2,256,4096]{3,2,1,0:T(8,128)(2,1)}, s32[16,4]{0,1:T(4,128)S(1)}, bf16[16,2,2,128,128]{4,3,0,1,2:T(8,128)(2,1)S(1)}, s32[]{:T(128)}) while((s32[]{:T(128)}, bf16[2,2,256,4096]{3,2,1,0:T(8,128)(2,1)}, s32[16,4]{0,1:T(4,128)S(1)}, bf16[16,2,2,128,128]{4,3,0,1,2:T(8,128)(2,1)S(1)}, s32[]{:T(128)}) %tuple.84), condition=%wide.while_cond, body=%wide.while_body.sunk | while | flops 2 | bytes 263793 | solution.py:122
  276.6 2.5 copy_dynamic-update-slice_fusion.2
  279.7 2.5 copy_dynamic-update-slice_fusion.2
  285.9 2.5 copy_dynamic-update-slice_fusion.2
  289.1 2.5 copy_dynamic-update-slice_fusion.2
  295.3 2.5 copy_dynamic-update-slice_fusion.2
  298.5 2.5 copy_dynamic-update-slice_fusion.2
  301.6 2.5 copy_dynamic-update-slice_fusion.2
  304.8 2.5 copy_dynamic-update-slice_fusion.2
  307.9 2.5 copy_dynamic-update-slice_fusion.2
  340.3 3.0 multiply_add_fusion.2
  357.4 3.4 multiply_add_fusion.1
  360.9 46.0 %all-reduce.3.cloned.1.call-done = f32[16,128,128]{2,1,0:T(8,128)} async-done(((f32[16,128,128]{2,1,0:T(8,128)}), f32[16,128,128]{2,1,0:T(8,128)}) %all-reduce.3.cloned.1.call-update) | async-done | bytes 1048592 | tf_op jit(solution)/shard_map/psum | solution.py:133
  408.6 3.3 fusion.16
  444.5 7.8 broadcast_in_dim.17
  452.3 153.9 %while.14 = (s32[]{:T(128)}, f32[2,2,256,4096]{3,2,1,0:T(8,128)}, s32[16,2]{0,1:T(2,128)S(1)}, f32[16,2,2,128,128]{4,3,0,1,2:T(8,128)}, s32[]{:T(128)}, /*index=5*/s32[]{:T(128)}, s32[]{:T(128)}, s32[]{:T(128)}) while((s32[]{:T(128)}, f32[2,2,256,4096]{3,2,1,0:T(8,128)}, s32[16,2]{0,1:T(2,128)S(1)}, f32[16,2,2,128,128]{4,3,0,1,2:T(8,128)}, ...), condition=%wide.region_6.7_spmd, body=%wide.region_5.6_spmd.sunk | while | flops 65544 | bytes 1311417 | solution.py:147
  458.0 4.3 dynamic_update_slice.8
  468.0 3.5 dynamic_update_slice.8
  484.7 3.6 dynamic_update_slice.8
  493.9 4.3 dynamic_update_slice.8
  503.9 3.2 dynamic_update_slice.8
  512.8 4.1 dynamic_update_slice.8
  522.5 4.3 dynamic_update_slice.8
  532.5 4.3 dynamic_update_slice.8
  542.5 4.3 dynamic_update_slice.8
  552.5 4.3 dynamic_update_slice.8
  562.4 4.3 dynamic_update_slice.8
  572.3 4.0 dynamic_update_slice.8
  581.9 4.3 dynamic_update_slice.8
  591.9 4.3 dynamic_update_slice.8
  601.9 4.3 dynamic_update_slice.8
  606.2 9.4 copy.200
  615.6 19.3 %copy.157 = f32[2,32,2,2,128,128]{5,4,3,2,1,0:T(8,128)} copy(f32[2,32,2,2,128,128]{5,1,4,0,3,2:T(8,128)S(1)} %bitcast.300) | data formatting | bytes 33554432 | tf_op jit(solution)/shard_map/transpose | solution.py:155
  634.9 14.6 %gather_fusion.5 = f32[64,2,2,128,128]{4,3,2,1,0:T(8,128)} fusion(f32[64,2,2,128,128]{4,3,2,1,0:T(8,128)} %bitcast.298, s32[1024]{0:T(1024)S(1)} %pad_clamp_fusion), kind=kCustom, calls=%fused_computation.5 | custom fusion | bytes 33554688 | tf_op jit(solution)/shard_map/gather | solution.py:161
  649.5 13.6 %all-to-all-start.1 = ((f32[64,2,2,128,128]{4,3,2,1,0:T(8,128)}), f32[64,2,2,128,128]{4,3,2,1,0:T(8,128)}, u32[]{:S(2)}, u32[]{:S(2)}) async-start(f32[64,2,2,128,128]{4,3,2,1,0:T(8,128)} %gather_fusion.5), calls=%async_computation.1 | async-start | bytes 33554432 | tf_op jit(solution)/shard_map/all_to_all | solution.py:164
  663.9 366.9 %all-to-all-done.1 = f32[64,2,2,128,128]{4,3,2,1,0:T(8,128)} async-done(((f32[64,2,2,128,128]{4,3,2,1,0:T(8,128)}), f32[64,2,2,128,128]{4,3,2,1,0:T(8,128)}, u32[]{:S(2)}, u32[]{:S(2)}) %all-to-all-start.1) | async-done | bytes 16777248 | tf_op jit(solution)/shard_map/all_to_all | solution.py:164
  1030.8 17.7 %copy.215 = f32[8,8,512,128]{3,1,2,0:T(8,128)} copy(f32[8,8,512,128]{3,2,1,0:T(8,128)} %bitcast.76) | data formatting | bytes 33554432
  1048.4 9.6 copy.202
  1058.1 15.2 %fusion.1 = f32[8,2,2,128,128]{4,0,3,2,1:T(8,128)S(1)} fusion(f32[2,2,128,128,64]{3,2,1,0,4:T(8,128)S(1)} %bitcast.299, s32[64]{0:T(128)S(1)} %gather_fusion.1), kind=kOutput, calls=%fused_computation.15 | convolution fusion | flops 402653696 | bytes 18874624 | tf_op jit(solution)/shard_map/dot_general | solution.py:166
  1073.6 3.0 copy.217
  1078.3 27.3 %reduce-scatter.5.cloned.1.call-done = f32[32,4096]{1,0:T(8,128)} async-done(((f32[128,4096]{1,0:T(8,128)}), f32[32,4096]{1,0:T(8,128)}) %reduce-scatter.5.cloned.1.call-update) | async-done | bytes 524304
  (185 shorter events, 133.7 us)
Async XLA Ops:
  7.2 29.6 %copy-start = (bf16[8,2,2,128,128]{4,3,2,1,0:T(8,128)(2,1)S(1)}, bf16[8,2,2,128,128]{4,3,2,1,0:T(8,128)(2,1)}, u32[]{:S(2)}) copy-start(bf16[8,2,2,128,128]{4,3,2,1,0:T(8,128)(2,1)} %param.8) | copy-start | bytes 3145732
  7.2 1.0 copy-start.2
  8.1 26.0 %copy-start.13 = (s32[64,64]{1,0:T(8,128)S(1)}, s32[64,64]{1,0:T(8,128)}, u32[]{:S(2)}) copy-start(s32[64,64]{1,0:T(8,128)} %param.10) | copy-start | bytes 49156
  42.2 15.9 %copy-start.14 = (s32[16,2]{0,1:T(2,128)S(1)}, s32[16,2]{0,1:T(2,128)}, u32[]{:S(2)}) copy-start(s32[16,2]{0,1:T(2,128)} %param.11) | copy-start | bytes 388
  42.3 199.2 %all-to-all-start = ((bf16[64,2,2,128,128]{4,3,2,1,0:T(8,128)(2,1)}), bf16[64,2,2,128,128]{4,3,2,1,0:T(8,128)(2,1)}, u32[]{:S(2)}, u32[]{:S(2)}) async-start(bf16[64,2,2,128,128]{4,3,2,1,0:T(8,128)(2,1)} %gather_fusion.2), calls=%async_computation | async-start | bytes 16777216 | tf_op jit(solution)/shard_map/all_to_all | solution.py:113
  55.7 3.5 copy-start.12
  55.7 351.2 %all-reduce.3.cloned.1.call-start = ((), (), s32[]{:S(2)}) async-start(), calls=%async_computation.3 | async-start | bytes 2097152 | tf_op jit(solution)/shard_map/psum | solution.py:133
  262.4 13.5 %copy-start.11 = (bf16[16,2,2,128,128]{4,3,0,1,2:T(8,128)(2,1)S(1)}, bf16[16,2,2,128,128]{4,3,0,1,2:T(8,128)(2,1)}, u32[]{:S(2)}) copy-start(bf16[16,2,2,128,128]{4,3,0,1,2:T(8,128)(2,1)} %custom-call.12) | copy-start | bytes 6291460
  327.3 13.0 %copy-start.3 = (f32[2,16,128,128]{3,2,1,0:T(8,128)}, f32[2,16,128,128]{3,2,1,0:T(8,128)S(1)}, u32[]{:S(2)}) copy-start(f32[2,16,128,128]{3,2,1,0:T(8,128)S(1)} %get-tuple-element.143) | copy-start | bytes 6291460
  340.3 3.0 copy-start.8
  357.4 3.4 copy-start.5
  408.6 3.3 copy-start.7
  416.1 3.9 copy-start.6
  420.0 4.0 copy-start.10
  422.0 2.0 copy-start.4
  422.0 2.0 copy-start.9
  649.5 381.2 %all-to-all-start.1 = ((f32[64,2,2,128,128]{4,3,2,1,0:T(8,128)}), f32[64,2,2,128,128]{4,3,2,1,0:T(8,128)}, u32[]{:S(2)}, u32[]{:S(2)}) async-start(f32[64,2,2,128,128]{4,3,2,1,0:T(8,128)} %gather_fusion.5), calls=%async_computation.1 | async-start | bytes 33554432 | tf_op jit(solution)/shard_map/all_to_all | solution.py:164
  663.1 413.5 %all-reduce.5.cloned.1.call-start = ((), (), s32[]{:S(2)}) async-start(), calls=%async_computation.4 | async-start | bytes 262144 | tf_op jit(solution)/shard_map/psum | solution.py:139
  663.9 441.7 %reduce-scatter.5.cloned.1.call-start = ((), (), s32[]{:S(2)}) async-start(), calls=%async_computation.5 | async-start | bytes 2621440
  1076.6 31.2 %copy-start.1 = (bf16[8,2,2,128,128]{4,3,2,1,0:T(8,128)(2,1)S(1)}, bf16[8,2,2,128,128]{4,3,2,1,0:T(8,128)(2,1)}, u32[]{:S(2)}) copy-start(bf16[8,2,2,128,128]{4,3,2,1,0:T(8,128)(2,1)} %param.8) | copy-start | bytes 3145732
Sparse Core Ops, SparseCore 0:
  360.9 45.9 all-reduce.2
  668.4 215.6 all-reduce.4
  1076.7 28.7 reduce-scatter.4
where the time goes:
time: 1120 us; the launch traced here: 1110 us
  waiting for transfers between devices  622 us (56%)
  local copies, waits for them, and re-layouts  275 us (25%)
  matrix products  83.5 us (7%)
  loops' own time  61.2 us (5%)
  other arithmetic  30.1 us (3%)
  starting transfers between devices  27.7 us (2%)
  between operations  14.8 us (1%)
    all_to_all x1, waiting for transfers between devices, shards(): lax.all_to_all(returning, 'scan', split_axis=0, concat_axis=0, tiled=True)  367 us
    all_to_all x1, waiting for transfers between devices, shards(): lax.all_to_all(outgoing, 'scan', split_axis=0, concat_axis=0, tiled=True)  182 us
    dynamic_update_slice x16, local copies, waits for them, and re-layouts, place(): return lax.dynamic_update_slice(canvas, current + terms[position], start)  63.4 us
    another operation x1, loops' own time, shards(): lax.fori_loop(0, batch_size, place, jnp.zeros((depth_count, 2, 2 * patter...  60.8 us
    gather x48, local copies, waits for them, and re-layouts  49.9 us
    psum x1, waiting for transfers between devices, shards(): intensity = lax.psum(partial_sum, 'mode') + background  46 us
    unnamed x37, local copies, waits for them, and re-layouts  42.2 us
    unnamed x4, waiting for transfers between devices  27.4 us
  transfers between devices with their start and end apart: 5, of which 4 were waited for; matrix products, arithmetic and copies ran while one was open for 5% of the time, Pallas kernels for 0%

commit v1 on v0

v1 whole, which is shorter than its diff:
```python
import functools

import jax
import jax.numpy as jnp
import ml_dtypes
import numpy as np
from jax import lax
from jax.experimental import pallas as pl
from jax.experimental.pallas import tpu as pltpu
from jax.sharding import PartitionSpec as P

background = 0.25
fresnel_number = 1.0
MIB = 1024 * 1024


def split_const(matrix):
    hi = matrix.astype(ml_dtypes.bfloat16)
    lo = (matrix - hi.astype(np.float64)).astype(ml_dtypes.bfloat16)
    return hi, lo


def transform_tables(side):
    index = np.arange(side)
    four = np.exp(-2j * np.pi * (index[:, None] * index[None, :] % side) / side) / np.sqrt(side)
    frequency = np.where(index < side // 2, index, index - side) / side
    chirp = np.exp(-1j * np.pi * fresnel_number * frequency * frequency)
    prop = (four.conj() * chirp[None, :]) @ four
    blocks = []
    for matrix in (four, prop):
        re, im = matrix.real, matrix.imag
        blocks.append(np.block([[re, im], [-im, re]]))
        blocks.append(np.block([[re, -im], [im, re]]))
    parts = []
    for block in blocks:
        parts.extend(split_const(block))
    return np.stack(parts)


def split_parts(value):
    hi = value.astype(jnp.bfloat16)
    lo = (value - hi.astype(jnp.float32)).astype(jnp.bfloat16)
    return hi, lo


def dot(a, b):
    return jnp.dot(a, b, preferred_element_type=jnp.float32)


def compute_kernel(rc_ref, q_ref, x_ref, probe_ref, counts_ref, tab_ref, e_ref, pg_ref, a_hi, a_lo, c_hi, c_lo, xs, p1, es):
    side = probe_ref.shape[-1]
    modes = probe_ref.shape[0]
    npos = x_ref.shape[1]
    quarter = x_ref.shape[3]
    nq = x_ref.shape[0]

    def block(m):
        return slice(m * side, (m + 1) * side)

    def two_sided(right, left, fields):
        for m, (re, im) in enumerate(fields):
            rh, rl = split_parts(re)
            ih, il = split_parts(im)
            a_hi[block(m), 0:side] = rh
            a_hi[block(m), side : 2 * side] = ih
            a_lo[block(m), 0:side] = rl
            a_lo[block(m), side : 2 * side] = il
        for m in range(modes):
            bh, bl = tab_ref[2 * right], tab_ref[2 * right + 1]
            y = dot(a_hi[block(m)], bh) + dot(a_lo[block(m)], bh) + dot(a_hi[block(m)], bl)
            hi, lo = split_parts(y)
            c_hi[0:side, block(m)] = hi[:, 0:side]
            c_hi[side : 2 * side, block(m)] = hi[:, side : 2 * side]
            c_lo[0:side, block(m)] = lo[:, 0:side]
            c_lo[side : 2 * side, block(m)] = lo[:, side : 2 * side]
        lh, ll = tab_ref[2 * left], tab_ref[2 * left + 1]
        out = []
        for h in range(modes // 2):
            cols = slice(h * 2 * side, (h + 1) * 2 * side)
            z = dot(lh, c_hi[:, cols]) + dot(lh, c_lo[:, cols]) + dot(ll, c_hi[:, cols])
            for k in range(2):
                out.append((z[0:side, block(k)], z[side : 2 * side, block(k)]))
        return out

    pg_ref[...] = jnp.zeros_like(pg_ref)

    def position(p, carry):
        row = rc_ref[p, 0]
        col = rc_ref[p, 1]
        for plane in range(4):
            whole = jnp.concatenate([x_ref[k, p, plane].astype(jnp.float32) for k in range(nq)], axis=0)
            whole = pltpu.roll(whole, (side - row) % side, 0)
            xs[plane] = pltpu.roll(whole, (side - col) % side, 1)
        fields = []
        for m in range(modes):
            pr, pi = probe_ref[m, 0], probe_ref[m, 1]
            xr, xi = xs[0], xs[1]
            fields.append((pr * xr - pi * xi, pr * xi + pi * xr))
        waves = two_sided(2, 3, fields)
        fields = []
        for m in range(modes):
            wr, wi = waves[m]
            p1[m, 0] = wr
            p1[m, 1] = wi
            xr, xi = xs[2], xs[3]
            fields.append((wr * xr - wi * xi, wr * xi + wi * xr))
        far = two_sided(0, 1, fields)
        intensity = background
        for re, im in far:
            intensity = intensity + (re * re + im * im)
        weight = 1.0 - counts_ref[p].astype(jnp.float32) / intensity
        grads = two_sided(1, 0, [(weight * re, weight * im) for re, im in far])
        fields = []
        er = ei = 0.0
        for m in range(modes):
            gr, gi = grads[m]
            wr, wi = p1[m, 0], p1[m, 1]
            er = er + (wr * gr + wi * gi)
            ei = ei + (wr * gi - wi * gr)
            xr, xi = xs[2], xs[3]
            fields.append((xr * gr + xi * gi, xr * gi - xi * gr))
        es[2] = er
        es[3] = ei
        grads = two_sided(3, 2, fields)
        er = ei = 0.0
        for m in range(modes):
            gr, gi = grads[m]
            wr, wi = probe_ref[m, 0], probe_ref[m, 1]
            er = er + (wr * gr + wi * gi)
            ei = ei + (wr * gi - wi * gr)
            xr, xi = xs[0], xs[1]
            pg_ref[m, 0] += xr * gr + xi * gi
            pg_ref[m, 1] += xr * gi - xi * gr
        es[0] = er
        es[1] = ei
        for plane in range(4):
            whole = pltpu.roll(pltpu.roll(es[plane], row, 0), col, 1)
            for k in range(nq):
                e_ref[k, p, plane] = whole[k * quarter : (k + 1) * quarter]
        return carry

    lax.fori_loop(0, npos, position, 0)


def compute(rc, q, x, probe_all, counts, tables):
    nq, npos, planes, quarter, side = x.shape
    modes = probe_all.shape[0]
    return pl.pallas_call(
        compute_kernel,
        grid_spec=pltpu.PrefetchScalarGridSpec(
            num_scalar_prefetch=2,
            grid=(1,),
            in_specs=[
                pl.BlockSpec(x.shape, lambda i, rc, q: (0, 0, 0, 0, 0)),
                pl.BlockSpec(probe_all.shape, lambda i, rc, q: (0, 0, 0, 0)),
                pl.BlockSpec((npos, side, side), lambda i, rc, q: (q[0], 0, 0)),
                pl.BlockSpec(tables.shape, lambda i, rc, q: (0, 0, 0)),
            ],
            out_specs=[
                pl.BlockSpec(x.shape, lambda i, rc, q: (0, 0, 0, 0, 0)),
                pl.BlockSpec(probe_all.shape, lambda i, rc, q: (0, 0, 0, 0)),
            ],
            scratch_shapes=[
                pltpu.VMEM((modes * side, 2 * side), jnp.bfloat16),
                pltpu.VMEM((modes * side, 2 * side), jnp.bfloat16),
                pltpu.VMEM((2 * side, modes * side), jnp.bfloat16),
                pltpu.VMEM((2 * side, modes * side), jnp.bfloat16),
                pltpu.VMEM((4, side, side), jnp.float32),
                pltpu.VMEM((modes, 2, side, side), jnp.float32),
                pltpu.VMEM((4, side, side), jnp.float32),
            ],
        ),
        out_shape=[
            jax.ShapeDtypeStruct(x.shape, jnp.float32),
            jax.ShapeDtypeStruct(probe_all.shape, jnp.float32),
        ],
        compiler_params=pltpu.CompilerParams(vmem_limit_bytes=40 * MIB),
        name="fields",
    )(rc, q, x, probe_all, counts, tables)


def residue_masks(row, col, first_row, shape):
    rows = lax.broadcasted_iota(jnp.int32, shape, len(shape) - 2) + first_row
    cols = lax.broadcasted_iota(jnp.int32, shape, len(shape) - 1)
    return rows >= row, cols >= col


def cut_kernel(place_ref, q_ref, win_ref, out_ref):
    quarter = win_ref.shape[2]

    def position(j, carry):
        up, left = residue_masks(place_ref[j, 4], place_ref[j, 5], q_ref[0] * quarter, win_ref.shape[1:])
        tiles = [win_ref[place_ref[j, k]].astype(jnp.float32) for k in range(4)]
        upper = jnp.where(left, tiles[0], tiles[1])
        lower = jnp.where(left, tiles[2], tiles[3])
        out_ref[j] = jnp.where(up, upper, lower).astype(jnp.bfloat16)
        return carry

    lax.fori_loop(0, out_ref.shape[0], position, 0)


def cut(place, q, window):
    npos = place.shape[0]
    return pl.pallas_call(
        cut_kernel,
        in_specs=[
            pl.BlockSpec(memory_space=pltpu.SMEM),
            pl.BlockSpec(memory_space=pltpu.SMEM),
            pl.BlockSpec(memory_space=pltpu.VMEM),
        ],
        out_specs=pl.BlockSpec(memory_space=pltpu.VMEM),
        out_shape=jax.ShapeDtypeStruct((npos,) + window.shape[1:], window.dtype),
        compiler_params=pltpu.CompilerParams(vmem_limit_bytes=32 * MIB),
        name="cut",
    )(place, q, window)


def lay_kernel(place_ref, q_ref, e_ref, out_ref):
    quarter = e_ref.shape[2]
    out_ref[...] = jnp.zeros_like(out_ref)

    def position(j, carry):
        up, left = residue_masks(place_ref[j, 4], place_ref[j, 5], q_ref[0] * quarter, e_ref.shape[1:])
        term = e_ref[j]
        upper = jnp.where(up, term, 0.0)
        lower = jnp.where(up, 0.0, term)
        out_ref[place_ref[j, 0]] += jnp.where(left, upper, 0.0)
        out_ref[place_ref[j, 1]] += jnp.where(left, 0.0, upper)
        out_ref[place_ref[j, 2]] += jnp.where(left, lower, 0.0)
        out_ref[place_ref[j, 3]] += jnp.where(left, 0.0, lower)
        return carry

    lax.fori_loop(0, e_ref.shape[0], position, 0)


def lay(place, q, terms, slots):
    return pl.pallas_call(
        lay_kernel,
        in_specs=[
            pl.BlockSpec(memory_space=pltpu.SMEM),
            pl.BlockSpec(memory_space=pltpu.SMEM),
            pl.BlockSpec(memory_space=pltpu.VMEM),
        ],
        out_specs=pl.BlockSpec(memory_space=pltpu.VMEM),
        out_shape=jax.ShapeDtypeStruct((slots,) + terms.shape[1:], terms.dtype),
        compiler_params=pltpu.CompilerParams(vmem_limit_bytes=32 * MIB),
        name="lay",
    )(place, q, terms)


def land_kernel(rows_ref, in_ref, out_ref):
    out_ref[...] = jnp.zeros_like(out_ref)

    def block(b, carry):
        out_ref[rows_ref[b]] += in_ref[b]
        return carry

    lax.fori_loop(0, in_ref.shape[0], block, 0)


def land(rows, returned, tile_dev):
    return pl.pallas_call(
        land_kernel,
        in_specs=[pl.BlockSpec(memory_space=pltpu.SMEM), pl.BlockSpec(memory_space=pltpu.VMEM)],
        out_specs=pl.BlockSpec(memory_space=pltpu.VMEM),
        out_shape=jax.ShapeDtypeStruct((tile_dev,) + returned.shape[1:], returned.dtype),
        compiler_params=pltpu.CompilerParams(vmem_limit_bytes=32 * MIB),
        name="land",
    )(rows, returned)


def shards(object_tiles, tile_owner, block_tiles, positions, counts, probe):
    scan_count = lax.axis_size("scan")
    mode_count = lax.axis_size("mode")
    scan_here = lax.axis_index("scan")
    mode_here = lax.axis_index("mode")
    tile_dev, slices, parts, side = object_tiles.shape[:4]
    batch = positions.shape[0]
    span = scan_count // 2
    quarter = side // mode_count
    npos = batch // mode_count
    planes = slices * parts
    tables = jnp.asarray(transform_tables(side))

    first = block_tiles[:, 0]
    tiles = tile_owner.shape[0]
    tile_range = jnp.arange(tiles, dtype=jnp.int32)
    same = (tile_owner[:, None] == tile_owner[None, :]) & (tile_range[None, :] < tile_range[:, None])
    rank = jnp.sum(same.astype(jnp.int32), axis=1)
    listed = (tile_range[None, :] >= first[:, None]) & (tile_range[None, :] < first[:, None] + scan_count)
    mine = listed & (tile_owner == scan_here)[None, :]
    local_rows = jnp.sum(jnp.where(mine, rank[None, :], 0), axis=1)
    my_first = lax.dynamic_index_in_dim(first, scan_here, 0, keepdims=False)
    slot_owner = lax.dynamic_slice(tile_owner, (my_first,), (scan_count,))
    q = mode_here.reshape(1)
    up, left = positions[:, 0] // side, positions[:, 1] // side
    down, right = jnp.minimum(up + 1, 1), jnp.minimum(left + 1, span - 1)
    slots = jnp.stack([up * span + left, up * span + right, down * span + left, down * span + right], axis=1)
    rc = positions % side
    place = jnp.concatenate([slot_owner[slots], rc], axis=1)

    part = lax.dynamic_slice_in_dim(object_tiles, mode_here * quarter, quarter, 3).reshape(
        tile_dev, planes, quarter, side
    )
    window = lax.all_to_all(part[local_rows], "scan", split_axis=0, concat_axis=0, tiled=True)
    pieces = cut(place, q, window)
    probe_all = lax.all_gather(probe, "mode", axis=0, tiled=True)
    x = lax.all_to_all(
        pieces.reshape(mode_count, npos, planes, quarter, side), "mode", split_axis=0, concat_axis=0, tiled=True
    )
    my_rc = lax.dynamic_slice_in_dim(rc, mode_here * npos, npos, 0)
    terms, probe_terms = compute(my_rc, q, x, probe_all, counts, tables)
    probe_part = lax.psum_scatter(probe_terms, "mode", scatter_dimension=0, tiled=True)
    probe_grad = lax.psum(probe_part, "scan") / (batch * scan_count)
    back = lax.all_to_all(terms, "mode", split_axis=0, concat_axis=0, tiled=True)
    canvas = lay(place, q, back.reshape(batch, planes, quarter, side), scan_count)
    returned = lax.all_to_all(canvas, "scan", split_axis=0, concat_axis=0, tiled=True)
    summed = land(local_rows, returned, tile_dev)
    return (summed.reshape(tile_dev, slices, parts, quarter, side), probe_grad)


def solution(mesh):
    placed = (
        P("scan", None, None, None, None),
        P(),
        P(),
        P("scan", None),
        P("scan", None, None),
        P("mode", None, None, None),
    )
    return jax.shard_map(
        shards,
        mesh=mesh,
        in_specs=placed,
        out_specs=(P("scan", None, None, "mode", None), P("mode", None, None, None)),
        check_vma=False,
    )
```

time: 1120 us -> 371 us (0.33)
  waiting for transfers between devices: 622 us -> 263 us
  local copies, waits for them, and re-layouts: 275 us -> 8.58 us
  matrix products: 83.5 us -> 0 us
  loops' own time: 61.2 us -> 0 us
  blocking collectives: 0 us -> 28.6 us
  other arithmetic: 30.1 us -> 4.49 us
  Pallas kernels: 0 us -> 20.2 us
    all_to_all x2 -> x3, waiting for transfers between devices: 549 us -> 46.7 us  [the longest x1 46.7 us: shards(): lax.all_to_all(part[local_rows], 'scan', split_axis=0, concat_axis=0, til...]
    psum x2 -> x1, waiting for transfers between devices: 46 us -> 190 us  [shards(): probe_grad = lax.psum(probe_part, 'scan') / (batch * scan_count)]
    gather x54 -> x3, local copies, waits for them, and re-layouts: 106 us -> 3.01 us  [the longest x1 2.16 us: shards(): part[local_rows]]
    dot_general x37 -> x0, matrix products: 83.5 us -> none  [the longest x1 15.2 us: shards(): summed = jnp.dot(landing, flattened, precision=highest)]
    dynamic_update_slice x16 -> x0, local copies, waits for them, and re-layouts: 63.4 us -> none  [place(): return lax.dynamic_update_slice(canvas, current + terms[position], start)]
    another operation x2 -> x0, loops' own time: 61.2 us -> none  [the longest x1 60.8 us: shards(): lax.fori_loop(0, batch_size, place, jnp.zeros((depth_count, 2, 2 * patter...]
    unnamed x37 -> x15, local copies, waits for them, and re-layouts: 42.2 us -> 4.08 us
    unnamed x4 -> x2, waiting for transfers between devices: 27.4 us -> 0.7 us
  transfers between devices with their start and end apart: 5 -> 5, of which waited for: 4 -> 3; matrix products, arithmetic and copies ran while one was open for 5% -> 1% of each run, Pallas kernels for 0% -> 0%
where the time goes in v1:
time: 371 us; the launch traced here: 370 us
  waiting for transfers between devices  263 us (71%)
  starting transfers between devices  29.5 us (8%)
  blocking collectives  28.6 us (8%)
  Pallas kernels  20.2 us (5%)
  between operations  16.1 us (4%)
  local copies, waits for them, and re-layouts  8.58 us (2%)
  other arithmetic  4.49 us (1%)
    psum x1, waiting for transfers between devices, shards(): probe_grad = lax.psum(probe_part, 'scan') / (batch * scan_count)  190 us
    all_to_all x1, waiting for transfers between devices, shards(): lax.all_to_all(part[local_rows], 'scan', split_axis=0, concat_axis=0, til...  46.7 us
    reduce_scatter x1, waiting for transfers between devices, shards(): lax.psum_scatter(probe_terms, 'mode', scatter_dimension=0, tiled=True)  24.9 us
    all_gather x1, blocking collectives, shards(): probe_all = lax.all_gather(probe, 'mode', axis=0, tiled=True)  14.3 us
    all_to_all x1, blocking collectives, shards(): lax.all_to_all(terms, 'mode', split_axis=0, concat_axis=0, tiled=True)  14.3 us
    pallas_call x1, Pallas kernels, compute(): pl.pallas_call(compute_kernel, grid_spec=pltpu.PrefetchScalarGridSpec(num...  13.9 us
    all_to_all x1, starting transfers between devices, shards(): lax.all_to_all(part[local_rows], 'scan', split_axis=0, concat_axis=0, til...  13.3 us
    all_to_all x1, starting transfers between devices, shards(): lax.all_to_all(canvas, 'scan', split_axis=0, concat_axis=0, tiled=True)  12 us
  transfers between devices with their start and end apart: 5, of which 3 were waited for; matrix products, arithmetic and copies ran while one was open for 1% of the time, Pallas kernels for 0%

profile of v1, /device:TPU:1, one launch (start us, length us, event | category | flops | bytes accessed | tf_op | source)
XLA Modules:
  0.0 370.0 jit_solution(3791509849683571238)
XLA Ops:
  7.2 0.0 copy-start
  7.2 1.0 convert_reduce_fusion
  8.2 0.7 broadcast_compare_fusion
  8.9 0.9 slice_reduce_fusion
  9.8 0.2 select_reduce_fusion.rows_ref
  10.0 0.0 copy-done
  10.1 2.2 gather_fusion.1
  12.2 0.0 copy-start.6
  12.2 13.3 %all-to-all-start = ((bf16[64,4,32,128]{3,2,1,0:T(8,128)(2,1)}), bf16[64,4,32,128]{3,2,1,0:T(8,128)(2,1)S(1)}, u32[]{:S(2)}, u32[]{:S(2)}) async-start(bf16[64,4,32,128]{3,2,1,0:T(8,128)(2,1)} %gather_fusion.1), calls=%async_computation | async-start | bytes 4194304 | tf_op jit(solution)/shard_map/all_to_all | solution.py:305
  25.5 0.0 copy-done.6
  25.5 0.1 copy.22
  25.6 0.1 copy.21
  25.7 0.1 reshape.202
  25.8 0.5 constant_dynamic-slice_fusion.2
  28.3 0.8 dynamic_slice.14
  29.0 0.8 gather_fusion
  29.8 0.0 copy-start.5
  29.8 0.1 reshape.201
  29.9 0.1 pad_add_fusion.place_ref
  30.0 46.7 %all-to-all-done.win_ref = bf16[64,4,32,128]{3,2,1,0:T(8,128)(2,1)S(1)} async-done(((bf16[64,4,32,128]{3,2,1,0:T(8,128)(2,1)}), bf16[64,4,32,128]{3,2,1,0:T(8,128)(2,1)S(1)}, u32[]{:S(2)}, u32[]{:S(2)}) %all-to-all-start) | async-done | bytes 2097184 | tf_op jit(solution)/shard_map/all_to_all | solution.py:305
  76.8 1.1 cut.1
  77.8 0.0 copy-start.2
  77.8 0.8 copy-done.2
  78.6 0.0 copy-start.3
  78.6 4.1 %all-to-all-start.1 = ((bf16[4,4,4,32,128]{4,3,2,1,0:T(8,128)(2,1)}), bf16[4,4,4,32,128]{4,3,2,1,0:T(8,128)(2,1)S(1)}, u32[]{:S(2)}, u32[]{:S(2)}) async-start(bf16[4,4,4,32,128]{4,3,2,1,0:T(8,128)(2,1)} %bitcast.21), calls=%async_computation.1 | async-start | bytes 1048576 | tf_op jit(solution)/shard_map/all_to_all | solution.py:308
  82.8 0.0 copy-done.5
  82.8 14.3 %all_gather.3.probe_ref = f32[4,2,128,128]{3,2,1,0:T(8,128)S(1)} all-gather(f32[1,2,128,128]{3,2,1,0:T(8,128)S(1)} %copy-done.5), channel_id=1, replica_groups=mesh['scan'=64,'mode'=4] {'mode'}, dimensions={0}, use_global_device_ids=true | all-gather | bytes 655360 | tf_op jit(solution)/shard_map/all_gather | solution.py:307
  97.1 0.0 all-to-all-done.1.x_ref
  97.1 0.0 copy-done.3
  97.1 0.0 copy-start.4
  97.1 1.2 copy-done.4
  98.3 13.9 %fields.1 = (f32[4,4,4,32,128]{4,3,2,1,0:T(8,128)S(1)}, f32[4,2,128,128]{3,2,1,0:T(8,128)}) custom-call(s32[4,2]{1,0:T(4,128)S(1)} %constant_dynamic-slice_fusion.1.rc_ref, s32[1]{0:T(128)} %bitcast.5.q_ref, bf16[4,4,4,32,128]{4,3,2,1,0:T(8,128)(2,1)S(1)} %all-to-all-done.1.x_ref, f32[4,2,128,128]{3,2,1,0:T(8,128)S(1)} %all_gather.3.probe_ref, ...), custom_call_target="tpu_custom_call" | custom-call | tf_op jit(solution)/shard_map/fields/pallas_call | solution.py:148
  112.2 14.3 %all_to_all.20 = f32[4,4,4,32,128]{4,3,2,1,0:T(8,128)S(1)} all-to-all(f32[4,4,4,32,128]{4,3,2,1,0:T(8,128)S(1)} %get-tuple-element.4), channel_id=1, replica_groups=mesh['scan'=64,'mode'=4] {'mode'}, dimensions={0} | all-to-all | bytes 2097152 | tf_op jit(solution)/shard_map/all_to_all | solution.py:315
  126.5 1.5 lay.1
  128.0 0.0 copy-start.1
  128.1 2.0 copy-done.1
  130.0 12.0 %all-to-all-start.3 = ((f32[64,4,32,128]{3,2,1,0:T(8,128)}), f32[64,4,32,128]{3,2,1,0:T(8,128)}, u32[]{:S(2)}, u32[]{:S(2)}) async-start(f32[64,4,32,128]{3,2,1,0:T(8,128)} %copy-done.1), calls=%async_computation.3 | async-start | bytes 8388608 | tf_op jit(solution)/shard_map/all_to_all | solution.py:317
  142.0 0.0 reduce-scatter.2.cloned.1.call-start
  142.1 0.7 reduce-scatter.2.cloned.1.call-update
  142.7 0.0 all-reduce.2.cloned.1.call-start
  142.8 24.9 %reduce-scatter.2.cloned.1.call-done = f32[1,2,128,128]{3,2,1,0:T(8,128)} async-done(((f32[4,2,128,128]{3,2,1,0:T(8,128)}), f32[1,2,128,128]{3,2,1,0:T(8,128)}) %reduce-scatter.2.cloned.1.call-update) | async-done | bytes 131088 | tf_op jit(solution)/shard_map/reduce_scatter | solution.py:313
  167.7 0.0 all-reduce.2.cloned.1.call-update
  167.7 190.2 %all-reduce.2.cloned.1.call-done = f32[1,2,128,128]{3,2,1,0:T(8,128)} async-done(((f32[1,2,128,128]{3,2,1,0:T(8,128)}), f32[1,2,128,128]{3,2,1,0:T(8,128)}) %all-reduce.2.cloned.1.call-update) | async-done | bytes 131088 | tf_op jit(solution)/shard_map/psum | solution.py:314
  357.9 1.6 broadcast_multiply_fusion
  359.5 0.0 all-to-all-done.3.in_ref
  359.5 3.7 land.1
  (9 shorter events, 0.1 us)
Async XLA Ops:
  7.2 2.8 copy-start
  12.2 13.3 %copy-start.6 = (s32[16,2]{0,1:T(2,128)S(1)}, s32[16,2]{0,1:T(2,128)}, u32[]{:S(2)}) copy-start(s32[16,2]{0,1:T(2,128)} %param.10) | copy-start | bytes 388
  12.2 64.5 %all-to-all-start = ((bf16[64,4,32,128]{3,2,1,0:T(8,128)(2,1)}), bf16[64,4,32,128]{3,2,1,0:T(8,128)(2,1)S(1)}, u32[]{:S(2)}, u32[]{:S(2)}) async-start(bf16[64,4,32,128]{3,2,1,0:T(8,128)(2,1)} %gather_fusion.1), calls=%async_computation | async-start | bytes 4194304 | tf_op jit(solution)/shard_map/all_to_all | solution.py:305
  29.8 52.9 %copy-start.5 = (f32[1,2,128,128]{3,2,1,0:T(8,128)S(1)}, f32[1,2,128,128]{3,2,1,0:T(8,128)}, u32[]{:S(2)}) copy-start(f32[1,2,128,128]{3,2,1,0:T(8,128)} %param.12) | copy-start | bytes 393220
  77.8 0.8 copy-start.2
  78.6 18.5 %copy-start.3 = (s32[16,128,128]{2,1,0:T(8,128)S(1)}, s32[16,128,128]{2,1,0:T(8,128)}, u32[]{:S(2)}) copy-start(s32[16,128,128]{2,1,0:T(8,128)} %counts_ref.1) | copy-start | bytes 3145732
  78.6 18.5 %all-to-all-start.1 = ((bf16[4,4,4,32,128]{4,3,2,1,0:T(8,128)(2,1)}), bf16[4,4,4,32,128]{4,3,2,1,0:T(8,128)(2,1)S(1)}, u32[]{:S(2)}, u32[]{:S(2)}) async-start(bf16[4,4,4,32,128]{4,3,2,1,0:T(8,128)(2,1)} %bitcast.21), calls=%async_computation.1 | async-start | bytes 1048576 | tf_op jit(solution)/shard_map/all_to_all | solution.py:308
  97.1 1.2 copy-start.4
  128.0 2.0 copy-start.1
  130.0 229.5 %all-to-all-start.3 = ((f32[64,4,32,128]{3,2,1,0:T(8,128)}), f32[64,4,32,128]{3,2,1,0:T(8,128)}, u32[]{:S(2)}, u32[]{:S(2)}) async-start(f32[64,4,32,128]{3,2,1,0:T(8,128)} %copy-done.1), calls=%async_computation.3 | async-start | bytes 8388608 | tf_op jit(solution)/shard_map/all_to_all | solution.py:317
  142.0 25.7 %reduce-scatter.2.cloned.1.call-start = ((), (), s32[]{:S(2)}) async-start(), calls=%async_computation.5 | async-start | bytes 655360 | tf_op jit(solution)/shard_map/reduce_scatter | solution.py:313
  142.7 215.2 %all-reduce.2.cloned.1.call-start = ((), (), s32[]{:S(2)}) async-start(), calls=%async_computation.6 | async-start | bytes 262144 | tf_op jit(solution)/shard_map/psum | solution.py:314
Sparse Core Ops, SparseCore 0:
  145.9 21.6 reduce-scatter.1
  171.1 186.7 all-reduce.1

commit v2 on v1

--- a/solution.py
+++ b/solution.py
@@ -12,6 +12,7 @@
 background = 0.25
 fresnel_number = 1.0
 MIB = 1024 * 1024
+RING = 8
 
 
 def split_const(matrix):
@@ -85,8 +86,8 @@
     pg_ref[...] = jnp.zeros_like(pg_ref)
 
     def position(p, carry):
-        row = rc_ref[p, 0]
-        col = rc_ref[p, 1]
+        row = rc_ref[q_ref[0] * npos + p, 4]
+        col = rc_ref[q_ref[0] * npos + p, 5]
         for plane in range(4):
             whole = jnp.concatenate([x_ref[k, p, plane].astype(jnp.float32) for k in range(nq)], axis=0)
             whole = pltpu.roll(whole, (side - row) % side, 0)
@@ -185,36 +186,6 @@
     return rows >= row, cols >= col
 
 
-def cut_kernel(place_ref, q_ref, win_ref, out_ref):
-    quarter = win_ref.shape[2]
-
-    def position(j, carry):
-        up, left = residue_masks(place_ref[j, 4], place_ref[j, 5], q_ref[0] * quarter, win_ref.shape[1:])
-        tiles = [win_ref[place_ref[j, k]].astype(jnp.float32) for k in range(4)]
-        upper = jnp.where(left, tiles[0], tiles[1])
-        lower = jnp.where(left, tiles[2], tiles[3])
-        out_ref[j] = jnp.where(up, upper, lower).astype(jnp.bfloat16)
-        return carry
-
-    lax.fori_loop(0, out_ref.shape[0], position, 0)
-
-
-def cut(place, q, window):
-    npos = place.shape[0]
-    return pl.pallas_call(
-        cut_kernel,
-        in_specs=[
-            pl.BlockSpec(memory_space=pltpu.SMEM),
-            pl.BlockSpec(memory_space=pltpu.SMEM),
-            pl.BlockSpec(memory_space=pltpu.VMEM),
-        ],
-        out_specs=pl.BlockSpec(memory_space=pltpu.VMEM),
-        out_shape=jax.ShapeDtypeStruct((npos,) + window.shape[1:], window.dtype),
-        compiler_params=pltpu.CompilerParams(vmem_limit_bytes=32 * MIB),
-        name="cut",
-    )(place, q, window)
-
-
 def lay_kernel(place_ref, q_ref, e_ref, out_ref):
     quarter = e_ref.shape[2]
     out_ref[...] = jnp.zeros_like(out_ref)
@@ -248,75 +219,405 @@
     )(place, q, terms)
 
 
-def land_kernel(rows_ref, in_ref, out_ref):
-    out_ref[...] = jnp.zeros_like(out_ref)
-
-    def block(b, carry):
-        out_ref[rows_ref[b]] += in_ref[b]
+def spot(scan):
+    return scan // (2 * RING), scan // 2 % RING, scan % 2
+
+
+def at_spot(y, z, core):
+    return (y * RING + z) * 2 + core
+
+
+def plane_peers(y, z, core):
+    peers = []
+    for number in range(1, 8):
+        there_y, there_core = (y + number // 2) % 4, (core + number % 2) % 2
+        peers.append((number - 1, at_spot(there_y, z, there_core), there_y * 2 + there_core))
+    return peers
+
+
+def plane_sources(y, core):
+    return [(y - number // 2 + 4) % 4 * 2 + (core + number % 2) % 2 for number in range(1, 8)]
+
+
+def send(src, dst, send_sem, recv_sem, scan, mode):
+    return pltpu.make_async_remote_copy(
+        src_ref=src,
+        dst_ref=dst,
+        send_sem=send_sem,
+        recv_sem=recv_sem,
+        device_id={"scan": scan, "mode": mode},
+        device_id_type=pl.DeviceIdType.MESH,
+    )
+
+
+def meet(partners):
+    barrier = pltpu.get_barrier_semaphore()
+    for scan, mode in partners:
+        pl.semaphore_signal(
+            barrier, inc=1, device_id={"scan": scan, "mode": mode}, device_id_type=pl.DeviceIdType.MESH
+        )
+    pl.semaphore_wait(barrier, len(partners))
+
+
+def gather_kernel(sel_ref, place_ref, obj_ref, probe_ref, x_ref, pall_ref, a0, a1, a2, a3, b1, b2, b3, h4, win, ybuf, xbuf, own_sem, zs, zr, ys, yr, xs, xr, ps, pr):
+    here, q = lax.axis_index("scan"), lax.axis_index("mode")
+    y, z, core = spot(here)
+    mine = y * 2 + core
+    quarter = a0.shape[2]
+    half = a0.shape[0] // 2
+    modes, npos = x_ref.shape[:2]
+    own = pltpu.make_async_copy(obj_ref.at[:, :, pl.ds(q * quarter, quarter), :], a0, own_sem)
+    own.start()
+    right, left = at_spot(y, (z + 1) % RING, core), at_spot(y, (z + RING - 1) % RING, core)
+    peers = plane_peers(y, z, core)
+    sources = plane_sources(y, core)
+    others = [(q + k) % modes for k in range(1, modes)]
+    meet([(right, q), (left, q)] + [(scan, q) for _, scan, _ in peers] + [(here, m) for m in others])
+    own.wait()
+
+    sends = []
+
+    def go(copy):
+        copy.start()
+        sends.append(copy)
+        return copy
+
+    def offer(buf, r, zi):
+        for n, scan, d in peers:
+            ybuf[n, r] = buf[sel_ref[d, zi]]
+            go(send(ybuf.at[n, r], win.at[mine * RING + zi], ys.at[n, r], yr.at[n, r], scan, q))
+        win[mine * RING + zi] = buf[sel_ref[mine, zi]]
+
+    to_right = go(send(a0, a1, zs.at[0, 0], zr.at[0, 0], right, q))
+    to_left = go(send(a0, b1, zs.at[1, 0], zr.at[1, 0], left, q))
+    shared = []
+    for k, m in enumerate(others):
+        shared.append(go(send(probe_ref.at[0], pall_ref.at[q], ps.at[k], pr.at[k], here, m)))
+    pall_ref[q] = probe_ref[0]
+    chunks = [(0, z)]
+    offer(a0, 0, z)
+    for step, (a, a_next, b, b_next) in enumerate(((a1, a2, b1, b2), (a2, a3, b2, b3), (a3, h4, b3, h4)), 1):
+        last = step == 3
+        to_right.wait_recv()
+        if last:
+            a, a_next = a.at[:half], a_next.at[:half]
+        to_right = go(send(a, a_next, zs.at[0, step], zr.at[0, step], right, q))
+        to_left.wait_recv()
+        if last:
+            b, b_next = b.at[half:], b_next.at[half:]
+        to_left = go(send(b, b_next, zs.at[1, step], zr.at[1, step], left, q))
+        behind, ahead = (z + RING - step) % RING, (z + step) % RING
+        offer((a1, a2, a3)[step - 1], 2 * step - 1, behind)
+        offer((b1, b2, b3)[step - 1], 2 * step, ahead)
+        chunks.extend([(2 * step - 1, behind), (2 * step, ahead)])
+    to_right.wait_recv()
+    to_left.wait_recv()
+    opposite = (z + 4) % RING
+    offer(h4, 7, opposite)
+    chunks.append((7, opposite))
+    for r, zi in chunks:
+        for n, source in enumerate(sources):
+            send(ybuf.at[n, r], win.at[source * RING + zi], ys.at[n, r], yr.at[n, r], here, q).wait_recv()
+
+    def piece(j):
+        up, left_side = residue_masks(place_ref[j, 4], place_ref[j, 5], q * quarter, win.shape[1:])
+        tiles = [win[place_ref[j, k]].astype(jnp.float32) for k in range(4)]
+        upper = jnp.where(left_side, tiles[0], tiles[1])
+        lower = jnp.where(left_side, tiles[2], tiles[3])
+        return jnp.where(up, upper, lower).astype(jnp.bfloat16)
+
+    arrivals = []
+    for k, m in enumerate(others):
+
+        def pack(i, carry, k=k, m=m):
+            xbuf[k, i] = piece(m * npos + i)
+            return carry
+
+        lax.fori_loop(0, npos, pack, 0)
+        go(send(xbuf.at[k], x_ref.at[q], xs.at[k], xr.at[k], here, m))
+
+    def keep(i, carry):
+        x_ref[q, i] = piece(q * npos + i)
         return carry
 
-    lax.fori_loop(0, in_ref.shape[0], block, 0)
-
-
-def land(rows, returned, tile_dev):
+    lax.fori_loop(0, npos, keep, 0)
+    for k in range(modes - 1):
+        source = (q + modes - 1 - k) % modes
+        send(xbuf.at[k], x_ref.at[source], xs.at[k], xr.at[k], here, q).wait_recv()
+        send(probe_ref.at[0], pall_ref.at[source], ps.at[k], pr.at[k], here, q).wait_recv()
+    for copy in sends:
+        copy.wait_send()
+
+
+def gather(sel, place, tiles, probe, modes):
+    tile_dev, planes, side, _ = tiles.shape
+    quarter = side // modes
+    npos = place.shape[0] // modes
+    chunk = pltpu.VMEM((tile_dev, planes, quarter, side), tiles.dtype)
+    dma = pltpu.SemaphoreType.DMA
     return pl.pallas_call(
-        land_kernel,
-        in_specs=[pl.BlockSpec(memory_space=pltpu.SMEM), pl.BlockSpec(memory_space=pltpu.VMEM)],
-        out_specs=pl.BlockSpec(memory_space=pltpu.VMEM),
-        out_shape=jax.ShapeDtypeStruct((tile_dev,) + returned.shape[1:], returned.dtype),
-        compiler_params=pltpu.CompilerParams(vmem_limit_bytes=32 * MIB),
-        name="land",
-    )(rows, returned)
+        gather_kernel,
+        in_specs=[
+            pl.BlockSpec(memory_space=pltpu.SMEM),
+            pl.BlockSpec(memory_space=pltpu.SMEM),
+            pl.BlockSpec(memory_space=pl.ANY),
+            pl.BlockSpec(memory_space=pltpu.VMEM),
+        ],
+        out_specs=[pl.BlockSpec(memory_space=pltpu.VMEM), pl.BlockSpec(memory_space=pltpu.VMEM)],
+        out_shape=[
+            jax.ShapeDtypeStruct((modes, npos, planes, quarter, side), tiles.dtype),
+            jax.ShapeDtypeStruct((modes,) + probe.shape[1:], probe.dtype),
+        ],
+        scratch_shapes=[chunk] * 8
+        + [
+            pltpu.VMEM((8 * RING, planes, quarter, side), tiles.dtype),
+            pltpu.VMEM((7, RING, planes, quarter, side), tiles.dtype),
+            pltpu.VMEM((modes - 1, npos, planes, quarter, side), tiles.dtype),
+            dma(()),
+            dma((2, 4)),
+            dma((2, 4)),
+            dma((7, 8)),
+            dma((7, 8)),
+            dma((modes - 1,)),
+            dma((modes - 1,)),
+            dma((modes - 1,)),
+            dma((modes - 1,)),
+        ],
+        compiler_params=pltpu.CompilerParams(
+            collective_id=0, has_side_effects=True, vmem_limit_bytes=40 * MIB
+        ),
+        name="gather",
+    )(sel, place, tiles, probe)
+
+
+def swap_kernel(e_ref, pg_ref, eq_ref, pr_ref, pbuf, es, er, ps, pr):
+    here, q = lax.axis_index("scan"), lax.axis_index("mode")
+    modes = e_ref.shape[0]
+    others = [(q + k) % modes for k in range(1, modes)]
+    meet([(here, m) for m in others])
+    sends = []
+    for k, m in enumerate(others):
+        sends.append(send(pg_ref.at[m], pbuf.at[k], ps.at[k], pr.at[k], here, m))
+    for k, m in enumerate(others):
+        sends.append(send(e_ref.at[m], eq_ref.at[q], es.at[k], er.at[k], here, m))
+    for copy in sends:
+        copy.start()
+    eq_ref[q] = e_ref[q]
+    for k in range(modes - 1):
+        sends[k].wait_recv()
+    total = pg_ref[q]
+    for k in range(modes - 1):
+        total = total + pbuf[k]
+    pr_ref[...] = total
+    for k in range(modes - 1):
+        source = (q + modes - 1 - k) % modes
+        send(e_ref.at[q], eq_ref.at[source], es.at[k], er.at[k], here, q).wait_recv()
+    for copy in sends:
+        copy.wait_send()
+
+
+def swap(terms, probe_terms):
+    modes = terms.shape[0]
+    dma = pltpu.SemaphoreType.DMA((modes - 1,))
+    vmem = pl.BlockSpec(memory_space=pltpu.VMEM)
+    return pl.pallas_call(
+        swap_kernel,
+        in_specs=[vmem, vmem],
+        out_specs=[vmem, vmem],
+        out_shape=[
+            jax.ShapeDtypeStruct(terms.shape, terms.dtype),
+            jax.ShapeDtypeStruct(probe_terms.shape[1:], probe_terms.dtype),
+        ],
+        scratch_shapes=[pltpu.VMEM((modes - 1,) + probe_terms.shape[1:], probe_terms.dtype), dma, dma, dma, dma],
+        compiler_params=pltpu.CompilerParams(
+            collective_id=1, has_side_effects=True, vmem_limit_bytes=32 * MIB
+        ),
+        name="swap",
+    )(terms, probe_terms)
+
+
+def return_kernel(hot_ref, canvas, pr_ref, out_ref, pg_ref, rbuf, sr0, sr1, sr2, sr3, sl0, sl1, sl2, sl3, rr0, rr1, rr2, rr3, rl0, rl1, rl2, rl3, pyb, pzs, pzb, zs, zr, ys, yr, p1s, p1r, p2s, p2r, p3s, p3r, scale=1.0):
+    here, q = lax.axis_index("scan"), lax.axis_index("mode")
+    y, z, core = spot(here)
+    mine = y * 2 + core
+    half = out_ref.shape[0] // 2
+    tile_dev = out_ref.shape[0]
+    right, left = at_spot(y, (z + 1) % RING, core), at_spot(y, (z + RING - 1) % RING, core)
+    peers = plane_peers(y, z, core)
+    sources = plane_sources(y, core)
+    column = [at_spot(y, (z + k) % RING, core) for k in range(1, RING)]
+    meet([(scan, q) for scan in column] + [(scan, q) for _, scan, _ in peers])
+    sends = []
+
+    def go(copy):
+        copy.start()
+        sends.append(copy)
+        return copy
+
+    def zi(offset):
+        return (z + offset + RING) % RING
+
+    def yield_up(r, offset):
+        for n, scan, d in peers:
+            go(send(canvas.at[d * RING + zi(offset)], rbuf.at[mine * RING + zi(offset)], ys.at[n, r], yr.at[n, r], scan, q))
+
+    def await_up(r, offset):
+        for n, source in enumerate(sources):
+            at = source * RING + zi(offset)
+            send(canvas.at[at], rbuf.at[at], ys.at[n, r], yr.at[n, r], here, q).wait_recv()
+
+    def combine(offset, tiles, into, received):
+        place = zi(offset)
+
+        def plane(l, carry):
+            terms = [canvas[mine * RING + place, l]]
+            terms.extend(rbuf[source * RING + place, l] for source in sources)
+            for at, k in enumerate(tiles):
+                total = hot_ref[(mine * RING + place) * tile_dev + k] * terms[0]
+                for source, term in zip(sources, terms[1:]):
+                    total = total + hot_ref[(source * RING + place) * tile_dev + k] * term
+                for ref, first in received:
+                    if first <= k < first + ref.shape[0]:
+                        total = total + ref[k - first, l]
+                into[at, l] = total
+            return carry
+
+        lax.fori_loop(0, into.shape[1], plane, 0)
+
+    for n, scan, d in peers:
+        go(send(pr_ref.at[d], pyb.at[n], p1s.at[n], p1r.at[n], scan, q))
+    yield_up(0, 4)
+    yield_up(1, 3)
+    yield_up(2, -3)
+    total = pr_ref[mine]
+    for n, source in enumerate(sources):
+        send(pr_ref.at[source], pyb.at[n], p1s.at[n], p1r.at[n], here, q).wait_recv()
+        total = total + pyb[n]
+    pzs[...] = total
+    for k, scan in enumerate(column):
+        go(send(pzs, pzb.at[k], p2s.at[k], p2r.at[k], scan, q))
+    await_up(0, 4)
+    low, high = range(half), range(half, tile_dev)
+    combine(4, low, sr0, [])
+    to_right = go(send(sr0, rr0, zs.at[0, 0], zr.at[0, 0], right, q))
+    combine(4, high, sl0, [])
+    to_left = go(send(sl0, rl0, zs.at[1, 0], zr.at[1, 0], left, q))
+    yield_up(3, 2)
+    yield_up(4, -2)
+    for k, scan in enumerate(column):
+        send(pzs, pzb.at[k], p2s.at[k], p2r.at[k], here, q).wait_recv()
+        total = total + pzb[k]
+    pg_ref[mine] = total * scale
+    for n, scan, d in peers:
+        go(send(pg_ref.at[mine], pg_ref.at[mine], p3s.at[n], p3r.at[n], scan, q))
+    firsts = (0, half)
+    whole = range(tile_dev)
+    steps = ((3, sr1, sl1, rr0, rl0, rr1, rl1), (2, sr2, sl2, rr1, rl1, rr2, rl2), (1, sr3, sl3, rr2, rl2, rr3, rl3))
+    for step, (offset, sr, sl, rr, rl, rr_next, rl_next) in enumerate(steps, 1):
+        await_up(2 * step - 1, offset)
+        to_right.wait_recv()
+        combine(offset, whole, sr, [(rr, 0)])
+        to_right = go(send(sr, rr_next, zs.at[0, step], zr.at[0, step], right, q))
+        await_up(2 * step, -offset)
+        to_left.wait_recv()
+        combine(-offset, whole, sl, [(rl, half if step == 1 else 0)])
+        to_left = go(send(sl, rl_next, zs.at[1, step], zr.at[1, step], left, q))
+        if step == 1:
+            yield_up(5, 1)
+            yield_up(6, -1)
+        elif step == 2:
+            yield_up(7, 0)
+    await_up(7, 0)
+    to_right.wait_recv()
+    to_left.wait_recv()
+    combine(0, whole, out_ref, [(rr3, 0), (rl3, 0)])
+    for n, source in enumerate(sources):
+        send(pg_ref.at[source], pg_ref.at[source], p3s.at[n], p3r.at[n], here, q).wait_recv()
+    for copy in sends:
+        copy.wait_send()
+
+
+def give_back(hot, canvas, probe_part, tile_dev, scale):
+    tile = canvas.shape[1:]
+    piece = probe_part.shape[1:]
+    dma = pltpu.SemaphoreType.DMA
+    vmem = pl.BlockSpec(memory_space=pltpu.VMEM)
+    chunk = pltpu.VMEM((tile_dev,) + tile, canvas.dtype)
+    part = pltpu.VMEM((tile_dev // 2,) + tile, canvas.dtype)
+    return pl.pallas_call(
+        functools.partial(return_kernel, scale=scale),
+        in_specs=[pl.BlockSpec(memory_space=pltpu.SMEM), vmem, vmem],
+        out_specs=[vmem, vmem],
+        out_shape=[
+            jax.ShapeDtypeStruct((tile_dev,) + tile, canvas.dtype),
+            jax.ShapeDtypeStruct(probe_part.shape, probe_part.dtype),
+        ],
+        scratch_shapes=[pltpu.VMEM(canvas.shape, canvas.dtype)]
+        + [part, chunk, chunk, chunk] * 4
+        + [
+            pltpu.VMEM((7,) + piece, probe_part.dtype),
+            pltpu.VMEM(piece, probe_part.dtype),
+            pltpu.VMEM((RING - 1,) + piece, probe_part.dtype),
+            dma((2, 4)),
+            dma((2, 4)),
+            dma((7, 8)),
+            dma((7, 8)),
+            dma((7,)),
+            dma((7,)),
+            dma((RING - 1,)),
+            dma((RING - 1,)),
+            dma((7,)),
+            dma((7,)),
+        ],
+        compiler_params=pltpu.CompilerParams(
+            collective_id=2, has_side_effects=True, vmem_limit_bytes=48 * MIB
+        ),
+        name="give_back",
+    )(hot, canvas, probe_part)
 
 
 def shards(object_tiles, tile_owner, block_tiles, positions, counts, probe):
     scan_count = lax.axis_size("scan")
     mode_count = lax.axis_size("mode")
-    scan_here = lax.axis_index("scan")
-    mode_here = lax.axis_index("mode")
+    here = lax.axis_index("scan")
+    q = lax.axis_index("mode").reshape(1)
     tile_dev, slices, parts, side = object_tiles.shape[:4]
     batch = positions.shape[0]
     span = scan_count // 2
     quarter = side // mode_count
-    npos = batch // mode_count
     planes = slices * parts
     tables = jnp.asarray(transform_tables(side))
 
+    y, z, core = spot(here)
     first = block_tiles[:, 0]
-    tiles = tile_owner.shape[0]
-    tile_range = jnp.arange(tiles, dtype=jnp.int32)
+    total = tile_owner.shape[0]
+    tile_range = jnp.arange(total, dtype=jnp.int32)
     same = (tile_owner[:, None] == tile_owner[None, :]) & (tile_range[None, :] < tile_range[:, None])
     rank = jnp.sum(same.astype(jnp.int32), axis=1)
-    listed = (tile_range[None, :] >= first[:, None]) & (tile_range[None, :] < first[:, None] + scan_count)
-    mine = listed & (tile_owner == scan_here)[None, :]
-    local_rows = jnp.sum(jnp.where(mine, rank[None, :], 0), axis=1)
-    my_first = lax.dynamic_index_in_dim(first, scan_here, 0, keepdims=False)
-    slot_owner = lax.dynamic_slice(tile_owner, (my_first,), (scan_count,))
-    q = mode_here.reshape(1)
+    near = lax.dynamic_index_in_dim(first.reshape(4, RING, 2), z, 1, keepdims=False).reshape(8)
+    ring = at_spot(y, jnp.arange(RING, dtype=jnp.int32), core)
+    listed = (tile_range[None, :] >= near[:, None]) & (tile_range[None, :] < near[:, None] + scan_count)
+    owned = tile_owner[None, :] == ring[:, None]
+    sel = jnp.sum(jnp.where(listed[:, None, :] & owned[None, :, :], rank[None, None, :], 0), axis=2)
+    hot = (sel[:, :, None] == jnp.arange(tile_dev, dtype=jnp.int32)).astype(jnp.float32).reshape(-1)
+    my_first = lax.dynamic_index_in_dim(first, here, 0, keepdims=False)
     up, left = positions[:, 0] // side, positions[:, 1] // side
     down, right = jnp.minimum(up + 1, 1), jnp.minimum(left + 1, span - 1)
     slots = jnp.stack([up * span + left, up * span + right, down * span + left, down * span + right], axis=1)
-    rc = positions % side
-    place = jnp.concatenate([slot_owner[slots], rc], axis=1)
-
-    part = lax.dynamic_slice_in_dim(object_tiles, mode_here * quarter, quarter, 3).reshape(
-        tile_dev, planes, quarter, side
+    wanted = my_first + slots
+    owner_y, owner_z, owner_core = spot(tile_owner)
+    homes = (owner_y * 2 + owner_core) * RING + owner_z
+    found = jnp.sum(jnp.where(wanted[:, :, None] == tile_range, homes, 0), axis=2)
+    place = jnp.concatenate([found, positions % side], axis=1)
+
+    x, probe_all = gather(sel, place, object_tiles.reshape(tile_dev, planes, side, side), probe, mode_count)
+    terms, probe_terms = compute(place, q, x, probe_all, counts, tables)
+    back, probe_part = swap(terms, probe_terms)
+    canvas = lay(place, q, back.reshape(batch, planes, quarter, side), scan_count)
+    summed, probe_grad = give_back(
+        hot, canvas, probe_part.reshape(8, parts * side // 8, side), tile_dev, 1.0 / (batch * scan_count)
     )
-    window = lax.all_to_all(part[local_rows], "scan", split_axis=0, concat_axis=0, tiled=True)
-    pieces = cut(place, q, window)
-    probe_all = lax.all_gather(probe, "mode", axis=0, tiled=True)
-    x = lax.all_to_all(
-        pieces.reshape(mode_count, npos, planes, quarter, side), "mode", split_axis=0, concat_axis=0, tiled=True
-    )
-    my_rc = lax.dynamic_slice_in_dim(rc, mode_here * npos, npos, 0)
-    terms, probe_terms = compute(my_rc, q, x, probe_all, counts, tables)
-    probe_part = lax.psum_scatter(probe_terms, "mode", scatter_dimension=0, tiled=True)
-    probe_grad = lax.psum(probe_part, "scan") / (batch * scan_count)
-    back = lax.all_to_all(terms, "mode", split_axis=0, concat_axis=0, tiled=True)
-    canvas = lay(place, q, back.reshape(batch, planes, quarter, side), scan_count)
-    returned = lax.all_to_all(canvas, "scan", split_axis=0, concat_axis=0, tiled=True)
-    summed = land(local_rows, returned, tile_dev)
-    return (summed.reshape(tile_dev, slices, parts, quarter, side), probe_grad)
+    return (summed.reshape(tile_dev, slices, parts, quarter, side), probe_grad.reshape(probe.shape))
 
 
 def solution(mesh):

time: 371 us -> 169 us (0.46)
  waiting for transfers between devices: 263 us -> 0 us
  Pallas kernels: 20.2 us -> 155 us
  starting transfers between devices: 29.5 us -> 0 us
  blocking collectives: 28.6 us -> 0 us
  between operations: 16.1 us -> 0.79 us
    psum x1 -> x0, waiting for transfers between devices: 190 us -> none  [shards(): probe_grad = lax.psum(probe_part, 'scan') / (batch * scan_count)]
    pallas_call x2 -> x3, Pallas kernels: 4.76 us -> 140 us  [the longest x1 69 us: give_back(): pl.pallas_call(functools.partial(return_kernel, scale=scale), in_specs=[p...]
    all_to_all x3 -> x0, waiting for transfers between devices: 46.7 us -> none  [the longest x1 46.7 us: shards(): lax.all_to_all(part[local_rows], 'scan', split_axis=0, concat_axis=0, til...]
    all_to_all x3 -> x0, starting transfers between devices: 29.4 us -> none  [the longest x1 13.3 us: shards(): lax.all_to_all(part[local_rows], 'scan', split_axis=0, concat_axis=0, til...]
    reduce_scatter x1 -> x0, waiting for transfers between devices: 24.9 us -> none  [shards(): lax.psum_scatter(probe_terms, 'mode', scatter_dimension=0, tiled=True)]
    all_gather x1 -> x0, blocking collectives: 14.3 us -> none  [shards(): probe_all = lax.all_gather(probe, 'mode', axis=0, tiled=True)]
    all_to_all x1 -> x0, blocking collectives: 14.3 us -> none  [shards(): lax.all_to_all(terms, 'mode', split_axis=0, concat_axis=0, tiled=True)]
  transfers between devices with their start and end apart: 5 -> 0, of which waited for: 3 -> 0; matrix products, arithmetic and copies ran while one was open for 1% -> 0% of each run, Pallas kernels for 0% -> 0%
where the time goes in v2:
time: 169 us
  Pallas kernels  155 us (92%)
  local copies, waits for them, and re-layouts  8.55 us (5%)
  other arithmetic  4.51 us (3%)
    pallas_call x1, Pallas kernels, give_back(): pl.pallas_call(functools.partial(return_kernel, scale=scale), in_specs=[p...  69 us
    pallas_call x1, Pallas kernels, gather(): pl.pallas_call(gather_kernel, in_specs=[pl.BlockSpec(memory_space=pltpu.S...  51 us
    pallas_call x1, Pallas kernels, swap(): pl.pallas_call(swap_kernel, in_specs=[vmem, vmem], out_specs=[vmem, vmem]...  20 us
    pallas_call x1, Pallas kernels, compute(): pl.pallas_call(compute_kernel, grid_spec=pltpu.PrefetchScalarGridSpec(num...  13.6 us
    unnamed x11, local copies, waits for them, and re-layouts  6.78 us

profile of v2, /device:TPU:1, one launch (start us, length us, event | category | flops | bytes accessed | tf_op | source)
XLA Modules:
  0.0 169.0 jit_solution(12446892514197759634)
XLA Ops:
  0.7 0.8 multiply_add_fusion.2
  1.5 1.0 convert_reduce_fusion
  2.5 0.7 fusion.8
  3.2 0.8 copy.17
  4.0 0.9 fusion.13
  4.8 0.5 constant_dynamic-slice_fusion
  5.3 0.7 add_add_fusion
  6.0 0.2 select_reduce_fusion
  6.2 0.1 copy.20
  6.3 0.1 pad_add_fusion.place_ref.rc_ref
  6.4 0.1 reshape_squeeze.3
  6.5 0.1 ge.22
  6.6 0.8 fusion.2
  7.4 0.2 select_reduce_fusion.1.sel_ref
  7.6 0.1 fusion.1
  7.7 0.1 reshape.148.hot_ref
  7.8 0.0 copy-start
  7.8 1.2 copy-done
  9.0 0.0 copy-start.3
  9.0 0.9 copy-done.3
  9.9 51.0 %gather.1 = (bf16[4,4,4,32,128]{4,3,2,1,0:T(8,128)(2,1)S(1)}, f32[4,2,128,128]{3,2,1,0:T(8,128)S(1)}) custom-call(s32[8,8]{1,0:T(8,128)S(1)} %select_reduce_fusion.1.sel_ref, s32[16,6]{1,0:T(8,128)S(1)} %pad_add_fusion.place_ref.rc_ref, bf16[8,4,128,128]{3,2,1,0:T(8,128)(2,1)S(1)} %bitcast.7, f32[1,2,128,128]{3,2,1,0:T(8,128)S(1)} %copy-done.3), custom_call_target="tpu_custom_call" | custom-call | tf_op jit(solution)/shard_map/gather/pallas_call | solution.py:358
  60.9 0.0 copy-start.1
  60.9 1.2 copy-done.1
  62.1 0.0 copy-start.2
  62.1 1.2 copy-done.2
  63.4 13.6 %fields.1 = (f32[4,4,4,32,128]{4,3,2,1,0:T(8,128)S(1)}, f32[4,2,128,128]{3,2,1,0:T(8,128)S(1)}) custom-call(s32[16,6]{1,0:T(8,128)S(1)} %pad_add_fusion.place_ref.rc_ref, s32[1]{0:T(128)} %bitcast.1.q_ref, bf16[4,4,4,32,128]{4,3,2,1,0:T(8,128)(2,1)S(1)} %get-tuple-element.10.x_ref, f32[4,2,128,128]{3,2,1,0:T(8,128)S(1)} %get-tuple-element.11.probe_ref, ...), custom_call_target="tpu_custom_call" | custom-call | tf_op jit(solution)/shard_map/fields/pallas_call | solution.py:149
  77.0 20.0 %swap.1 = (f32[4,4,4,32,128]{4,3,2,1,0:T(8,128)S(1)}, f32[2,128,128]{2,1,0:T(8,128)S(1)}) custom-call(f32[4,4,4,32,128]{4,3,2,1,0:T(8,128)S(1)} %get-tuple-element.12.e_ref, f32[4,2,128,128]{3,2,1,0:T(8,128)S(1)} %get-tuple-element.13.pg_ref), custom_call_target="tpu_custom_call" | custom-call | tf_op jit(solution)/shard_map/swap/pallas_call | solution.py:423
  97.0 1.5 lay.1.canvas
  98.5 69.0 %give_back.1 = (f32[8,4,32,128]{3,2,1,0:T(8,128)S(1)}, f32[8,32,128]{2,1,0:T(8,128)S(1)}) custom-call(f32[512]{0:T(512)S(1)} %reshape.148.hot_ref, f32[64,4,32,128]{3,2,1,0:T(8,128)S(1)} %lay.1.canvas, f32[8,32,128]{2,1,0:T(8,128)S(1)} %bitcast.10), custom_call_target="tpu_custom_call" | custom-call | tf_op jit(solution)/shard_map/give_back/pallas_call | solution.py:547
  167.5 0.8 copy.23
  168.3 0.7 copy.24
  (5 shorter events, 0.1 us)
Async XLA Ops:
  7.8 1.2 copy-start
  9.0 0.9 copy-start.3
  60.9 1.2 copy-start.1
  62.1 1.2 copy-start.2

commit v3 on v1

v3 whole, which is shorter than its diff:
```python
import functools

import jax
import jax.numpy as jnp
import ml_dtypes
import numpy as np
from jax import lax
from jax.experimental import pallas as pl
from jax.experimental.pallas import tpu as pltpu
from jax.sharding import PartitionSpec as P

background = 0.25
fresnel_number = 1.0
MIB = 1024 * 1024
RING = 8
STEPS = 32767.0


def split_const(matrix):
    hi = matrix.astype(ml_dtypes.bfloat16)
    lo = (matrix - hi.astype(np.float64)).astype(ml_dtypes.bfloat16)
    return hi, lo


def transform_tables(side):
    index = np.arange(side)
    four = np.exp(-2j * np.pi * (index[:, None] * index[None, :] % side) / side) / np.sqrt(side)
    frequency = np.where(index < side // 2, index, index - side) / side
    chirp = np.exp(-1j * np.pi * fresnel_number * frequency * frequency)
    prop = (four.conj() * chirp[None, :]) @ four
    blocks = []
    for matrix in (four, prop):
        re, im = matrix.real, matrix.imag
        blocks.append(np.block([[re, im], [-im, re]]))
        blocks.append(np.block([[re, -im], [im, re]]))
    parts = []
    for block in blocks:
        parts.extend(split_const(block))
    return np.stack(parts)


def split_parts(value):
    hi = value.astype(jnp.bfloat16)
    lo = (value - hi.astype(jnp.float32)).astype(jnp.bfloat16)
    return hi, lo


def dot(a, b):
    return jnp.dot(a, b, preferred_element_type=jnp.float32)


def residue_masks(row, col, first_row, shape):
    rows = lax.broadcasted_iota(jnp.int32, shape, len(shape) - 2) + first_row
    cols = lax.broadcasted_iota(jnp.int32, shape, len(shape) - 1)
    return rows >= row, cols >= col


def spot(scan):
    return scan // (2 * RING), scan // 2 % RING, scan % 2


def at_spot(y, z, core):
    return (y * RING + z) * 2 + core


def plane_peers(y, z, core):
    peers = []
    for number in range(1, 8):
        there_y, there_core = (y + number // 2) % 4, (core + number % 2) % 2
        peers.append((number - 1, at_spot(there_y, z, there_core), there_y * 2 + there_core))
    return peers


def plane_sources(y, core):
    return [(y - number // 2 + 4) % 4 * 2 + (core + number % 2) % 2 for number in range(1, 8)]


def send(src, dst, send_sem, recv_sem, scan, mode):
    return pltpu.make_async_remote_copy(
        src_ref=src,
        dst_ref=dst,
        send_sem=send_sem,
        recv_sem=recv_sem,
        device_id={"scan": scan, "mode": mode},
        device_id_type=pl.DeviceIdType.MESH,
    )


def meet(partners):
    barrier = pltpu.get_barrier_semaphore()
    for scan, mode in partners:
        pl.semaphore_signal(
            barrier, inc=1, device_id={"scan": scan, "mode": mode}, device_id_type=pl.DeviceIdType.MESH
        )
    pl.semaphore_wait(barrier, len(partners))


def front_kernel(sel_ref, place_ref, obj_ref, probe_ref, counts_any, tab_any, eq_ref, pg_ref, a0, a1, a2, a3, b1, b2, b3, h4, win, ybuf, xbuf, x_ref, pall_ref, counts_ref, tab_ref, ebuf, a_hi, a_lo, c_hi, c_lo, planes_ref, wave_ref, sum_ref, local_sem, zs, zr, ys, yr, xs, xr, ps, pr, es, er):
    here, q = lax.axis_index("scan"), lax.axis_index("mode")
    y, z, core = spot(here)
    mine = y * 2 + core
    quarter = a0.shape[2]
    half = a0.shape[0] // 2
    modes, npos = x_ref.shape[:2]
    side = pall_ref.shape[-1]
    own = pltpu.make_async_copy(obj_ref.at[:, :, pl.ds(q * quarter, quarter), :], a0, local_sem.at[0])
    own.start()
    local = [
        pltpu.make_async_copy(tab_any, tab_ref, local_sem.at[1]),
        pltpu.make_async_copy(counts_any.at[pl.ds(q * npos, npos)], counts_ref, local_sem.at[2]),
        pltpu.make_async_copy(probe_ref.at[0], pall_ref.at[q], local_sem.at[3]),
    ]
    for copy in local:
        copy.start()
    right, left = at_spot(y, (z + 1) % RING, core), at_spot(y, (z + RING - 1) % RING, core)
    peers = plane_peers(y, z, core)
    sources = plane_sources(y, core)
    others = [(q + k) % modes for k in range(1, modes)]
    meet([(right, q), (left, q)] + [(scan, q) for _, scan, _ in peers] + [(here, m) for m in others])
    own.wait()

    sends = []

    def go(copy):
        copy.start()
        sends.append(copy)
        return copy

    def offer(buf, r, zi):
        for n, scan, d in peers:
            ybuf[n, r] = buf[sel_ref[d, zi]]
            go(send(ybuf.at[n, r], win.at[mine * RING + zi], ys.at[n, r], yr.at[n, r], scan, q))
        win[mine * RING + zi] = buf[sel_ref[mine, zi]]

    parts = (slice(0, half), slice(half, 2 * half))

    def pass_on(direction, step, part, src, dst, scan):
        rows = parts[part]
        return go(send(src.at[rows], dst.at[rows], zs.at[direction, step, part], zr.at[direction, step, part], scan, q))

    to_right = [pass_on(0, 0, part, a0, a1, right) for part in range(2)]
    to_left = [pass_on(1, 0, part, a0, b1, left) for part in (1, 0)][::-1]
    for k, m in enumerate(others):
        go(send(probe_ref.at[0], pall_ref.at[q], ps.at[k], pr.at[k], here, m))
    chunks = [(0, z)]
    offer(a0, 0, z)
    for step, (a, a_next, b, b_next) in enumerate(((a1, a2, b1, b2), (a2, a3, b2, b3), (a3, h4, b3, h4)), 1):
        last = step == 3
        next_right, next_left = [None, None], [None, None]
        for turn in range(2):
            part = turn
            to_right[part].wait_recv()
            if not last or part == 0:
                next_right[part] = pass_on(0, step, part, a, a_next, right)
            part = 1 - turn
            to_left[part].wait_recv()
            if not last or part == 1:
                next_left[part] = pass_on(1, step, part, b, b_next, left)
        to_right, to_left = next_right, next_left
        behind, ahead = (z + RING - step) % RING, (z + step) % RING
        offer(a, 2 * step - 1, behind)
        offer(b, 2 * step, ahead)
        chunks.extend([(2 * step - 1, behind), (2 * step, ahead)])
    to_right[0].wait_recv()
    to_left[1].wait_recv()
    opposite = (z + 4) % RING
    offer(h4, 7, opposite)
    chunks.append((7, opposite))
    for r, zi in chunks:
        for n, source in enumerate(sources):
            send(ybuf.at[n, r], win.at[source * RING + zi], ys.at[n, r], yr.at[n, r], here, q).wait_recv()

    def piece(j):
        up, left_side = residue_masks(place_ref[j, 4], place_ref[j, 5], q * quarter, win.shape[1:])
        tiles = [win[place_ref[j, k]].astype(jnp.float32) for k in range(4)]
        upper = jnp.where(left_side, tiles[0], tiles[1])
        lower = jnp.where(left_side, tiles[2], tiles[3])
        return jnp.where(up, upper, lower).astype(jnp.bfloat16)

    def x_copy(k, i, scan_mode, target):
        return send(xbuf.at[k, i], x_ref.at[target, i], xs.at[k, i], xr.at[k, i], here, scan_mode)

    def pack(i, carry):
        for k in (1, 0, 2):
            xbuf[k, i] = piece(others[k] * npos + i)
            x_copy(k, i, others[k], q).start()
        x_ref[q, i] = piece(q * npos + i)
        return carry

    lax.fori_loop(0, npos, pack, 0)
    for copy in local:
        copy.wait()
    froms = [(q + modes - 1 - k) % modes for k in range(modes - 1)]
    for k in range(modes - 1):
        send(probe_ref.at[0], pall_ref.at[froms[k]], ps.at[k], pr.at[k], here, q).wait_recv()

    def block(m):
        return slice(m * side, (m + 1) * side)

    def two_sided(right_table, left_table, fields):
        for m, (re, im) in enumerate(fields):
            rh, rl = split_parts(re)
            ih, il = split_parts(im)
            a_hi[block(m), 0:side] = rh
            a_hi[block(m), side : 2 * side] = ih
            a_lo[block(m), 0:side] = rl
            a_lo[block(m), side : 2 * side] = il
        for m in range(modes):
            bh, bl = tab_ref[2 * right_table], tab_ref[2 * right_table + 1]
            whole = dot(a_hi[block(m)], bh) + dot(a_lo[block(m)], bh) + dot(a_hi[block(m)], bl)
            hi, lo = split_parts(whole)
            c_hi[0:side, block(m)] = hi[:, 0:side]
            c_hi[side : 2 * side, block(m)] = hi[:, side : 2 * side]
            c_lo[0:side, block(m)] = lo[:, 0:side]
            c_lo[side : 2 * side, block(m)] = lo[:, side : 2 * side]
        lh, ll = tab_ref[2 * left_table], tab_ref[2 * left_table + 1]
        out = []
        for h in range(modes // 2):
            cols = slice(h * 2 * side, (h + 1) * 2 * side)
            whole = dot(lh, c_hi[:, cols]) + dot(lh, c_lo[:, cols]) + dot(ll, c_hi[:, cols])
            for k in range(2):
                out.append((whole[0:side, block(k)], whole[side : 2 * side, block(k)]))
        return out

    pg_ref[...] = jnp.zeros_like(pg_ref)

    def e_copy(k, p, mode, target):
        return send(ebuf.at[k, p], eq_ref.at[target, p], es.at[k, p], er.at[k, p], here, mode)

    def position(p, carry):
        for k in range(modes - 1):
            x_copy(k, p, q, froms[k]).wait_recv()
        row = place_ref[q * npos + p, 4]
        col = place_ref[q * npos + p, 5]
        for plane in range(4):
            whole = jnp.concatenate([x_ref[k, p, plane].astype(jnp.float32) for k in range(modes)], axis=0)
            whole = pltpu.roll(whole, (side - row) % side, 0)
            planes_ref[plane] = pltpu.roll(whole, (side - col) % side, 1)
        fields = []
        for m in range(modes):
            wr, wi = pall_ref[m, 0], pall_ref[m, 1]
            xr_, xi_ = planes_ref[0], planes_ref[1]
            fields.append((wr * xr_ - wi * xi_, wr * xi_ + wi * xr_))
        waves = two_sided(2, 3, fields)
        fields = []
        for m in range(modes):
            wr, wi = waves[m]
            wave_ref[m, 0] = wr
            wave_ref[m, 1] = wi
            xr_, xi_ = planes_ref[2], planes_ref[3]
            fields.append((wr * xr_ - wi * xi_, wr * xi_ + wi * xr_))
        far = two_sided(0, 1, fields)
        intensity = background
        for re, im in far:
            intensity = intensity + (re * re + im * im)
        weight = 1.0 - counts_ref[p].astype(jnp.float32) / intensity
        grads = two_sided(1, 0, [(weight * re, weight * im) for re, im in far])
        fields = []
        e_re = e_im = 0.0
        for m in range(modes):
            gr, gi = grads[m]
            wr, wi = wave_ref[m, 0], wave_ref[m, 1]
            e_re = e_re + (wr * gr + wi * gi)
            e_im = e_im + (wr * gi - wi * gr)
            xr_, xi_ = planes_ref[2], planes_ref[3]
            fields.append((xr_ * gr + xi_ * gi, xr_ * gi - xi_ * gr))
        sum_ref[2] = e_re
        sum_ref[3] = e_im
        grads = two_sided(3, 2, fields)
        e_re = e_im = 0.0
        for m in range(modes):
            gr, gi = grads[m]
            wr, wi = pall_ref[m, 0], pall_ref[m, 1]
            e_re = e_re + (wr * gr + wi * gi)
            e_im = e_im + (wr * gi - wi * gr)
            xr_, xi_ = planes_ref[0], planes_ref[1]
            pg_ref[m, 0] += xr_ * gr + xi_ * gi
            pg_ref[m, 1] += xr_ * gi - xi_ * gr
        sum_ref[0] = e_re
        sum_ref[1] = e_im
        for plane in range(4):
            sum_ref[plane] = pltpu.roll(pltpu.roll(sum_ref[plane], row, 0), col, 1)
        for k in range(modes - 1):
            rows = pl.ds(pl.multiple_of(others[k] * quarter, quarter), quarter)
            for plane in range(4):
                ebuf[k, p, plane] = sum_ref[plane, rows]
            e_copy(k, p, others[k], q).start()
        rows = pl.ds(pl.multiple_of(q * quarter, quarter), quarter)
        for plane in range(4):
            eq_ref[q, p, plane] = sum_ref[plane, rows]
        return carry

    lax.fori_loop(0, npos, position, 0)

    def finish(p, carry):
        for k in range(modes - 1):
            e_copy(k, p, q, froms[k]).wait_recv()
            e_copy(k, p, others[k], q).wait_send()
            x_copy(k, p, others[k], q).wait_send()
        return carry

    lax.fori_loop(0, npos, finish, 0)
    for copy in sends:
        copy.wait_send()


def front(sel, place, tiles, probe, counts, tables, modes):
    tile_dev, planes, side, _ = tiles.shape
    quarter = side // modes
    npos = place.shape[0] // modes
    chunk = pltpu.VMEM((tile_dev, planes, quarter, side), tiles.dtype)
    dma = pltpu.SemaphoreType.DMA
    smem, anywhere, vmem = (pl.BlockSpec(memory_space=space) for space in (pltpu.SMEM, pl.ANY, pltpu.VMEM))
    pieces = (modes - 1, npos, planes, quarter, side)
    return pl.pallas_call(
        front_kernel,
        in_specs=[smem, smem, anywhere, anywhere, anywhere, anywhere],
        out_specs=[vmem, vmem],
        out_shape=[
            jax.ShapeDtypeStruct((modes, npos, planes, quarter, side), jnp.float32),
            jax.ShapeDtypeStruct((modes,) + probe.shape[1:], jnp.float32),
        ],
        scratch_shapes=[chunk] * 8
        + [
            pltpu.VMEM((8 * RING, planes, quarter, side), tiles.dtype),
            pltpu.VMEM((7, RING, planes, quarter, side), tiles.dtype),
            pltpu.VMEM(pieces, tiles.dtype),
            pltpu.VMEM((modes,) + pieces[1:], tiles.dtype),
            pltpu.VMEM((modes,) + probe.shape[1:], probe.dtype),
            pltpu.VMEM((npos, side, side), counts.dtype),
            pltpu.VMEM(tables.shape, tables.dtype),
            pltpu.VMEM(pieces, jnp.float32),
            pltpu.VMEM((modes * side, 2 * side), jnp.bfloat16),
            pltpu.VMEM((modes * side, 2 * side), jnp.bfloat16),
            pltpu.VMEM((2 * side, modes * side), jnp.bfloat16),
            pltpu.VMEM((2 * side, modes * side), jnp.bfloat16),
            pltpu.VMEM((planes, side, side), jnp.float32),
            pltpu.VMEM((modes, 2, side, side), jnp.float32),
            pltpu.VMEM((planes, side, side), jnp.float32),
            dma((4,)),
            dma((2, 4, 2)),
            dma((2, 4, 2)),
            dma((7, 8)),
            dma((7, 8)),
            dma((modes - 1, npos)),
            dma((modes - 1, npos)),
            dma((modes - 1,)),
            dma((modes - 1,)),
            dma((modes - 1, npos)),
            dma((modes - 1, npos)),
        ],
        compiler_params=pltpu.CompilerParams(
            collective_id=0, has_side_effects=True, vmem_limit_bytes=48 * MIB
        ),
        name="front",
    )(sel, place, tiles, probe, counts, tables)


def column_scale(value):
    most = jnp.max(jnp.max(jnp.abs(value), axis=0), axis=0, keepdims=True)
    return jnp.maximum(most, 1e-30) * (1.0 / STEPS)


def encode(value, scale):
    return jnp.round(value * (1.0 / scale)).astype(jnp.int32).astype(jnp.int16)


def decode(code):
    return code.astype(jnp.int32).astype(jnp.float32)


def lay_kernel(place_ref, q_ref, e_ref, code_ref, scale_ref, canvas):
    quarter = e_ref.shape[2]
    canvas[...] = jnp.zeros_like(canvas)

    def position(j, carry):
        up, left = residue_masks(place_ref[j, 4], place_ref[j, 5], q_ref[0] * quarter, e_ref.shape[1:])
        term = e_ref[j]
        upper = jnp.where(up, term, 0.0)
        lower = jnp.where(up, 0.0, term)
        canvas[place_ref[j, 0]] += jnp.where(left, upper, 0.0)
        canvas[place_ref[j, 1]] += jnp.where(left, 0.0, upper)
        canvas[place_ref[j, 2]] += jnp.where(left, lower, 0.0)
        canvas[place_ref[j, 3]] += jnp.where(left, 0.0, lower)
        return carry

    lax.fori_loop(0, e_ref.shape[0], position, 0)

    def group(d, carry):
        for k in range(RING):
            value = canvas[d * RING + k]
            scale = column_scale(value)
            scale_ref[d, k : k + 1, :] = scale
            code_ref[d * RING + k] = encode(value, scale)
        return carry

    lax.fori_loop(0, scale_ref.shape[0], group, 0)


def lay(place, q, terms, slots):
    smem, vmem = (pl.BlockSpec(memory_space=space) for space in (pltpu.SMEM, pltpu.VMEM))
    return pl.pallas_call(
        lay_kernel,
        in_specs=[smem, smem, vmem],
        out_specs=[vmem, vmem],
        out_shape=[
            jax.ShapeDtypeStruct((slots,) + terms.shape[1:], jnp.int16),
            jax.ShapeDtypeStruct((slots // RING, RING, terms.shape[-1]), jnp.float32),
        ],
        scratch_shapes=[pltpu.VMEM((slots,) + terms.shape[1:], jnp.float32)],
        compiler_params=pltpu.CompilerParams(vmem_limit_bytes=32 * MIB),
        name="lay",
    )(place, q, terms)


def return_kernel(hot_ref, canvas, cscale, pp_ref, out_ref, pg_ref, rbuf, rscale, sr0, sr1, sr2, sr3, sl0, sl1, sl2, sl3, rr0, rr1, rr2, rr3, rl0, rl1, rl2, rl3, sscale, zscale, total_ref, pxb, pxs, pyb, pzs, pzb, zs, zr, zcs, zcr, ys, yr, ycs, ycr, p0s, p0r, p1s, p1r, p2s, p2r, p3s, p3r, scale=1.0):
    here, q = lax.axis_index("scan"), lax.axis_index("mode")
    y, z, core = spot(here)
    mine = y * 2 + core
    tile_dev, planes = out_ref.shape[:2]
    half = tile_dev // 2
    modes = pp_ref.shape[0]
    right, left = at_spot(y, (z + 1) % RING, core), at_spot(y, (z + RING - 1) % RING, core)
    peers = plane_peers(y, z, core)
    sources = plane_sources(y, core)
    column = [at_spot(y, (z + k) % RING, core) for k in range(1, RING)]
    others = [(q + k) % modes for k in range(1, modes)]
    meet([(scan, q) for scan in column] + [(scan, q) for _, scan, _ in peers] + [(here, m) for m in others])
    sends = []

    def go(copy):
        copy.start()
        sends.append(copy)
        return copy

    def zi(offset):
        return (z + offset + RING) % RING

    def yield_up(r, offset):
        for n, scan, d in peers:
            go(send(canvas.at[d * RING + zi(offset)], rbuf.at[mine * RING + zi(offset)], ys.at[n, r], yr.at[n, r], scan, q))

    def await_up(r, offset):
        for n, source in enumerate(sources):
            at = source * RING + zi(offset)
            send(canvas.at[at], rbuf.at[at], ys.at[n, r], yr.at[n, r], here, q).wait_recv()

    def combine(offset, first, count, received):
        place = zi(offset)
        steps = [cscale[mine, pl.ds(place, 1)]] + [rscale[source, pl.ds(place, 1)] for source in sources]
        givers = [mine] + sources
        weights = [
            [hot_ref[(giver * RING + place) * tile_dev + first + k] for k in range(count)] for giver in givers
        ]

        def plane(l, carry):
            terms = [decode(canvas[mine * RING + place, l]) * steps[0]]
            terms.extend(
                decode(rbuf[source * RING + place, l]) * step for source, step in zip(sources, steps[1:])
            )
            for k in range(count):
                total = weights[0][k] * terms[0]
                for weight, term in zip(weights[1:], terms[1:]):
                    total = total + weight[k] * term
                for ref, ref_scale, ref_first in received:
                    at = first + k - ref_first
                    if 0 <= at < ref.shape[0]:
                        total = total + decode(ref[at, l]) * ref_scale[at : at + 1]
                total_ref[k, l] = total
            return carry

        lax.fori_loop(0, planes, plane, 0)

    def ship(direction, step, count, buf, to, scan):
        for k in range(count):
            value = total_ref[k]
            step_size = column_scale(value)
            sscale[direction, step, k : k + 1] = step_size
            buf[k] = encode(value, step_size)
        return (
            go(send(sscale.at[direction, step], zscale.at[direction, step], zcs.at[direction, step], zcr.at[direction, step], scan, q)),
            go(send(buf, to, zs.at[direction, step], zr.at[direction, step], scan, q)),
        )

    def landed(pair):
        for copy in pair:
            copy.wait_recv()

    sscale[...] = jnp.zeros_like(sscale)
    for n, scan, d in peers:
        go(send(cscale.at[d], rscale.at[mine], ycs.at[n], ycr.at[n], scan, q))
    for k, m in enumerate(others):
        go(send(pp_ref.at[m], pxb.at[k], p0s.at[k], p0r.at[k], here, m))
    yield_up(0, 4)
    yield_up(1, 3)
    yield_up(2, -3)
    for n, source in enumerate(sources):
        send(cscale.at[source], rscale.at[source], ycs.at[n], ycr.at[n], here, q).wait_recv()
    await_up(0, 4)
    combine(4, 0, half, [])
    to_right = ship(0, 0, half, sr0, rr0, right)
    combine(4, half, half, [])
    to_left = ship(1, 0, half, sl0, rl0, left)
    yield_up(3, 2)
    yield_up(4, -2)
    total = pp_ref[q]
    for k in range(modes - 1):
        send(pp_ref.at[q], pxb.at[k], p0s.at[k], p0r.at[k], here, q).wait_recv()
        total = total + pxb[k]
    pxs[...] = total
    for n, scan, d in peers:
        go(send(pxs.at[d], pyb.at[n], p1s.at[n], p1r.at[n], scan, q))
    steps = ((3, sr1, sl1, rr0, rl0, rr1, rl1), (2, sr2, sl2, rr1, rl1, rr2, rl2), (1, sr3, sl3, rr2, rl2, rr3, rl3))
    for step, (offset, sr, sl, rr, rl, rr_next, rl_next) in enumerate(steps, 1):
        await_up(2 * step - 1, offset)
        landed(to_right)
        combine(offset, 0, tile_dev, [(rr, zscale.at[0, step - 1], 0)])
        to_right = ship(0, step, tile_dev, sr, rr_next, right)
        await_up(2 * step, -offset)
        landed(to_left)
        combine(-offset, 0, tile_dev, [(rl, zscale.at[1, step - 1], half if step == 1 else 0)])
        to_left = ship(1, step, tile_dev, sl, rl_next, left)
        if step == 1:
            yield_up(5, 1)
            yield_up(6, -1)
            total = pxs[mine]
            for n, source in enumerate(sources):
                send(pxs.at[source], pyb.at[n], p1s.at[n], p1r.at[n], here, q).wait_recv()
                total = total + pyb[n]
            pzs[...] = total
            for k, scan in enumerate(column):
                go(send(pzs, pzb.at[k], p2s.at[k], p2r.at[k], scan, q))
        elif step == 2:
            yield_up(7, 0)
            total = pzs[...]
            for k, scan in enumerate(column):
                send(pzs, pzb.at[k], p2s.at[k], p2r.at[k], here, q).wait_recv()
                total = total + pzb[k]
            pg_ref[mine] = total * scale
            for n, scan, d in peers:
                go(send(pg_ref.at[mine], pg_ref.at[mine], p3s.at[n], p3r.at[n], scan, q))
    await_up(7, 0)
    landed(to_right)
    landed(to_left)
    combine(0, 0, tile_dev, [(rr3, zscale.at[0, 3], 0), (rl3, zscale.at[1, 3], 0)])
    out_ref[...] = total_ref[...]
    for n, source in enumerate(sources):
        send(pg_ref.at[source], pg_ref.at[source], p3s.at[n], p3r.at[n], here, q).wait_recv()
    for copy in sends:
        copy.wait_send()


def give_back(hot, codes, scales, probe_terms, tile_dev, scale):
    tile = codes.shape[1:]
    modes, pieces, rows, columns = probe_terms.shape
    piece = (rows, columns)
    dma = pltpu.SemaphoreType.DMA
    smem, vmem = (pl.BlockSpec(memory_space=space) for space in (pltpu.SMEM, pltpu.VMEM))
    chunk = pltpu.VMEM((tile_dev,) + tile, codes.dtype)
    part = pltpu.VMEM((tile_dev // 2,) + tile, codes.dtype)
    ring_scale = pltpu.VMEM((2, 4, tile_dev, columns), jnp.float32)
    return pl.pallas_call(
        functools.partial(return_kernel, scale=scale),
        in_specs=[smem, vmem, vmem, vmem],
        out_specs=[vmem, vmem],
        out_shape=[
            jax.ShapeDtypeStruct((tile_dev,) + tile, jnp.float32),
            jax.ShapeDtypeStruct((pieces,) + piece, jnp.float32),
        ],
        scratch_shapes=[pltpu.VMEM(codes.shape, codes.dtype), pltpu.VMEM(scales.shape, jnp.float32)]
        + [part, chunk, chunk, chunk] * 4
        + [
            ring_scale,
            ring_scale,
            pltpu.VMEM((tile_dev,) + tile, jnp.float32),
            pltpu.VMEM((modes - 1, pieces) + piece, jnp.float32),
            pltpu.VMEM((pieces,) + piece, jnp.float32),
            pltpu.VMEM((7,) + piece, jnp.float32),
            pltpu.VMEM(piece, jnp.float32),
            pltpu.VMEM((RING - 1,) + piece, jnp.float32),
            dma((2, 4)),
            dma((2, 4)),
            dma((2, 4)),
            dma((2, 4)),
            dma((7, 8)),
            dma((7, 8)),
            dma((7,)),
            dma((7,)),
            dma((modes - 1,)),
            dma((modes - 1,)),
            dma((7,)),
            dma((7,)),
            dma((RING - 1,)),
            dma((RING - 1,)),
            dma((7,)),
            dma((7,)),
        ],
        compiler_params=pltpu.CompilerParams(
            collective_id=2, has_side_effects=True, vmem_limit_bytes=48 * MIB
        ),
        name="give_back",
    )(hot, codes, scales, probe_terms)


def shards(object_tiles, tile_owner, block_tiles, positions, counts, probe):
    scan_count = lax.axis_size("scan")
    mode_count = lax.axis_size("mode")
    here = lax.axis_index("scan")
    q = lax.axis_index("mode").reshape(1)
    tile_dev, slices, parts, side = object_tiles.shape[:4]
    batch = positions.shape[0]
    span = scan_count // 2
    quarter = side // mode_count
    planes = slices * parts
    tables = jnp.asarray(transform_tables(side))

    y, z, core = spot(here)
    first = block_tiles[:, 0]
    total = tile_owner.shape[0]
    tile_range = jnp.arange(total, dtype=jnp.int32)
    same = (tile_owner[:, None] == tile_owner[None, :]) & (tile_range[None, :] < tile_range[:, None])
    rank = jnp.sum(same.astype(jnp.int32), axis=1)
    near = lax.dynamic_index_in_dim(first.reshape(4, RING, 2), z, 1, keepdims=False).reshape(8)
    ring = at_spot(y, jnp.arange(RING, dtype=jnp.int32), core)
    listed = (tile_range[None, :] >= near[:, None]) & (tile_range[None, :] < near[:, None] + scan_count)
    owned = tile_owner[None, :] == ring[:, None]
    sel = jnp.sum(jnp.where(listed[:, None, :] & owned[None, :, :], rank[None, None, :], 0), axis=2)
    hot = (sel[:, :, None] == jnp.arange(tile_dev, dtype=jnp.int32)).astype(jnp.float32).reshape(-1)
    my_first = lax.dynamic_index_in_dim(first, here, 0, keepdims=False)
    up, left = positions[:, 0] // side, positions[:, 1] // side
    down, right = jnp.minimum(up + 1, 1), jnp.minimum(left + 1, span - 1)
    slots = jnp.stack([up * span + left, up * span + right, down * span + left, down * span + right], axis=1)
    wanted = my_first + slots
    owner_y, owner_z, owner_core = spot(tile_owner)
    homes = (owner_y * 2 + owner_core) * RING + owner_z
    found = jnp.sum(jnp.where(wanted[:, :, None] == tile_range, homes, 0), axis=2)
    place = jnp.concatenate([found, positions % side], axis=1)

    terms, probe_terms = front(
        sel, place, object_tiles.reshape(tile_dev, planes, side, side), probe, counts, tables, mode_count
    )
    codes, scales = lay(place, q, terms.reshape(batch, planes, quarter, side), scan_count)
    summed, probe_grad = give_back(
        hot, codes, scales, probe_terms.reshape(mode_count, 8, parts * side // 8, side), tile_dev, 1.0 / (batch * scan_count)
    )
    return (summed.reshape(tile_dev, slices, parts, quarter, side), probe_grad.reshape(probe.shape))


def solution(mesh):
    placed = (
        P("scan", None, None, None, None),
        P(),
        P(),
        P("scan", None),
        P("scan", None, None),
        P("mode", None, None, None),
    )
    return jax.shard_map(
        shards,
        mesh=mesh,
        in_specs=placed,
        out_specs=(P("scan", None, None, "mode", None), P("mode", None, None, None)),
        check_vma=False,
    )
```

time: 371 us -> 124 us (0.33)
  waiting for transfers between devices: 263 us -> 0 us
  Pallas kernels: 20.2 us -> 110 us
  starting transfers between devices: 29.5 us -> 0 us
  blocking collectives: 28.6 us -> 0 us
  between operations: 16.1 us -> 0.77 us
    psum x1 -> x0, waiting for transfers between devices: 190 us -> none  [shards(): probe_grad = lax.psum(probe_part, 'scan') / (batch * scan_count)]
    pallas_call x4 -> x3, Pallas kernels: 20.2 us -> 110 us  [the longest x1 62.7 us: front(): pl.pallas_call(front_kernel, in_specs=[smem, smem, anywhere, anywhere, an...]
    all_to_all x3 -> x0, waiting for transfers between devices: 46.7 us -> none  [the longest x1 46.7 us: shards(): lax.all_to_all(part[local_rows], 'scan', split_axis=0, concat_axis=0, til...]
    all_to_all x3 -> x0, starting transfers between devices: 29.4 us -> none  [the longest x1 13.3 us: shards(): lax.all_to_all(part[local_rows], 'scan', split_axis=0, concat_axis=0, til...]
    reduce_scatter x1 -> x0, waiting for transfers between devices: 24.9 us -> none  [shards(): lax.psum_scatter(probe_terms, 'mode', scatter_dimension=0, tiled=True)]
    all_gather x1 -> x0, blocking collectives: 14.3 us -> none  [shards(): probe_all = lax.all_gather(probe, 'mode', axis=0, tiled=True)]
    all_to_all x1 -> x0, blocking collectives: 14.3 us -> none  [shards(): lax.all_to_all(terms, 'mode', split_axis=0, concat_axis=0, tiled=True)]
  transfers between devices with their start and end apart: 5 -> 0, of which waited for: 3 -> 0; matrix products, arithmetic and copies ran while one was open for 1% -> 0% of each run, Pallas kernels for 0% -> 0%
where the time goes in v3:
time: 124 us
  Pallas kernels  110 us (89%)
  local copies, waits for them, and re-layouts  8.55 us (7%)
  other arithmetic  4.51 us (4%)
    pallas_call x1, Pallas kernels, front(): pl.pallas_call(front_kernel, in_specs=[smem, smem, anywhere, anywhere, an...  62.7 us
    pallas_call x1, Pallas kernels, give_back(): pl.pallas_call(functools.partial(return_kernel, scale=scale), in_specs=[s...  44.7 us
    unnamed x11, local copies, waits for them, and re-layouts  6.78 us

profile of v3, /device:TPU:1, one launch (start us, length us, event | category | flops | bytes accessed | tf_op | source)
XLA Modules:
  0.0 123.5 jit_solution(8992034301870403800)
XLA Ops:
  0.7 0.8 multiply_add_fusion.2
  1.5 1.0 convert_reduce_fusion
  2.5 0.7 fusion.8
  3.2 0.8 copy.17
  4.0 0.9 fusion.13
  4.8 0.5 constant_dynamic-slice_fusion
  5.3 0.7 add_add_fusion
  6.0 0.2 select_reduce_fusion
  6.2 0.1 copy.20
  6.3 0.1 pad_add_fusion.place_ref
  6.4 0.1 reshape_squeeze.3
  6.5 0.1 ge.22
  6.6 0.8 fusion.2
  7.4 0.2 select_reduce_fusion.1.sel_ref
  7.6 0.1 fusion.1
  7.7 0.1 reshape.148.hot_ref
  7.8 0.0 copy-start
  7.8 1.2 copy-done
  9.0 0.0 copy-start.1
  9.0 1.2 copy-done.1
  10.2 0.0 copy-start.2
  10.2 1.2 copy-done.2
  11.5 0.0 copy-start.3
  11.5 0.9 copy-done.3
  12.4 62.7 %front.1 = (f32[4,4,4,32,128]{4,3,2,1,0:T(8,128)S(1)}, f32[4,2,128,128]{3,2,1,0:T(8,128)S(1)}) custom-call(s32[8,8]{1,0:T(8,128)S(1)} %select_reduce_fusion.1.sel_ref, s32[16,6]{1,0:T(8,128)S(1)} %pad_add_fusion.place_ref, bf16[8,4,128,128]{3,2,1,0:T(8,128)(2,1)S(1)} %bitcast.7, f32[1,2,128,128]{3,2,1,0:T(8,128)S(1)} %copy-done.3, ...), custom_call_target="tpu_custom_call" | custom-call | tf_op jit(solution)/shard_map/front/pallas_call | solution.py:315
  75.0 2.3 %lay.1 = (s16[64,4,32,128]{3,2,1,0:T(8,128)(2,1)S(1)}, f32[8,8,128]{2,1,0:T(8,128)S(1)}) custom-call(s32[16,6]{1,0:T(8,128)S(1)} %pad_add_fusion.place_ref, s32[1]{0:T(128)} %bitcast.1.q_ref, f32[16,4,32,128]{3,2,1,0:T(8,128)S(1)} %bitcast.8), custom_call_target="tpu_custom_call" | custom-call | tf_op jit(solution)/shard_map/lay/pallas_call | solution.py:402
  77.4 44.7 %give_back.1 = (f32[8,4,32,128]{3,2,1,0:T(8,128)S(1)}, f32[8,32,128]{2,1,0:T(8,128)S(1)}) custom-call(f32[512]{0:T(512)S(1)} %reshape.148.hot_ref, s16[64,4,32,128]{3,2,1,0:T(8,128)(2,1)S(1)} %get-tuple-element.9.canvas, f32[8,8,128]{2,1,0:T(8,128)S(1)} %get-tuple-element.10.cscale, f32[4,8,32,128]{3,2,1,0:T(8,128)S(1)} %bitcast.10), custom_call_target="tpu_custom_call" | custom-call | tf_op jit(solution)/shard_map/give_back/pallas_call | solution.py:562
  122.1 0.8 copy.23
  122.9 0.7 copy.24
  (5 shorter events, 0.1 us)
Async XLA Ops:
  7.8 1.2 copy-start
  9.0 1.2 copy-start.1
  10.2 1.2 copy-start.2
  11.5 0.9 copy-start.3

commit v4 on v3

v4 whole, which is shorter than its diff:
```python
import functools

import jax
import jax.numpy as jnp
import ml_dtypes
import numpy as np
from jax import lax
from jax.experimental import pallas as pl
from jax.experimental.pallas import tpu as pltpu
from jax.sharding import PartitionSpec as P

background = 0.25
fresnel_number = 1.0
MIB = 1024 * 1024
RING = 8
STEPS = 32767.0


def split_const(matrix):
    hi = matrix.astype(ml_dtypes.bfloat16)
    lo = (matrix - hi.astype(np.float64)).astype(ml_dtypes.bfloat16)
    return hi, lo


def transform_tables(side):
    index = np.arange(side)
    four = np.exp(-2j * np.pi * (index[:, None] * index[None, :] % side) / side) / np.sqrt(side)
    frequency = np.where(index < side // 2, index, index - side) / side
    chirp = np.exp(-1j * np.pi * fresnel_number * frequency * frequency)
    prop = (four.conj() * chirp[None, :]) @ four
    blocks = []
    for matrix in (four, prop):
        re, im = matrix.real, matrix.imag
        blocks.append(np.block([[re, im], [-im, re]]))
        blocks.append(np.block([[re, -im], [im, re]]))
    parts = []
    for block in blocks:
        parts.extend(split_const(block))
    return np.stack(parts)


def split_parts(value):
    hi = value.astype(jnp.bfloat16)
    lo = (value - hi.astype(jnp.float32)).astype(jnp.bfloat16)
    return hi, lo


def dot(a, b):
    return jnp.dot(a, b, preferred_element_type=jnp.float32)


def spot(scan):
    return scan // (2 * RING), scan // 2 % RING, scan % 2


def at_spot(y, z, core):
    return (y * RING + z) * 2 + core


def plane_peers(y, z, core):
    peers = []
    for number in range(1, 8):
        there_y, there_core = (y + number // 2) % 4, (core + number % 2) % 2
        peers.append((number - 1, at_spot(there_y, z, there_core), there_y * 2 + there_core))
    return peers


def plane_sources(y, core):
    return [(y - number // 2 + 4) % 4 * 2 + (core + number % 2) % 2 for number in range(1, 8)]


def send(src, dst, send_sem, recv_sem, scan, mode):
    return pltpu.make_async_remote_copy(
        src_ref=src,
        dst_ref=dst,
        send_sem=send_sem,
        recv_sem=recv_sem,
        device_id={"scan": scan, "mode": mode},
        device_id_type=pl.DeviceIdType.MESH,
    )


def meet(partners):
    barrier = pltpu.get_barrier_semaphore()
    for scan, mode in partners:
        pl.semaphore_signal(
            barrier, inc=1, device_id={"scan": scan, "mode": mode}, device_id_type=pl.DeviceIdType.MESH
        )
    pl.semaphore_wait(barrier, len(partners))


def home(owner):
    y, z, core = owner >> 4, (owner >> 1) & (RING - 1), owner & 1
    return (y * 2 + core) * RING + z


def front_kernel(owner_ref, first_ref, pos_ref, owner_rows, obj_ref, probe_ref, counts_any, tab_any, eq_ref, pg_ref, sel_out, *scratch):
    rings, (win0, win1, ybuf, xbuf, x_ref, pall_ref, counts_ref, tab_ref, ebuf, a_hi, a_lo, b_hi, b_lo, c_hi, c_lo, planes_ref, xroll, wave_ref, sum_ref, sel_ref, local_sem, zs, zr, ys, yr, xs, xr, ps, pr, es, er) = scratch[:16], scratch[16:]
    chunk = [rings[8 * l : 8 * l + 8] for l in range(2)]
    win = (win0, win1)
    here, q = lax.axis_index("scan"), lax.axis_index("mode")
    y, z, core = spot(here)
    mine = y * 2 + core
    tile_dev, _, quarter, side = chunk[0][0].shape
    modes, npos = x_ref.shape[1:3]
    local = [
        pltpu.make_async_copy(
            obj_ref.at[:, l, :, pl.ds(q * quarter, quarter), :], chunk[l][0], local_sem.at[l]
        )
        for l in range(2)
    ]
    local.extend(
        [
            pltpu.make_async_copy(probe_ref.at[0], pall_ref.at[q], local_sem.at[2]),
            pltpu.make_async_copy(tab_any, tab_ref, local_sem.at[3]),
            pltpu.make_async_copy(counts_any.at[pl.ds(q * npos, npos)], counts_ref, local_sem.at[4]),
        ]
    )
    for copy in local:
        copy.start()
    right, left = at_spot(y, (z + 1) % RING, core), at_spot(y, (z + RING - 1) % RING, core)
    peers = plane_peers(y, z, core)
    sources = plane_sources(y, core)
    others = [(q + k) % modes for k in range(1, modes)]
    froms = [(q + modes - 1 - k) % modes for k in range(modes - 1)]
    meet([(right, q), (left, q)] + [(scan, q) for _, scan, _ in peers] + [(here, m) for m in others])

    sends = []

    def go(copy):
        copy.start()
        sends.append(copy)
        return copy

    def pass_on(l, direction, step):
        if step == 3 and direction != l:
            return None
        rightward = chunk[l][0:4] + chunk[l][7:8]
        leftward = chunk[l][0:1] + chunk[l][4:8]
        lane = (rightward, leftward)[direction]
        scan = (right, left)[direction]
        return go(send(lane[step], lane[step + 1], zs.at[l, direction, step], zr.at[l, direction, step], scan, q))

    moving = {}

    def step_on(l, step):
        for direction in (0, 1):
            if step > 0:
                moving[l, direction].wait_recv()
            moving[l, direction] = pass_on(l, direction, step)

    for l in range(2):
        local[l].wait()
        if l == 0:
            step_on(0, 0)
    for k, m in enumerate(others):
        go(send(probe_ref.at[0], pall_ref.at[q], ps.at[k], pr.at[k], here, m))

    lanes = lax.broadcasted_iota(jnp.int32, (RING, side), 1)
    ring = at_spot(y, lax.broadcasted_iota(jnp.int32, (RING, side), 0), core)
    owned = [(owner_rows[n : n + 1, :] == ring).astype(jnp.int32) for n in range(owner_rows.shape[0])]
    table = jnp.zeros((RING, side), jnp.int32)
    for d in range(8):
        first = first_ref[at_spot(d // 2, z, d % 2), 0]
        before = jnp.zeros((RING, side), jnp.int32)
        for n, hit in enumerate(owned):
            before = before + jnp.where(lanes + n * side < first, hit, 0)
        table = jnp.where(lanes == d, jnp.sum(before, axis=1, keepdims=True), table)
    sel_out[...] = table
    sel_copy = pltpu.make_async_copy(sel_out, sel_ref, local_sem.at[5])
    sel_copy.start()
    sel_copy.wait()

    rounds = [0, -1, 1, -2, 2, -3, 3, 4]

    def offer(l, r):
        zi = (z + rounds[r] + RING) % RING
        buf = chunk[l][(0, 1, 4, 2, 5, 3, 6, 7)[r]]
        for n, scan, d in peers:
            ybuf[l, n, r] = buf[sel_ref[zi, d]]
            go(send(ybuf.at[l, n, r], win[l].at[mine * RING + zi], ys.at[l, n, r], yr.at[l, n, r], scan, q))
        win[l][mine * RING + zi] = buf[sel_ref[zi, mine]]

    def await_window(l):
        for r in range(RING):
            zi = (z + rounds[r] + RING) % RING
            for n, source in enumerate(sources):
                send(ybuf.at[l, n, r], win[l].at[source * RING + zi], ys.at[l, n, r], yr.at[l, n, r], here, q).wait_recv()

    my_first = first_ref[here, 0]
    span = first_ref.shape[0] // 2
    shape = (2, quarter, side)
    rows = lax.broadcasted_iota(jnp.int32, shape, 1) + q * quarter
    cols = lax.broadcasted_iota(jnp.int32, shape, 2)

    def piece(l, j):
        row, col = pos_ref[j, 0], pos_ref[j, 1]
        near = my_first + (col >> 7)
        far = my_first + jnp.minimum((col >> 7) + 1, span - 1)
        tiles = [win[l][home(owner_ref[t])].astype(jnp.float32) for t in (near, far, near + span, far + span)]
        kept = cols >= (col & (side - 1))
        upper = jnp.where(kept, tiles[0], tiles[1])
        lower = jnp.where(kept, tiles[2], tiles[3])
        return jnp.where(rows >= row, upper, lower).astype(jnp.bfloat16)

    def x_copy(l, k, i, mode, target):
        return send(xbuf.at[l, k, i], x_ref.at[l, target, i], xs.at[l, k, i], xr.at[l, k, i], here, mode)

    def share(l):
        def pack(i, carry):
            for k in (1, 0, 2):
                xbuf[l, k, i] = piece(l, others[k] * npos + i)
                x_copy(l, k, i, others[k], q).start()
            x_ref[l, q, i] = piece(l, q * npos + i)
            return carry

        lax.fori_loop(0, npos, pack, 0)

    offer(0, 0)
    step_on(0, 1)
    step_on(1, 0)
    offer(0, 1)
    offer(0, 2)
    step_on(0, 2)
    step_on(1, 1)
    offer(0, 3)
    offer(0, 4)
    offer(1, 0)
    step_on(0, 3)
    step_on(1, 2)
    offer(0, 5)
    offer(0, 6)
    offer(1, 1)
    offer(1, 2)
    moving[0, 0].wait_recv()
    offer(0, 7)
    step_on(1, 3)
    offer(1, 3)
    offer(1, 4)
    offer(1, 5)
    offer(1, 6)
    await_window(0)
    share(0)
    moving[1, 1].wait_recv()
    offer(1, 7)
    for copy in local[2:]:
        copy.wait()
    for k in range(modes - 1):
        send(probe_ref.at[0], pall_ref.at[froms[k]], ps.at[k], pr.at[k], here, q).wait_recv()

    def block(m):
        return slice(m * side, (m + 1) * side)

    def load(hi_ref, lo_ref, fields):
        for m, (re, im) in enumerate(fields):
            rh, rl = split_parts(re)
            ih, il = split_parts(im)
            hi_ref[block(m), 0:side] = rh
            hi_ref[block(m), side : 2 * side] = ih
            lo_ref[block(m), 0:side] = rl
            lo_ref[block(m), side : 2 * side] = il

    def two_sided(right_table, left_table, hi_ref, lo_ref):
        for m in range(modes):
            bh, bl = tab_ref[2 * right_table], tab_ref[2 * right_table + 1]
            whole = dot(hi_ref[block(m)], bh) + dot(lo_ref[block(m)], bh) + dot(hi_ref[block(m)], bl)
            hi, lo = split_parts(whole)
            c_hi[0:side, block(m)] = hi[:, 0:side]
            c_hi[side : 2 * side, block(m)] = hi[:, side : 2 * side]
            c_lo[0:side, block(m)] = lo[:, 0:side]
            c_lo[side : 2 * side, block(m)] = lo[:, side : 2 * side]
        lh, ll = tab_ref[2 * left_table], tab_ref[2 * left_table + 1]
        out = []
        for h in range(modes // 2):
            cut = slice(h * 2 * side, (h + 1) * 2 * side)
            whole = dot(lh, c_hi[:, cut]) + dot(lh, c_lo[:, cut]) + dot(ll, c_hi[:, cut])
            for k in range(2):
                out.append((whole[0:side, block(k)], whole[side : 2 * side, block(k)]))
        return out

    def patch(l, p):
        for k in range(modes - 1):
            x_copy(l, k, p, q, froms[k]).wait_recv()
        row, col = pos_ref[q * npos + p, 0], pos_ref[q * npos + p, 1]
        for part in range(2):
            whole = jnp.concatenate([x_ref[l, k, p, part].astype(jnp.float32) for k in range(modes)], axis=0)
            whole = pltpu.roll(whole, (side - row) & (side - 1), 0)
            planes_ref[part] = pltpu.roll(whole, (side - (col & (side - 1))) & (side - 1), 1)

    def times(wave, field):
        (wr, wi), (fr, fi) = wave, field
        return wr * fr - wi * fi, wr * fi + wi * fr

    def conj_times(wave, field):
        (wr, wi), (fr, fi) = wave, field
        return wr * fr + wi * fi, wr * fi - wi * fr

    def e_copy(l, k, p, mode, target):
        return send(ebuf.at[l, k, p], eq_ref.at[l, target, p], es.at[l, k, p], er.at[l, k, p], here, mode)

    def hand_out(l, p, total):
        row, col = pos_ref[q * npos + p, 0], pos_ref[q * npos + p, 1]
        for part in range(2):
            sum_ref[part] = pltpu.roll(pltpu.roll(total[part], row & (side - 1), 0), col & (side - 1), 1)
        for k in range(modes - 1):
            cut = pl.ds(pl.multiple_of(others[k] * quarter, quarter), quarter)
            for part in range(2):
                ebuf[l, k, p, part] = sum_ref[part, cut]
            e_copy(l, k, p, others[k], q).start()
        cut = pl.ds(pl.multiple_of(q * quarter, quarter), quarter)
        for part in range(2):
            eq_ref[l, q, p, part] = sum_ref[part, cut]

    def enter(p, carry):
        patch(0, p)
        for part in range(2):
            xroll[p, part] = planes_ref[part]
        load(a_hi, a_lo, [times((pall_ref[m, 0], pall_ref[m, 1]), (planes_ref[0], planes_ref[1])) for m in range(modes)])
        for m, (re, im) in enumerate(two_sided(2, 3, a_hi, a_lo)):
            wave_ref[p, m, 0] = re
            wave_ref[p, m, 1] = im
        return carry

    lax.fori_loop(0, npos, enter, 0)
    await_window(1)
    share(1)

    def detect(p, carry):
        patch(1, p)
        load(a_hi, a_lo, [times((wave_ref[p, m, 0], wave_ref[p, m, 1]), (planes_ref[0], planes_ref[1])) for m in range(modes)])
        far = two_sided(0, 1, a_hi, a_lo)
        intensity = background
        for re, im in far:
            intensity = intensity + (re * re + im * im)
        weight = 1.0 - counts_ref[p].astype(jnp.float32) / intensity
        load(a_hi, a_lo, [(weight * re, weight * im) for re, im in far])
        grads = two_sided(1, 0, a_hi, a_lo)
        load(b_hi.at[p], b_lo.at[p], [conj_times((planes_ref[0], planes_ref[1]), grad) for grad in grads])
        terms = [conj_times((wave_ref[p, m, 0], wave_ref[p, m, 1]), grad) for m, grad in enumerate(grads)]
        hand_out(1, p, [functools.reduce(jnp.add, part) for part in zip(*terms)])
        return carry

    lax.fori_loop(0, npos, detect, 0)
    pg_ref[...] = jnp.zeros_like(pg_ref)

    def leave(p, carry):
        grads = two_sided(3, 2, b_hi.at[p], b_lo.at[p])
        for m, grad in enumerate(grads):
            re, im = conj_times((xroll[p, 0], xroll[p, 1]), grad)
            pg_ref[m, 0] += re
            pg_ref[m, 1] += im
        terms = [conj_times((pall_ref[m, 0], pall_ref[m, 1]), grad) for m, grad in enumerate(grads)]
        hand_out(0, p, [functools.reduce(jnp.add, part) for part in zip(*terms)])
        return carry

    lax.fori_loop(0, npos, leave, 0)

    def finish(p, carry):
        for l in (1, 0):
            for k in range(modes - 1):
                e_copy(l, k, p, q, froms[k]).wait_recv()
                e_copy(l, k, p, others[k], q).wait_send()
                x_copy(l, k, p, others[k], q).wait_send()
        return carry

    lax.fori_loop(0, npos, finish, 0)
    for copy in sends:
        copy.wait_send()


def front(tile_owner, block_tiles, positions, tiles, probe, counts, tables, modes):
    tile_dev, slices, parts, side, _ = tiles.shape
    quarter = side // modes
    npos = positions.shape[0] // modes
    dma = pltpu.SemaphoreType.DMA
    smem, anywhere, vmem = (pl.BlockSpec(memory_space=space) for space in (pltpu.SMEM, pl.ANY, pltpu.VMEM))
    tile = (parts, quarter, side)
    field = pltpu.VMEM((modes * side, 2 * side), jnp.bfloat16)
    saved = pltpu.VMEM((npos, modes * side, 2 * side), jnp.bfloat16)
    column = pltpu.VMEM((2 * side, modes * side), jnp.bfloat16)
    plane = pltpu.VMEM((parts, side, side), jnp.float32)
    return pl.pallas_call(
        front_kernel,
        in_specs=[smem, smem, smem, vmem, anywhere, anywhere, anywhere, anywhere],
        out_specs=[vmem, vmem, vmem],
        out_shape=[
            jax.ShapeDtypeStruct((slices, modes, npos) + tile, jnp.float32),
            jax.ShapeDtypeStruct((modes,) + probe.shape[1:], jnp.float32),
            jax.ShapeDtypeStruct((RING, side), jnp.int32),
        ],
        scratch_shapes=[pltpu.VMEM((tile_dev,) + tile, tiles.dtype)] * 16
        + [
            pltpu.VMEM((8 * RING,) + tile, tiles.dtype),
            pltpu.VMEM((8 * RING,) + tile, tiles.dtype),
            pltpu.VMEM((slices, 7, RING) + tile, tiles.dtype),
            pltpu.VMEM((slices, modes - 1, npos) + tile, tiles.dtype),
            pltpu.VMEM((slices, modes, npos) + tile, tiles.dtype),
            pltpu.VMEM((modes,) + probe.shape[1:], probe.dtype),
            pltpu.VMEM((npos, side, side), counts.dtype),
            pltpu.VMEM(tables.shape, tables.dtype),
            pltpu.VMEM((slices, modes - 1, npos) + tile, jnp.float32),
            field,
            field,
            saved,
            saved,
            column,
            column,
            plane,
            pltpu.VMEM((npos, parts, side, side), jnp.float32),
            pltpu.VMEM((npos, modes, parts, side, side), jnp.float32),
            plane,
            pltpu.SMEM((RING, side), jnp.int32),
            dma((6,)),
            dma((slices, 2, 4)),
            dma((slices, 2, 4)),
            dma((slices, 7, RING)),
            dma((slices, 7, RING)),
            dma((slices, modes - 1, npos)),
            dma((slices, modes - 1, npos)),
            dma((modes - 1,)),
            dma((modes - 1,)),
            dma((slices, modes - 1, npos)),
            dma((slices, modes - 1, npos)),
        ],
        compiler_params=pltpu.CompilerParams(
            collective_id=0, has_side_effects=True, vmem_limit_bytes=60 * MIB
        ),
        name="front",
    )(tile_owner, block_tiles, positions, tile_owner.reshape(-1, side), tiles, probe, counts, tables)


def column_scale(value):
    most = jnp.max(jnp.max(jnp.abs(value), axis=0), axis=0, keepdims=True)
    return jnp.maximum(most, 1e-30) * (1.0 / STEPS)


def encode(value, scale):
    return jnp.round(value * (1.0 / scale)).astype(jnp.int32).astype(jnp.int16)


def decode(code):
    return code.astype(jnp.int32).astype(jnp.float32)


def lay_kernel(owner_ref, first_ref, pos_ref, at_ref, e_ref, code_ref, scale_ref, canvas):
    slices, batch, _, quarter, side = e_ref.shape
    here, q = at_ref[0], at_ref[1]
    my_first = first_ref[here, 0]
    span = first_ref.shape[0] // 2
    canvas[...] = jnp.zeros_like(canvas)
    shape = e_ref.shape[2:]
    rows = lax.broadcasted_iota(jnp.int32, shape, 1) + q * quarter
    cols = lax.broadcasted_iota(jnp.int32, shape, 2)

    def position(j, carry):
        row, col = pos_ref[j, 0], pos_ref[j, 1]
        near = my_first + (col >> 7)
        far = my_first + jnp.minimum((col >> 7) + 1, span - 1)
        spots = [home(owner_ref[t]) for t in (near, far, near + span, far + span)]
        up = rows >= row
        kept = cols >= (col & (side - 1))
        for l in range(slices):
            term = e_ref[l, j]
            upper = jnp.where(up, term, 0.0)
            lower = jnp.where(up, 0.0, term)
            canvas[l, spots[0]] += jnp.where(kept, upper, 0.0)
            canvas[l, spots[1]] += jnp.where(kept, 0.0, upper)
            canvas[l, spots[2]] += jnp.where(kept, lower, 0.0)
            canvas[l, spots[3]] += jnp.where(kept, 0.0, lower)
        return carry

    lax.fori_loop(0, batch, position, 0)

    def group(d, carry):
        for l in range(slices):
            for k in range(RING):
                value = canvas[l, d * RING + k]
                scale = column_scale(value)
                scale_ref[l, d, k : k + 1, :] = scale
                code_ref[l, d * RING + k] = encode(value, scale)
        return carry

    lax.fori_loop(0, scale_ref.shape[1], group, 0)


def lay(tile_owner, block_tiles, positions, at, terms, slots):
    smem, vmem = (pl.BlockSpec(memory_space=space) for space in (pltpu.SMEM, pltpu.VMEM))
    slices, tile = terms.shape[0], terms.shape[2:]
    return pl.pallas_call(
        lay_kernel,
        in_specs=[smem, smem, smem, smem, vmem],
        out_specs=[vmem, vmem],
        out_shape=[
            jax.ShapeDtypeStruct((slices, slots) + tile, jnp.int16),
            jax.ShapeDtypeStruct((slices, slots // RING, RING, terms.shape[-1]), jnp.float32),
        ],
        scratch_shapes=[pltpu.VMEM((slices, slots) + tile, jnp.float32)],
        compiler_params=pltpu.CompilerParams(vmem_limit_bytes=32 * MIB),
        name="lay",
    )(tile_owner, block_tiles, positions, at, terms)


def return_kernel(sel_ref, canvas, cscale, pp_ref, out_ref, pg_ref, *scratch, scale=1.0):
    rings, (rbuf, rscale, sscale, zscale, total_ref, pxb, pxs, pyb, pzs, pzb, zs, zr, zcs, zcr, ys, yr, ycs, ycr, p0s, p0r, p1s, p1r, p2s, p2r, p3s, p3r) = scratch[:32], scratch[32:]
    out_of = [[rings[16 * l + 4 * direction : 16 * l + 4 * direction + 4] for direction in range(2)] for l in range(2)]
    into = [[rings[16 * l + 8 + 4 * direction : 16 * l + 12 + 4 * direction] for direction in range(2)] for l in range(2)]
    here, q = lax.axis_index("scan"), lax.axis_index("mode")
    y, z, core = spot(here)
    mine = y * 2 + core
    tile_dev = out_ref.shape[0]
    modes = pp_ref.shape[0]
    right, left = at_spot(y, (z + 1) % RING, core), at_spot(y, (z + RING - 1) % RING, core)
    peers = plane_peers(y, z, core)
    sources = plane_sources(y, core)
    column = [at_spot(y, (z + k) % RING, core) for k in range(1, RING)]
    others = [(q + k) % modes for k in range(1, modes)]
    meet([(scan, q) for scan in column] + [(scan, q) for _, scan, _ in peers] + [(here, m) for m in others])
    sends = []

    def go(copy):
        copy.start()
        sends.append(copy)
        return copy

    rounds = [4, 3, -3, 2, -2, 1, -1, 0]

    def zi(r):
        return (z + rounds[r] + RING) % RING

    def yield_up(l, r):
        for n, scan, d in peers:
            go(send(canvas.at[l, d * RING + zi(r)], rbuf.at[l, mine * RING + zi(r)], ys.at[l, n, r], yr.at[l, n, r], scan, q))

    def await_up(l, r):
        for n, source in enumerate(sources):
            at = source * RING + zi(r)
            send(canvas.at[l, at], rbuf.at[l, at], ys.at[l, n, r], yr.at[l, n, r], here, q).wait_recv()

    def combine(l, r, received):
        place = zi(r)
        steps = [cscale[l, mine, pl.ds(place, 1)]] + [rscale[l, source, pl.ds(place, 1)] for source in sources]
        chosen = [sel_ref[place, giver] for giver in [mine] + sources]
        weights = [[jnp.where(pick == k, 1.0, 0.0) for k in range(tile_dev)] for pick in chosen]

        def plane(part, carry):
            terms = [decode(canvas[l, mine * RING + place, part]) * steps[0]]
            terms.extend(
                decode(rbuf[l, source * RING + place, part]) * step for source, step in zip(sources, steps[1:])
            )
            for k in range(tile_dev):
                total = weights[0][k] * terms[0]
                for weight, term in zip(weights[1:], terms[1:]):
                    total = total + weight[k] * term
                for ref, ref_scale in received:
                    total = total + decode(ref[k, part]) * ref_scale[k : k + 1]
                total_ref[k, part] = total
            return carry

        lax.fori_loop(0, total_ref.shape[1], plane, 0)

    def ship(l, direction, step):
        buf, to = out_of[l][direction][step], into[l][direction][step]
        for k in range(tile_dev):
            value = total_ref[k]
            step_size = column_scale(value)
            sscale[l, direction, step, k : k + 1] = step_size
            buf[k] = encode(value, step_size)
        at = (l, direction, step)
        scan = (right, left)[direction]
        return (
            go(send(sscale.at[at], zscale.at[at], zcs.at[at], zcr.at[at], scan, q)),
            go(send(buf, to, zs.at[at], zr.at[at], scan, q)),
        )

    moving = {}

    def arrived(l, direction, step):
        if step == 0 or (l, direction) not in moving:
            return []
        for copy in moving[l, direction]:
            copy.wait_recv()
        return [(into[l][direction][step - 1], zscale.at[l, direction, step - 1])]

    def turn(l, step):
        if step == 0:
            await_up(l, 0)
            combine(l, 0, [])
            moving[l, l] = ship(l, l, 0)
            return
        for direction in (l, 1 - l):
            r = 2 * step - 1 + direction
            await_up(l, r)
            combine(l, r, arrived(l, direction, step))
            moving[l, direction] = ship(l, direction, step)

    for n, scan, d in peers:
        for l in range(2):
            go(send(cscale.at[l, d], rscale.at[l, mine], ycs.at[l, n], ycr.at[l, n], scan, q))
    for r in range(3):
        for l in range(2):
            yield_up(l, r)
    for k, m in enumerate(others):
        go(send(pp_ref.at[m], pxb.at[k], p0s.at[k], p0r.at[k], here, m))
    for n, source in enumerate(sources):
        for l in range(2):
            send(cscale.at[l, source], rscale.at[l, source], ycs.at[l, n], ycr.at[l, n], here, q).wait_recv()
    turn(0, 0)
    turn(1, 0)
    for r in (3, 4):
        for l in range(2):
            yield_up(l, r)
    total = pp_ref[q]
    for k in range(modes - 1):
        send(pp_ref.at[q], pxb.at[k], p0s.at[k], p0r.at[k], here, q).wait_recv()
        total = total + pxb[k]
    pxs[...] = total
    for n, scan, d in peers:
        go(send(pxs.at[d], pyb.at[n], p1s.at[n], p1r.at[n], scan, q))
    turn(0, 1)
    turn(1, 1)
    for r in (5, 6):
        for l in range(2):
            yield_up(l, r)
    total = pxs[mine]
    for n, source in enumerate(sources):
        send(pxs.at[source], pyb.at[n], p1s.at[n], p1r.at[n], here, q).wait_recv()
        total = total + pyb[n]
    pzs[...] = total
    for k, scan in enumerate(column):
        go(send(pzs, pzb.at[k], p2s.at[k], p2r.at[k], scan, q))
    turn(0, 2)
    turn(1, 2)
    for l in range(2):
        yield_up(l, 7)
    for k, scan in enumerate(column):
        send(pzs, pzb.at[k], p2s.at[k], p2r.at[k], here, q).wait_recv()
        total = total + pzb[k]
    pg_ref[mine] = total * scale
    for n, scan, d in peers:
        go(send(pg_ref.at[mine], pg_ref.at[mine], p3s.at[n], p3r.at[n], scan, q))
    turn(0, 3)
    turn(1, 3)
    for l in range(2):
        await_up(l, 7)
        combine(l, 7, arrived(l, 0, 4) + arrived(l, 1, 4))
        out_ref[:, l] = total_ref[...]
    for n, source in enumerate(sources):
        send(pg_ref.at[source], pg_ref.at[source], p3s.at[n], p3r.at[n], here, q).wait_recv()
    for copy in sends:
        copy.wait_send()


def give_back(sel, codes, scales, probe_terms, tile_dev, scale):
    slices, tile = codes.shape[0], codes.shape[2:]
    modes, pieces, rows, columns = probe_terms.shape
    piece = (rows, columns)
    dma = pltpu.SemaphoreType.DMA
    smem, vmem = (pl.BlockSpec(memory_space=space) for space in (pltpu.SMEM, pltpu.VMEM))
    ring_scale = pltpu.VMEM((slices, 2, 4, tile_dev, columns), jnp.float32)
    return pl.pallas_call(
        functools.partial(return_kernel, scale=scale),
        in_specs=[smem, vmem, vmem, vmem],
        out_specs=[vmem, vmem],
        out_shape=[
            jax.ShapeDtypeStruct((tile_dev, slices) + tile, jnp.float32),
            jax.ShapeDtypeStruct((pieces,) + piece, jnp.float32),
        ],
        scratch_shapes=[pltpu.VMEM((tile_dev,) + tile, codes.dtype)] * 32
        + [
            pltpu.VMEM(codes.shape, codes.dtype),
            pltpu.VMEM(scales.shape, jnp.float32),
            ring_scale,
            ring_scale,
            pltpu.VMEM((tile_dev,) + tile, jnp.float32),
            pltpu.VMEM((modes - 1, pieces) + piece, jnp.float32),
            pltpu.VMEM((pieces,) + piece, jnp.float32),
            pltpu.VMEM((7,) + piece, jnp.float32),
            pltpu.VMEM(piece, jnp.float32),
            pltpu.VMEM((RING - 1,) + piece, jnp.float32),
            dma((slices, 2, 4)),
            dma((slices, 2, 4)),
            dma((slices, 2, 4)),
            dma((slices, 2, 4)),
            dma((slices, 7, RING)),
            dma((slices, 7, RING)),
            dma((slices, 7)),
            dma((slices, 7)),
            dma((modes - 1,)),
            dma((modes - 1,)),
            dma((7,)),
            dma((7,)),
            dma((RING - 1,)),
            dma((RING - 1,)),
            dma((7,)),
            dma((7,)),
        ],
        compiler_params=pltpu.CompilerParams(
            collective_id=2, has_side_effects=True, vmem_limit_bytes=60 * MIB
        ),
        name="give_back",
    )(sel, codes, scales, probe_terms)


def shards(object_tiles, tile_owner, block_tiles, positions, counts, probe):
    scan_count = lax.axis_size("scan")
    mode_count = lax.axis_size("mode")
    at = jnp.stack([lax.axis_index("scan"), lax.axis_index("mode")])
    tile_dev, slices, parts, side = object_tiles.shape[:4]
    batch = positions.shape[0]
    quarter = side // mode_count
    tables = jnp.asarray(transform_tables(side))
    terms, probe_terms, sel = front(tile_owner, block_tiles, positions, object_tiles, probe, counts, tables, mode_count)
    terms = terms.reshape(slices, batch, parts, quarter, side)
    codes, scales = lay(tile_owner, block_tiles, positions, at, terms, scan_count)
    summed, probe_grad = give_back(
        sel, codes, scales, probe_terms.reshape(mode_count, 8, parts * side // 8, side), tile_dev, 1.0 / (batch * scan_count)
    )
    return (summed, probe_grad.reshape(probe.shape))


def solution(mesh):
    placed = (
        P("scan", None, None, None, None),
        P(),
        P(),
        P("scan", None),
        P("scan", None, None),
        P("mode", None, None, None),
    )
    return jax.shard_map(
        shards,
        mesh=mesh,
        in_specs=placed,
        out_specs=(P("scan", None, None, "mode", None), P("mode", None, None, None)),
        check_vma=False,
    )
```

time: 124 us -> 130 us (1.048)
  Pallas kernels: 110 us -> 121 us
  other arithmetic: 4.51 us -> 0.08 us
    pallas_call x2, Pallas kernels: 65 us -> 72.6 us  [the longest x1 69.5 us: front(): pl.pallas_call(front_kernel, in_specs=[smem, smem, smem, vmem, anywhere,...]
    pallas_call x1, Pallas kernels: 44.7 us -> 48.3 us  [give_back(): pl.pallas_call(functools.partial(return_kernel, scale=scale), in_specs=[s...]
    add x6 -> x0, other arithmetic: 2.15 us -> none  [the longest x1 0.77 us: shards(): up * span + left]
    reduce_sum x3 -> x0, other arithmetic: 1.44 us -> none  [the longest x1 1 us: shards(): rank = jnp.sum(same.astype(jnp.int32), axis=1)]
    unnamed x11 -> x15, local copies, waits for them, and re-layouts: 6.78 us -> 8 us
where the time goes in v4:
time: 130 us
  Pallas kernels  121 us (93%)
  local copies, waits for them, and re-layouts  8 us (6%)
    pallas_call x1, Pallas kernels, front(): pl.pallas_call(front_kernel, in_specs=[smem, smem, smem, vmem, anywhere,...  69.5 us
    pallas_call x1, Pallas kernels, give_back(): pl.pallas_call(functools.partial(return_kernel, scale=scale), in_specs=[s...  48.3 us
    unnamed x15, local copies, waits for them, and re-layouts  8 us
    pallas_call x1, Pallas kernels, lay(): pl.pallas_call(lay_kernel, in_specs=[smem, smem, smem, smem, vmem], out_s...  3.04 us

profile of v4, /device:TPU:1, one launch (start us, length us, event | category | flops | bytes accessed | tf_op | source)
XLA Modules:
  0.0 129.7 jit_solution(16873482591442184269)
XLA Ops:
  0.6 0.0 copy-start.5
  0.6 0.0 copy-start.2
  0.7 0.1 pad_add_fusion.at_ref
  0.7 1.4 %copy.9.pos_ref = s32[16,2]{1,0:T(8,128)} copy(s32[16,2]{0,1:T(2,128)} %param.10) | data formatting | bytes 256 | tf_op args[3]
  2.1 0.0 copy-start.3
  2.1 69.5 %front.1 = (f32[2,4,4,2,32,128]{5,4,3,2,1,0:T(8,128)}, f32[4,2,128,128]{3,2,1,0:T(8,128)}, s32[8,128]{1,0:T(8,128)}) custom-call(s32[512]{0:T(512)} %owner_ref.3, s32[64,64]{1,0:T(8,128)} %first_ref.3, s32[16,2]{1,0:T(8,128)} %copy.9.pos_ref, s32[4,128]{1,0:T(4,128)} %bitcast.7, bf16[8,2,2,128,128]{4,3,2,1,0:T(8,128)(2,1)} %obj_ref.1, ...), custom_call_target="tpu_custom_call" | custom-call | tf_op jit(solution)/shard_map/front/pallas_call | solution.py:382
  71.6 0.0 copy-done.5
  71.6 0.0 copy-done.2
  71.6 0.0 copy-done.3
  71.7 0.0 copy-start.1
  71.7 1.2 copy-done.1
  72.9 3.0 %lay.1 = (s16[2,64,2,32,128]{4,3,2,1,0:T(8,128)(2,1)S(1)}, f32[2,8,8,128]{3,2,1,0:T(8,128)S(1)}) custom-call(s32[512]{0:T(512)S(1)} %copy-done.5, s32[64,64]{1,0:T(8,128)S(1)} %copy-done.2, s32[16,2]{1,0:T(8,128)S(1)} %copy-done.3, s32[2]{0:T(128)S(1)} %pad_add_fusion.at_ref, f32[2,16,2,32,128]{4,3,2,1,0:T(8,128)S(1)} %bitcast.6), custom_call_target="tpu_custom_call" | custom-call | tf_op jit(solution)/shard_map/lay/pallas_call | solution.py:489
  75.9 0.0 copy-start
  75.9 1.3 %copy-done = s16[2,64,2,32,128]{4,3,2,1,0:T(8,128)(2,1)} copy-done((s16[2,64,2,32,128]{4,3,2,1,0:T(8,128)(2,1)}, s16[2,64,2,32,128]{4,3,2,1,0:T(8,128)(2,1)S(1)}, u32[]{:S(2)}) %copy-start) | copy-done | bytes 2097176
  77.3 0.0 copy-start.4
  77.3 0.6 copy-done.4
  77.9 48.3 %give_back.1 = (f32[8,2,2,32,128]{4,3,2,1,0:T(8,128)}, f32[8,32,128]{2,1,0:T(8,128)}) custom-call(s32[8,128]{1,0:T(8,128)} %get-tuple-element.9.sel_ref, s16[2,64,2,32,128]{4,3,2,1,0:T(8,128)(2,1)} %copy-done, f32[2,8,8,128]{3,2,1,0:T(8,128)} %copy-done.4, f32[4,8,32,128]{3,2,1,0:T(8,128)} %bitcast.8), custom_call_target="tpu_custom_call" | custom-call | tf_op jit(solution)/shard_map/give_back/pallas_call | solution.py:660
  126.2 1.9 %copy.13 = f32[8,2,2,32,128]{4,3,2,1,0:T(8,128)} copy(f32[8,2,2,32,128]{4,3,2,1,0:T(8,128)} %get-tuple-element.18) | data formatting | bytes 1048576
  128.1 1.6 %copy.14 = f32[1,2,128,128]{3,2,1,0:T(8,128)} copy(f32[1,2,128,128]{3,2,1,0:T(8,128)} %bitcast.9) | data formatting | bytes 262144
Async XLA Ops:
  0.6 71.0 %copy-start.5 = (s32[512]{0:T(512)S(1)}, s32[512]{0:T(512)}, u32[]{:S(2)}) copy-start(s32[512]{0:T(512)} %owner_ref.3) | copy-start | bytes 6148
  0.6 71.0 %copy-start.2 = (s32[64,64]{1,0:T(8,128)S(1)}, s32[64,64]{1,0:T(8,128)}, u32[]{:S(2)}) copy-start(s32[64,64]{1,0:T(8,128)} %first_ref.3) | copy-start | bytes 49156
  2.1 69.6 %copy-start.3 = (s32[16,2]{1,0:T(8,128)S(1)}, s32[16,2]{1,0:T(8,128)}, u32[]{:S(2)}) copy-start(s32[16,2]{1,0:T(8,128)} %copy.9.pos_ref) | copy-start | bytes 388
  71.7 1.2 copy-start.1
  75.9 1.3 %copy-start = (s16[2,64,2,32,128]{4,3,2,1,0:T(8,128)(2,1)}, s16[2,64,2,32,128]{4,3,2,1,0:T(8,128)(2,1)S(1)}, u32[]{:S(2)}) copy-start(s16[2,64,2,32,128]{4,3,2,1,0:T(8,128)(2,1)S(1)} %get-tuple-element.11.canvas) | copy-start | bytes 6291460
  77.3 0.6 copy-start.4

commit v5 on v4

v5 whole, which is shorter than its diff:
```python
import functools

import jax
import jax.numpy as jnp
import ml_dtypes
import numpy as np
from jax import lax
from jax.experimental import pallas as pl
from jax.experimental.pallas import tpu as pltpu
from jax.sharding import PartitionSpec as P

background = 0.25
fresnel_number = 1.0
MIB = 1024 * 1024
RING = 8
STEPS = 32767.0


def split_const(matrix):
    hi = matrix.astype(ml_dtypes.bfloat16)
    lo = (matrix - hi.astype(np.float64)).astype(ml_dtypes.bfloat16)
    return hi, lo


def transform_tables(side):
    index = np.arange(side)
    four = np.exp(-2j * np.pi * (index[:, None] * index[None, :] % side) / side) / np.sqrt(side)
    frequency = np.where(index < side // 2, index, index - side) / side
    chirp = np.exp(-1j * np.pi * fresnel_number * frequency * frequency)
    prop = (four.conj() * chirp[None, :]) @ four
    blocks = []
    for matrix in (four, prop):
        re, im = matrix.real, matrix.imag
        blocks.append(np.block([[re, im], [-im, re]]))
        blocks.append(np.block([[re, -im], [im, re]]))
    parts = []
    for block in blocks:
        parts.extend(split_const(block))
    return np.stack(parts)


def split_parts(value):
    hi = value.astype(jnp.bfloat16)
    lo = (value - hi.astype(jnp.float32)).astype(jnp.bfloat16)
    return hi, lo


def dot(a, b):
    return jnp.dot(a, b, preferred_element_type=jnp.float32)


def spot(scan):
    return scan // (2 * RING), scan // 2 % RING, scan % 2


def at_spot(y, z, core):
    return (y * RING + z) * 2 + core


def plane_peers(y, z, core):
    peers = []
    for number in range(1, 8):
        there_y, there_core = (y + number // 2) % 4, (core + number % 2) % 2
        peers.append((number - 1, at_spot(there_y, z, there_core), there_y * 2 + there_core))
    return peers


def plane_sources(y, core):
    return [(y - number // 2 + 4) % 4 * 2 + (core + number % 2) % 2 for number in range(1, 8)]


def send(src, dst, send_sem, recv_sem, scan, mode):
    return pltpu.make_async_remote_copy(
        src_ref=src,
        dst_ref=dst,
        send_sem=send_sem,
        recv_sem=recv_sem,
        device_id={"scan": scan, "mode": mode},
        device_id_type=pl.DeviceIdType.MESH,
    )


def meet(partners):
    barrier = pltpu.get_barrier_semaphore()
    for scan, mode in partners:
        pl.semaphore_signal(
            barrier, inc=1, device_id={"scan": scan, "mode": mode}, device_id_type=pl.DeviceIdType.MESH
        )
    pl.semaphore_wait(barrier, len(partners))


def home(owner):
    y, z, core = owner >> 4, (owner >> 1) & (RING - 1), owner & 1
    return (y * 2 + core) * RING + z


def column_scale(value):
    most = jnp.max(jnp.max(jnp.abs(value), axis=0), axis=0, keepdims=True)
    return jnp.maximum(most, 1e-30) * (1.0 / STEPS)


def encode(value, scale):
    return jnp.round(value * (1.0 / scale)).astype(jnp.int32).astype(jnp.int16)


def decode(code):
    return code.astype(jnp.int32).astype(jnp.float32)


def kernel_body(owner_ref, first_ref, pos_ref, owner_rows, obj_ref, probe_ref, counts_any, tab_any, out_ref, pg_ref, *scratch, scale=1.0):
    names = iter(scratch)

    def several(count):
        return [next(names) for _ in range(count)]

    chunk = [several(8) for _ in range(2)]
    win = several(2)
    ybuf, xbuf, x_ref, pall_ref, counts_ref, tab_ref, ebuf = several(7)
    eq_ref = several(2)
    pp_ref = next(names)
    a_hi, a_lo, b_hi, b_lo, c_hi, c_lo, planes_ref, xroll, wave_ref, sum_ref = several(10)
    left_sum, right_sum = several(2), several(2)
    rbuf = [several(8) for _ in range(2)]
    rscale = several(2)
    out_of = [[several(4) for _ in range(2)] for _ in range(2)]
    into = [[several(4) for _ in range(2)] for _ in range(2)]
    codes, cscale, sscale, zscale, given, pxb, pxs, pyb, pzs, pzb, table_ref, pick_ref = several(12)
    local_sem, zs, zr, ys, yr, xs, xr, ps, pr, es, er = several(11)
    ts, tr, tcs, tcr, us, ur, ucs, ucr, p0s, p0r, p1s, p1r, p2s, p2r, p3s, p3r = several(16)

    here, q = lax.axis_index("scan"), lax.axis_index("mode")
    y, z, core = spot(here)
    mine = y * 2 + core
    tile_dev, _, quarter, side = chunk[0][0].shape
    modes, npos = x_ref.shape[1:3]
    batch = modes * npos
    local = [
        pltpu.make_async_copy(
            obj_ref.at[:, l, :, pl.ds(q * quarter, quarter), :], chunk[l][0], local_sem.at[l]
        )
        for l in range(2)
    ]
    local.extend(
        [
            pltpu.make_async_copy(probe_ref.at[0], pall_ref.at[q], local_sem.at[2]),
            pltpu.make_async_copy(tab_any, tab_ref, local_sem.at[3]),
            pltpu.make_async_copy(counts_any.at[pl.ds(q * npos, npos)], counts_ref, local_sem.at[4]),
        ]
    )
    for copy in local:
        copy.start()
    right, left = at_spot(y, (z + 1) % RING, core), at_spot(y, (z + RING - 1) % RING, core)
    peers = plane_peers(y, z, core)
    sources = plane_sources(y, core)
    column = [at_spot(y, (z + k) % RING, core) for k in range(1, RING)]
    others = [(q + k) % modes for k in range(1, modes)]
    froms = [(q + modes - 1 - k) % modes for k in range(modes - 1)]
    meet([(scan, q) for scan in column] + [(scan, q) for _, scan, _ in peers] + [(here, m) for m in others])

    sends = []

    def go(copy):
        copy.start()
        sends.append(copy)
        return copy


    def pass_on(l, direction, step):
        if step == 3 and direction != l:
            return None
        rightward = chunk[l][0:4] + chunk[l][7:8]
        leftward = chunk[l][0:1] + chunk[l][4:8]
        lane = (rightward, leftward)[direction]
        scan = (right, left)[direction]
        return go(send(lane[step], lane[step + 1], zs.at[l, direction, step], zr.at[l, direction, step], scan, q))

    moving = {}

    def step_on(l, step):
        for direction in (0, 1):
            if step > 0:
                moving[l, direction].wait_recv()
            moving[l, direction] = pass_on(l, direction, step)

    for l in range(2):
        local[l].wait()
        step_on(l, 0)
    for k, m in enumerate(others):
        go(send(probe_ref.at[0], pall_ref.at[q], ps.at[k], pr.at[k], here, m))

    lanes = lax.broadcasted_iota(jnp.int32, (RING, side), 1)
    depth = lax.broadcasted_iota(jnp.int32, (RING, side), 0)
    zero = jnp.zeros((RING, side), jnp.int32)
    owners = [owner_rows[n : n + 1, :] for n in range(owner_rows.shape[0])]
    my_first = first_ref[here, 0]
    span = first_ref.shape[0] // 2
    ring = at_spot(y, depth, core)
    owned = [jnp.where(row == ring, 1, 0) for row in owners]
    picks = []
    slots = zero
    for d in range(8):
        first = first_ref[at_spot(d // 2, z, d % 2), 0]
        before, slot = zero, zero
        ring = at_spot(d // 2, depth, d % 2)
        for n, row in enumerate(owners):
            tile = lanes + n * side
            before = before + jnp.where(tile < first, owned[n], 0)
            inside = (tile >= my_first) & (tile < my_first + 2 * span) & (row == ring)
            slot = jnp.maximum(slot, jnp.where(inside, tile - my_first, 0))
        picks.append(jnp.sum(before, axis=1, keepdims=True))
        slots = jnp.where(lanes == d, jnp.max(slot, axis=1, keepdims=True), slots)
    chosen, order, ends = zero, zero, zero
    for d in range(8):
        ahead = jnp.zeros_like(picks[d])
        for e in range(8):
            if e != d:
                ahead = ahead + jnp.where(picks[e] <= picks[d] if e < d else picks[e] < picks[d], 1, 0)
        chosen = jnp.where(lanes == d, picks[d], chosen)
        order = order + jnp.where(lanes == ahead, d, 0)
        ends = ends + jnp.where(picks[d] <= lanes, 1, 0)
    places = [pos_ref[j, 1] >> 7 for j in range(batch)]
    ranks = [jnp.int32(0)] * batch
    for j in range(batch):
        for k in range(j):
            earlier = jnp.where(places[k] <= places[j], 1, 0)
            ranks[j] = ranks[j] + earlier
            ranks[k] = ranks[k] + (1 - earlier)
    queue, counted = zero, zero
    for j in range(batch):
        queue = queue + jnp.where(lanes == ranks[j], j, 0)
        counted = counted + jnp.where(places[j] < lanes - 1, 1, 0)
    for n, table in enumerate((chosen, order, ends, slots, jnp.where(depth == 0, queue, counted))):
        table_ref[n] = table
    pick_copy = pltpu.make_async_copy(table_ref, pick_ref, local_sem.at[5])
    pick_copy.start()
    pick_copy.wait()

    rounds = [0, -1, 1, -2, 2, -3, 3, 4]

    def offer(l, r):
        zi = (z + rounds[r] + RING) % RING
        buf = chunk[l][(0, 1, 4, 2, 5, 3, 6, 7)[r]]
        for n, scan, d in peers:
            ybuf[l, n, r] = buf[pick_ref[0, zi, d]]
            go(send(ybuf.at[l, n, r], win[l].at[mine * RING + zi], ys.at[l, n, r], yr.at[l, n, r], scan, q))
        win[l][mine * RING + zi] = buf[pick_ref[0, zi, mine]]

    def await_window(l):
        for r in range(RING):
            zi = (z + rounds[r] + RING) % RING
            for n, source in enumerate(sources):
                send(ybuf.at[l, n, r], win[l].at[source * RING + zi], ys.at[l, n, r], yr.at[l, n, r], here, q).wait_recv()

    shape = (2, quarter, side)
    rows = lax.broadcasted_iota(jnp.int32, shape, 1) + q * quarter
    cols = lax.broadcasted_iota(jnp.int32, shape, 2)

    def piece(l, j):
        row, col = pos_ref[j, 0], pos_ref[j, 1]
        near = my_first + (col >> 7)
        far = my_first + jnp.minimum((col >> 7) + 1, span - 1)
        tiles = [win[l][home(owner_ref[t])].astype(jnp.float32) for t in (near, far, near + span, far + span)]
        kept = cols >= (col & (side - 1))
        upper = jnp.where(kept, tiles[0], tiles[1])
        lower = jnp.where(kept, tiles[2], tiles[3])
        return jnp.where(rows >= row, upper, lower).astype(jnp.bfloat16)

    def x_copy(l, k, i, mode, target):
        return send(xbuf.at[l, k, i], x_ref.at[l, target, i], xs.at[l, k, i], xr.at[l, k, i], here, mode)

    def share(l):
        def pack(i, carry):
            for k in (1, 0, 2):
                xbuf[l, k, i] = piece(l, others[k] * npos + i)
                x_copy(l, k, i, others[k], q).start()
            x_ref[l, q, i] = piece(l, q * npos + i)
            return carry

        lax.fori_loop(0, npos, pack, 0)

    for l in range(2):
        offer(l, 0)
    for step in range(1, 4):
        for l in range(2):
            step_on(l, step)
            offer(l, 2 * step - 1)
            offer(l, 2 * step)
    for l in range(2):
        moving[l, l].wait_recv()
        offer(l, 7)
    for l in range(2):
        await_window(l)
        share(l)
    for copy in local[2:]:
        copy.wait()
    for k in range(modes - 1):
        send(probe_ref.at[0], pall_ref.at[froms[k]], ps.at[k], pr.at[k], here, q).wait_recv()


    def block(m):
        return slice(m * side, (m + 1) * side)

    def load(hi_ref, lo_ref, fields):
        for m, (re, im) in enumerate(fields):
            rh, rl = split_parts(re)
            ih, il = split_parts(im)
            hi_ref[block(m), 0:side] = rh
            hi_ref[block(m), side : 2 * side] = ih
            lo_ref[block(m), 0:side] = rl
            lo_ref[block(m), side : 2 * side] = il

    def two_sided(right_table, left_table, hi_ref, lo_ref):
        for m in range(modes):
            bh, bl = tab_ref[2 * right_table], tab_ref[2 * right_table + 1]
            whole = dot(hi_ref[block(m)], bh) + dot(lo_ref[block(m)], bh) + dot(hi_ref[block(m)], bl)
            hi, lo = split_parts(whole)
            c_hi[0:side, block(m)] = hi[:, 0:side]
            c_hi[side : 2 * side, block(m)] = hi[:, side : 2 * side]
            c_lo[0:side, block(m)] = lo[:, 0:side]
            c_lo[side : 2 * side, block(m)] = lo[:, side : 2 * side]
        lh, ll = tab_ref[2 * left_table], tab_ref[2 * left_table + 1]
        out = []
        for h in range(modes // 2):
            cut = slice(h * 2 * side, (h + 1) * 2 * side)
            whole = dot(lh, c_hi[:, cut]) + dot(lh, c_lo[:, cut]) + dot(ll, c_hi[:, cut])
            for k in range(2):
                out.append((whole[0:side, block(k)], whole[side : 2 * side, block(k)]))
        return out

    def patch(l, p):
        for k in range(modes - 1):
            x_copy(l, k, p, q, froms[k]).wait_recv()
        row, col = pos_ref[q * npos + p, 0], pos_ref[q * npos + p, 1]
        for part in range(2):
            whole = jnp.concatenate([x_ref[l, k, p, part].astype(jnp.float32) for k in range(modes)], axis=0)
            whole = pltpu.roll(whole, (side - row) & (side - 1), 0)
            planes_ref[part] = pltpu.roll(whole, (side - (col & (side - 1))) & (side - 1), 1)

    def times(wave, field):
        (wr, wi), (fr, fi) = wave, field
        return wr * fr - wi * fi, wr * fi + wi * fr

    def conj_times(wave, field):
        (wr, wi), (fr, fi) = wave, field
        return wr * fr + wi * fi, wr * fi - wi * fr

    def e_copy(l, k, p, mode, target):
        return send(ebuf.at[l, k, p], eq_ref[l].at[target, p], es.at[l, k, p], er.at[l, k, p], here, mode)

    def hand_out(l, p, total):
        row, col = pos_ref[q * npos + p, 0], pos_ref[q * npos + p, 1]
        for part in range(2):
            sum_ref[part] = pltpu.roll(pltpu.roll(total[part], row & (side - 1), 0), col & (side - 1), 1)
        for k in range(modes - 1):
            cut = pl.ds(pl.multiple_of(others[k] * quarter, quarter), quarter)
            for part in range(2):
                ebuf[l, k, p, part] = sum_ref[part, cut]
            e_copy(l, k, p, others[k], q).start()
        cut = pl.ds(pl.multiple_of(q * quarter, quarter), quarter)
        for part in range(2):
            eq_ref[l][q, p, part] = sum_ref[part, cut]

    def enter(p, carry):
        patch(0, p)
        for part in range(2):
            xroll[p, part] = planes_ref[part]
        load(a_hi, a_lo, [times((pall_ref[m, 0], pall_ref[m, 1]), (planes_ref[0], planes_ref[1])) for m in range(modes)])
        for m, (re, im) in enumerate(two_sided(2, 3, a_hi, a_lo)):
            wave_ref[p, m, 0] = re
            wave_ref[p, m, 1] = im
        return carry

    lax.fori_loop(0, npos, enter, 0)

    def detect(p, carry):
        patch(1, p)
        load(a_hi, a_lo, [times((wave_ref[p, m, 0], wave_ref[p, m, 1]), (planes_ref[0], planes_ref[1])) for m in range(modes)])
        far = two_sided(0, 1, a_hi, a_lo)
        intensity = background
        for re, im in far:
            intensity = intensity + (re * re + im * im)
        weight = 1.0 - counts_ref[p].astype(jnp.float32) / intensity
        load(a_hi, a_lo, [(weight * re, weight * im) for re, im in far])
        grads = two_sided(1, 0, a_hi, a_lo)
        load(b_hi.at[p], b_lo.at[p], [conj_times((planes_ref[0], planes_ref[1]), grad) for grad in grads])
        terms = [conj_times((wave_ref[p, m, 0], wave_ref[p, m, 1]), grad) for m, grad in enumerate(grads)]
        hand_out(1, p, [functools.reduce(jnp.add, part) for part in zip(*terms)])
        return carry

    lax.fori_loop(0, npos, detect, 0)
    pp_ref[...] = jnp.zeros_like(pp_ref)

    def leave(p, carry):
        grads = two_sided(3, 2, b_hi.at[p], b_lo.at[p])
        for m, grad in enumerate(grads):
            for part, term in enumerate(conj_times((xroll[p, 0], xroll[p, 1]), grad)):
                pp_ref[m, part * side : (part + 1) * side] += term
        terms = [conj_times((pall_ref[m, 0], pall_ref[m, 1]), grad) for m, grad in enumerate(grads)]
        hand_out(0, p, [functools.reduce(jnp.add, part) for part in zip(*terms)])
        return carry

    lax.fori_loop(0, npos, leave, 0)


    def gather_e(l):
        def take(p, carry):
            for k in range(modes - 1):
                e_copy(l, k, p, q, froms[k]).wait_recv()
            return carry

        lax.fori_loop(0, npos, take, 0)

    def lay(l):
        blank = jnp.zeros(shape, jnp.float32)
        for u in range(2):
            left_sum[l][u, 0] = blank
            right_sum[l][u, 0] = blank

        def add(n, carry):
            j = pick_ref[4, 0, n]
            kept = cols >= (pos_ref[j, 1] & (side - 1))
            upper = rows >= pos_ref[j, 0]
            term = eq_ref[l][j // npos, j % npos]
            lefts, rights = jnp.where(kept, term, 0.0), jnp.where(kept, 0.0, term)
            for sums, part in ((left_sum[l], lefts), (right_sum[l], rights)):
                sums[0, n + 1] = sums[0, n] + jnp.where(upper, part, 0.0)
                sums[1, n + 1] = sums[1, n] + jnp.where(upper, 0.0, part)
            return carry

        lax.fori_loop(0, batch, add, 0)

    back = [4, 3, -3, 2, -2, 1, -1, 0]

    def zi(r):
        return (z + back[r] + RING) % RING

    def code(l):
        def one(place, carry):
            for d in range(8):
                slot = pick_ref[3, place, d]
                u, w = slot >> 5, slot & (span - 1)
                low, middle, high = pick_ref[4, 1, w], pick_ref[4, 1, w + 1], pick_ref[4, 1, w + 2]
                value = (left_sum[l][u, high] - left_sum[l][u, middle]) + (right_sum[l][u, middle] - right_sum[l][u, low])
                step = column_scale(value)
                cscale[l, d, pl.ds(place, 1)] = step
                codes[l, d, place] = encode(value, step)
            return carry

        lax.fori_loop(0, RING, one, 0)
        for n, scan, d in peers:
            go(send(cscale.at[l, d], rscale[l].at[mine], tcs.at[l, n], tcr.at[l, n], scan, q))
        rscale[l][mine] = cscale[l, mine]

    def yield_up(l, r):
        for n, scan, d in peers:
            go(send(codes.at[l, d, zi(r)], rbuf[l][r].at[mine], ts.at[l, n, r], tr.at[l, n, r], scan, q))
        rbuf[l][r][mine] = codes[l, mine, zi(r)]

    def await_up(l, r):
        for n, source in enumerate(sources):
            send(codes.at[l, source, zi(r)], rbuf[l][r].at[source], ts.at[l, n, r], tr.at[l, n, r], here, q).wait_recv()

    def await_scales(l):
        for n, source in enumerate(sources):
            send(cscale.at[l, source], rscale[l].at[source], tcs.at[l, n], tcr.at[l, n], here, q).wait_recv()

    given[0] = jnp.zeros(shape, jnp.float32)

    def combine(l, r, received, use):
        place = zi(r)
        total = jnp.zeros(shape, jnp.float32)
        for n in range(8):
            giver = pick_ref[1, place, n]
            total = total + decode(rbuf[l][r][giver]) * rscale[l][giver, pl.ds(place, 1)]
            given[n + 1] = total
        start = 0
        for k in range(tile_dev):
            end = pick_ref[2, place, k]
            value = given[end] - given[start]
            for ref, ref_scale in received:
                value = value + decode(ref[k]) * ref_scale[k : k + 1]
            use(k, value)
            start = end

    def ship(l, direction, step, r, received):
        at = (l, direction, step)
        buf, to = out_of[l][direction][step], into[l][direction][step]

        def pack(k, value):
            step_size = column_scale(value)
            sscale[l, direction, step, k : k + 1] = step_size
            buf[k] = encode(value, step_size)

        combine(l, r, received, pack)
        scan = (right, left)[direction]
        return (
            go(send(sscale.at[at], zscale.at[at], ucs.at[at], ucr.at[at], scan, q)),
            go(send(buf, to, us.at[at], ur.at[at], scan, q)),
        )

    flying = {}

    def arrived(l, direction, step):
        if (l, direction) not in flying:
            return []
        for copy in flying[l, direction]:
            copy.wait_recv()
        return [(into[l][direction][step - 1], zscale.at[l, direction, step - 1])]

    def turn(l, step):
        if step == 0:
            await_scales(l)
            await_up(l, 0)
            flying[l, l] = ship(l, l, 0, 0, [])
            return
        for direction in (l, 1 - l):
            r = 2 * step - 1 + direction
            await_up(l, r)
            flying[l, direction] = ship(l, direction, step, r, arrived(l, direction, step))

    gather_e(1)
    lay(1)
    code(1)
    for r in range(3):
        yield_up(1, r)
    for k, m in enumerate(others):
        go(send(pp_ref.at[m], pxb.at[k], p0s.at[k], p0r.at[k], here, m))
    gather_e(0)
    lay(0)
    code(0)
    for r in range(3):
        yield_up(0, r)
    turn(1, 0)
    yield_up(1, 3)
    yield_up(1, 4)
    turn(0, 0)
    yield_up(0, 3)
    yield_up(0, 4)
    turn(1, 1)
    yield_up(1, 5)
    yield_up(1, 6)
    turn(0, 1)
    yield_up(0, 5)
    yield_up(0, 6)
    total = pp_ref[q]
    for k in range(modes - 1):
        send(pp_ref.at[q], pxb.at[k], p0s.at[k], p0r.at[k], here, q).wait_recv()
        total = total + pxb[k]
    pxs[...] = total.reshape(pxs.shape)
    for n, scan, d in peers:
        go(send(pxs.at[d], pyb.at[n], p1s.at[n], p1r.at[n], scan, q))
    turn(1, 2)
    yield_up(1, 7)
    turn(0, 2)
    yield_up(0, 7)
    total = pxs[mine]
    for n, source in enumerate(sources):
        send(pxs.at[source], pyb.at[n], p1s.at[n], p1r.at[n], here, q).wait_recv()
        total = total + pyb[n]
    pzs[...] = total
    for k, scan in enumerate(column):
        go(send(pzs, pzb.at[k], p2s.at[k], p2r.at[k], scan, q))
    turn(1, 3)
    turn(0, 3)
    for k, scan in enumerate(column):
        send(pzs, pzb.at[k], p2s.at[k], p2r.at[k], here, q).wait_recv()
        total = total + pzb[k]
    pg_ref[mine] = total * scale
    for n, scan, d in peers:
        go(send(pg_ref.at[mine], pg_ref.at[mine], p3s.at[n], p3r.at[n], scan, q))
    for l in (1, 0):
        await_up(l, 7)

        def keep(k, value, l=l):
            out_ref[k, l] = value

        combine(l, 7, arrived(l, 0, 4) + arrived(l, 1, 4), keep)
    for n, source in enumerate(sources):
        send(pg_ref.at[source], pg_ref.at[source], p3s.at[n], p3r.at[n], here, q).wait_recv()

    def finish(p, carry):
        for l in (1, 0):
            for k in range(modes - 1):
                e_copy(l, k, p, others[k], q).wait_send()
                x_copy(l, k, p, others[k], q).wait_send()
        return carry

    lax.fori_loop(0, npos, finish, 0)
    for copy in sends:
        copy.wait_send()


def gradients(tile_owner, block_tiles, positions, tiles, probe, counts, tables, modes, scale):
    tile_dev, slices, parts, side, _ = tiles.shape
    quarter = side // modes
    batch = positions.shape[0]
    npos = batch // modes
    dma = pltpu.SemaphoreType.DMA
    smem, anywhere, vmem = (pl.BlockSpec(memory_space=space) for space in (pltpu.SMEM, pl.ANY, pltpu.VMEM))
    tile = (parts, quarter, side)

    def wide(*dims):
        return pltpu.VMEM(dims, jnp.float32)

    def half(*dims):
        return pltpu.VMEM(dims, jnp.bfloat16)

    def short(*dims):
        return pltpu.VMEM(dims, jnp.int16)

    piece = (parts * side // 8, side)
    scratch = [half(tile_dev, *tile)] * 16 + [half(8 * RING, *tile)] * 2
    scratch += [
        half(slices, 7, RING, *tile),
        half(slices, modes - 1, npos, *tile),
        half(slices, modes, npos, *tile),
        wide(modes, parts, side, side),
        pltpu.VMEM((npos, side, side), counts.dtype),
        half(*tables.shape),
        wide(slices, modes - 1, npos, *tile),
        wide(modes, npos, *tile),
        wide(modes, npos, *tile),
        wide(modes, parts * side, side),
        half(modes * side, 2 * side),
        half(modes * side, 2 * side),
        half(npos, modes * side, 2 * side),
        half(npos, modes * side, 2 * side),
        half(2 * side, modes * side),
        half(2 * side, modes * side),
        wide(parts, side, side),
        wide(npos, parts, side, side),
        wide(npos, modes, parts, side, side),
        wide(parts, side, side),
    ]
    scratch += [wide(2, batch + 1, *tile)] * 4
    scratch += [short(8, *tile)] * 16 + [wide(8, RING, side)] * 2
    scratch += [short(tile_dev, *tile)] * 32
    scratch += [
        short(slices, 8, RING, *tile),
        wide(slices, 8, RING, side),
        wide(slices, 2, 4, tile_dev, side),
        wide(slices, 2, 4, tile_dev, side),
        wide(9, *tile),
        wide(modes - 1, parts * side, side),
        wide(8, *piece),
        wide(7, *piece),
        wide(*piece),
        wide(RING - 1, *piece),
        pltpu.VMEM((5, RING, side), jnp.int32),
        pltpu.SMEM((5, RING, side), jnp.int32),
    ]
    sizes = [(6,)] + [(slices, 2, 4)] * 2 + [(slices, 7, RING)] * 2 + [(slices, modes - 1, npos)] * 2
    sizes += [(modes - 1,)] * 2 + [(slices, modes - 1, npos)] * 2
    sizes += [(slices, 7, RING)] * 2 + [(slices, 7)] * 2 + [(slices, 2, 4)] * 4
    sizes += [(modes - 1,)] * 2 + [(7,)] * 2 + [(RING - 1,)] * 2 + [(7,)] * 2
    scratch += [dma(size) for size in sizes]
    return pl.pallas_call(
        functools.partial(kernel_body, scale=scale),
        in_specs=[smem, smem, smem, vmem, anywhere, anywhere, anywhere, anywhere],
        out_specs=[vmem, vmem],
        out_shape=[
            jax.ShapeDtypeStruct((tile_dev, slices) + tile, jnp.float32),
            jax.ShapeDtypeStruct((8,) + piece, jnp.float32),
        ],
        scratch_shapes=scratch,
        compiler_params=pltpu.CompilerParams(
            collective_id=0, has_side_effects=True, vmem_limit_bytes=60 * MIB
        ),
        name="gradients",
    )(tile_owner, block_tiles, positions, tile_owner.reshape(-1, side), tiles, probe, counts, tables)


def shards(object_tiles, tile_owner, block_tiles, positions, counts, probe):
    scan_count = lax.axis_size("scan")
    mode_count = lax.axis_size("mode")
    batch = positions.shape[0]
    tables = jnp.asarray(transform_tables(object_tiles.shape[3]))
    object_grad, probe_grad = gradients(
        tile_owner, block_tiles, positions, object_tiles, probe, counts, tables, mode_count, 1.0 / (batch * scan_count)
    )
    return (object_grad, probe_grad.reshape(probe.shape))


def solution(mesh):
    placed = (
        P("scan", None, None, None, None),
        P(),
        P(),
        P("scan", None),
        P("scan", None, None),
        P("mode", None, None, None),
    )
    return jax.shard_map(
        shards,
        mesh=mesh,
        in_specs=placed,
        out_specs=(P("scan", None, None, "mode", None), P("mode", None, None, None)),
        check_vma=False,
    )
```

time: 130 us -> 108 us (0.83)
  Pallas kernels: 121 us -> 103 us
  local copies, waits for them, and re-layouts: 8 us -> 3.93 us
    pallas_call x3 -> x1, Pallas kernels: 121 us -> 103 us  [gradients(): pl.pallas_call(functools.partial(kernel_body, scale=scale), in_specs=[sme...]
    unnamed x15 -> x7, local copies, waits for them, and re-layouts: 8 us -> 3.93 us
where the time goes in v5:
time: 108 us
  Pallas kernels  103 us (95%)
  local copies, waits for them, and re-layouts  3.93 us (4%)
    pallas_call x1, Pallas kernels, gradients(): pl.pallas_call(functools.partial(kernel_body, scale=scale), in_specs=[sme...  103 us
    unnamed x7, local copies, waits for them, and re-layouts  3.93 us

profile of v5, /device:TPU:1, one launch (start us, length us, event | category | flops | bytes accessed | tf_op | source)
XLA Modules:
  0.0 107.7 jit_solution(17113151150705362806)
XLA Ops:
  0.6 0.0 copy-start.1
  0.6 0.7 copy-done.1
  1.3 0.7 copy.9.pos_ref
  2.0 103.1 %gradients.1 = (f32[8,2,2,32,128]{4,3,2,1,0:T(8,128)}, f32[8,32,128]{2,1,0:T(8,128)}) custom-call(s32[512]{0:T(512)} %owner_ref.1, s32[64,64]{1,0:T(8,128)} %first_ref.1, s32[16,2]{1,0:T(8,128)} %copy.9.pos_ref, s32[4,128]{1,0:T(4,128)} %bitcast.3, bf16[8,2,2,128,128]{4,3,2,1,0:T(8,128)(2,1)} %obj_ref.1, f32[1,2,128,128]{3,2,1,0:T(8,128)} %probe_ref.1, ...), custom_call_target="tpu_custom_call" | custom-call | tf_op jit(solution)/shard_map/gradients/pallas_call | solution.py:657
  105.1 0.0 copy-start
  105.1 1.9 %copy.12 = f32[8,2,2,32,128]{4,3,2,1,0:T(8,128)} copy(f32[8,2,2,32,128]{4,3,2,1,0:T(8,128)} %get-tuple-element.8) | data formatting | bytes 1048576
  107.1 0.0 copy-done
  107.1 0.7 copy.13
Async XLA Ops:
  0.6 0.7 copy-start.1
  105.1 1.9 %copy-start = (f32[8,32,128]{2,1,0:T(8,128)S(1)}, f32[8,32,128]{2,1,0:T(8,128)}, u32[]{:S(2)}) copy-start(f32[8,32,128]{2,1,0:T(8,128)} %get-tuple-element.5) | copy-start | bytes 393220

commit v6 on v5

--- a/solution.py
+++ b/solution.py
@@ -65,10 +65,6 @@
     return peers
 
 
-def plane_sources(y, core):
-    return [(y - number // 2 + 4) % 4 * 2 + (core + number % 2) % 2 for number in range(1, 8)]
-
-
 def send(src, dst, send_sem, recv_sem, scan, mode):
     return pltpu.make_async_remote_copy(
         src_ref=src,
@@ -78,6 +74,10 @@
         device_id={"scan": scan, "mode": mode},
         device_id_type=pl.DeviceIdType.MESH,
     )
+
+
+def received(ref, sem, scan, mode):
+    send(ref, ref, sem, sem, scan, mode).wait_recv()
 
 
 def meet(partners):
@@ -151,28 +151,28 @@
         copy.start()
     right, left = at_spot(y, (z + 1) % RING, core), at_spot(y, (z + RING - 1) % RING, core)
     peers = plane_peers(y, z, core)
-    sources = plane_sources(y, core)
     column = [at_spot(y, (z + k) % RING, core) for k in range(1, RING)]
     others = [(q + k) % modes for k in range(1, modes)]
-    froms = [(q + modes - 1 - k) % modes for k in range(modes - 1)]
     meet([(scan, q) for scan in column] + [(scan, q) for _, scan, _ in peers] + [(here, m) for m in others])
-
-    sends = []
 
     def go(copy):
         copy.start()
-        sends.append(copy)
         return copy
 
+    def arrive(ref, sem):
+        received(ref, sem, here, q)
+
 
     def pass_on(l, direction, step):
-        if step == 3 and direction != l:
-            return None
         rightward = chunk[l][0:4] + chunk[l][7:8]
         leftward = chunk[l][0:1] + chunk[l][4:8]
         lane = (rightward, leftward)[direction]
         scan = (right, left)[direction]
-        return go(send(lane[step], lane[step + 1], zs.at[l, direction, step], zr.at[l, direction, step], scan, q))
+        src, dst = lane[step], lane[step + 1]
+        if step == 3:
+            part = pl.ds(direction * (tile_dev // 2), tile_dev // 2)
+            src, dst = src.at[part], dst.at[part]
+        return go(send(src, dst, zs.at[l], zr.at[l, direction, step], scan, q))
 
     moving = {}
 
@@ -186,7 +186,7 @@
         local[l].wait()
         step_on(l, 0)
     for k, m in enumerate(others):
-        go(send(probe_ref.at[0], pall_ref.at[q], ps.at[k], pr.at[k], here, m))
+        go(send(probe_ref.at[0], pall_ref.at[q], ps.at[0], pr.at[0], here, m))
 
     lanes = lax.broadcasted_iota(jnp.int32, (RING, side), 1)
     depth = lax.broadcasted_iota(jnp.int32, (RING, side), 0)
@@ -218,7 +218,7 @@
         chosen = jnp.where(lanes == d, picks[d], chosen)
         order = order + jnp.where(lanes == ahead, d, 0)
         ends = ends + jnp.where(picks[d] <= lanes, 1, 0)
-    places = [pos_ref[j, 1] >> 7 for j in range(batch)]
+    places = [pos_ref[1, j] >> 7 for j in range(batch)]
     ranks = [jnp.int32(0)] * batch
     for j in range(batch):
         for k in range(j):
@@ -242,21 +242,15 @@
         buf = chunk[l][(0, 1, 4, 2, 5, 3, 6, 7)[r]]
         for n, scan, d in peers:
             ybuf[l, n, r] = buf[pick_ref[0, zi, d]]
-            go(send(ybuf.at[l, n, r], win[l].at[mine * RING + zi], ys.at[l, n, r], yr.at[l, n, r], scan, q))
+            go(send(ybuf.at[l, n, r], win[l].at[mine * RING + zi], ys.at[l], yr.at[l], scan, q))
         win[l][mine * RING + zi] = buf[pick_ref[0, zi, mine]]
-
-    def await_window(l):
-        for r in range(RING):
-            zi = (z + rounds[r] + RING) % RING
-            for n, source in enumerate(sources):
-                send(ybuf.at[l, n, r], win[l].at[source * RING + zi], ys.at[l, n, r], yr.at[l, n, r], here, q).wait_recv()
 
     shape = (2, quarter, side)
     rows = lax.broadcasted_iota(jnp.int32, shape, 1) + q * quarter
     cols = lax.broadcasted_iota(jnp.int32, shape, 2)
 
     def piece(l, j):
-        row, col = pos_ref[j, 0], pos_ref[j, 1]
+        row, col = pos_ref[0, j], pos_ref[1, j]
         near = my_first + (col >> 7)
         far = my_first + jnp.minimum((col >> 7) + 1, span - 1)
         tiles = [win[l][home(owner_ref[t])].astype(jnp.float32) for t in (near, far, near + span, far + span)]
@@ -266,7 +260,7 @@
         return jnp.where(rows >= row, upper, lower).astype(jnp.bfloat16)
 
     def x_copy(l, k, i, mode, target):
-        return send(xbuf.at[l, k, i], x_ref.at[l, target, i], xs.at[l, k, i], xr.at[l, k, i], here, mode)
+        return send(xbuf.at[l, k, i], x_ref.at[l, target, i], xs.at[l], xr.at[l, i], here, mode)
 
     def share(l):
         def pack(i, carry):
@@ -286,15 +280,15 @@
             offer(l, 2 * step - 1)
             offer(l, 2 * step)
     for l in range(2):
-        moving[l, l].wait_recv()
+        for direction in (0, 1):
+            moving[l, direction].wait_recv()
         offer(l, 7)
     for l in range(2):
-        await_window(l)
+        arrive(ybuf.at[l], yr.at[l])
         share(l)
     for copy in local[2:]:
         copy.wait()
-    for k in range(modes - 1):
-        send(probe_ref.at[0], pall_ref.at[froms[k]], ps.at[k], pr.at[k], here, q).wait_recv()
+    arrive(pall_ref.at[pl.ds(0, modes - 1)], pr.at[0])
 
 
     def block(m):
@@ -328,9 +322,8 @@
         return out
 
     def patch(l, p):
-        for k in range(modes - 1):
-            x_copy(l, k, p, q, froms[k]).wait_recv()
-        row, col = pos_ref[q * npos + p, 0], pos_ref[q * npos + p, 1]
+        arrive(x_ref.at[l, pl.ds(0, modes - 1), p], xr.at[l, p])
+        row, col = pos_ref[0, q * npos + p], pos_ref[1, q * npos + p]
         for part in range(2):
             whole = jnp.concatenate([x_ref[l, k, p, part].astype(jnp.float32) for k in range(modes)], axis=0)
             whole = pltpu.roll(whole, (side - row) & (side - 1), 0)
@@ -345,10 +338,10 @@
         return wr * fr + wi * fi, wr * fi - wi * fr
 
     def e_copy(l, k, p, mode, target):
-        return send(ebuf.at[l, k, p], eq_ref[l].at[target, p], es.at[l, k, p], er.at[l, k, p], here, mode)
+        return send(ebuf.at[l, k, p], eq_ref[l].at[target, p], es.at[l], er.at[l], here, mode)
 
     def hand_out(l, p, total):
-        row, col = pos_ref[q * npos + p, 0], pos_ref[q * npos + p, 1]
+        row, col = pos_ref[0, q * npos + p], pos_ref[1, q * npos + p]
         for part in range(2):
             sum_ref[part] = pltpu.roll(pltpu.roll(total[part], row & (side - 1), 0), col & (side - 1), 1)
         for k in range(modes - 1):
@@ -403,12 +396,7 @@
 
 
     def gather_e(l):
-        def take(p, carry):
-            for k in range(modes - 1):
-                e_copy(l, k, p, q, froms[k]).wait_recv()
-            return carry
-
-        lax.fori_loop(0, npos, take, 0)
+        arrive(eq_ref[l].at[pl.ds(0, modes - 1)], er.at[l])
 
     def lay(l):
         blank = jnp.zeros(shape, jnp.float32)
@@ -418,8 +406,8 @@
 
         def add(n, carry):
             j = pick_ref[4, 0, n]
-            kept = cols >= (pos_ref[j, 1] & (side - 1))
-            upper = rows >= pos_ref[j, 0]
+            kept = cols >= (pos_ref[1, j] & (side - 1))
+            upper = rows >= pos_ref[0, j]
             term = eq_ref[l][j // npos, j % npos]
             lefts, rights = jnp.where(kept, term, 0.0), jnp.where(kept, 0.0, term)
             for sums, part in ((left_sum[l], lefts), (right_sum[l], rights)):
@@ -448,21 +436,19 @@
 
         lax.fori_loop(0, RING, one, 0)
         for n, scan, d in peers:
-            go(send(cscale.at[l, d], rscale[l].at[mine], tcs.at[l, n], tcr.at[l, n], scan, q))
+            go(send(cscale.at[l, d], rscale[l].at[mine], tcs.at[l], tcr.at[l], scan, q))
         rscale[l][mine] = cscale[l, mine]
 
     def yield_up(l, r):
         for n, scan, d in peers:
-            go(send(codes.at[l, d, zi(r)], rbuf[l][r].at[mine], ts.at[l, n, r], tr.at[l, n, r], scan, q))
+            go(send(codes.at[l, d, zi(r)], rbuf[l][r].at[mine], ts.at[l], tr.at[l, r], scan, q))
         rbuf[l][r][mine] = codes[l, mine, zi(r)]
 
     def await_up(l, r):
-        for n, source in enumerate(sources):
-            send(codes.at[l, source, zi(r)], rbuf[l][r].at[source], ts.at[l, n, r], tr.at[l, n, r], here, q).wait_recv()
+        arrive(rbuf[l][r].at[pl.ds(0, 7)], tr.at[l, r])
 
     def await_scales(l):
-        for n, source in enumerate(sources):
-            send(cscale.at[l, source], rscale[l].at[source], tcs.at[l, n], tcr.at[l, n], here, q).wait_recv()
+        arrive(rscale[l].at[pl.ds(0, 7)], tcr.at[l])
 
     given[0] = jnp.zeros(shape, jnp.float32)
 
@@ -494,8 +480,8 @@
         combine(l, r, received, pack)
         scan = (right, left)[direction]
         return (
-            go(send(sscale.at[at], zscale.at[at], ucs.at[at], ucr.at[at], scan, q)),
-            go(send(buf, to, us.at[at], ur.at[at], scan, q)),
+            go(send(sscale.at[at], zscale.at[at], ucs.at[l], ucr.at[at], scan, q)),
+            go(send(buf, to, us.at[l], ur.at[at], scan, q)),
         )
 
     flying = {}
@@ -524,7 +510,7 @@
     for r in range(3):
         yield_up(1, r)
     for k, m in enumerate(others):
-        go(send(pp_ref.at[m], pxb.at[k], p0s.at[k], p0r.at[k], here, m))
+        go(send(pp_ref.at[m], pxb.at[k], p0s.at[0], p0r.at[0], here, m))
     gather_e(0)
     lay(0)
     code(0)
@@ -543,31 +529,31 @@
     yield_up(0, 5)
     yield_up(0, 6)
     total = pp_ref[q]
+    arrive(pxb, p0r.at[0])
     for k in range(modes - 1):
-        send(pp_ref.at[q], pxb.at[k], p0s.at[k], p0r.at[k], here, q).wait_recv()
         total = total + pxb[k]
     pxs[...] = total.reshape(pxs.shape)
     for n, scan, d in peers:
-        go(send(pxs.at[d], pyb.at[n], p1s.at[n], p1r.at[n], scan, q))
+        go(send(pxs.at[d], pyb.at[n], p1s.at[0], p1r.at[0], scan, q))
     turn(1, 2)
     yield_up(1, 7)
     turn(0, 2)
     yield_up(0, 7)
     total = pxs[mine]
-    for n, source in enumerate(sources):
-        send(pxs.at[source], pyb.at[n], p1s.at[n], p1r.at[n], here, q).wait_recv()
+    arrive(pyb, p1r.at[0])
+    for n in range(7):
         total = total + pyb[n]
     pzs[...] = total
     for k, scan in enumerate(column):
-        go(send(pzs, pzb.at[k], p2s.at[k], p2r.at[k], scan, q))
+        go(send(pzs, pzb.at[k], p2s.at[0], p2r.at[0], scan, q))
     turn(1, 3)
     turn(0, 3)
-    for k, scan in enumerate(column):
-        send(pzs, pzb.at[k], p2s.at[k], p2r.at[k], here, q).wait_recv()
+    arrive(pzb, p2r.at[0])
+    for k in range(RING - 1):
         total = total + pzb[k]
     pg_ref[mine] = total * scale
     for n, scan, d in peers:
-        go(send(pg_ref.at[mine], pg_ref.at[mine], p3s.at[n], p3r.at[n], scan, q))
+        go(send(pg_ref.at[mine], pg_ref.at[mine], p3s.at[0], p3r.at[0], scan, q))
     for l in (1, 0):
         await_up(l, 7)
 
@@ -575,19 +561,25 @@
             out_ref[k, l] = value
 
         combine(l, 7, arrived(l, 0, 4) + arrived(l, 1, 4), keep)
-    for n, source in enumerate(sources):
-        send(pg_ref.at[source], pg_ref.at[source], p3s.at[n], p3r.at[n], here, q).wait_recv()
-
-    def finish(p, carry):
-        for l in (1, 0):
-            for k in range(modes - 1):
-                e_copy(l, k, p, others[k], q).wait_send()
-                x_copy(l, k, p, others[k], q).wait_send()
-        return carry
-
-    lax.fori_loop(0, npos, finish, 0)
-    for copy in sends:
-        copy.wait_send()
+    arrive(pg_ref.at[pl.ds(0, 7)], p3r.at[0])
+
+    def departed(ref, sem):
+        send(ref, ref, sem, sem, here, q).wait_send()
+
+    for l in range(2):
+        departed(ybuf.at[l], zs.at[l])
+        departed(ybuf.at[l], ys.at[l])
+        departed(xbuf.at[l], xs.at[l])
+        departed(ebuf.at[l], es.at[l])
+        departed(codes.at[l, pl.ds(0, 7)], ts.at[l])
+        departed(cscale.at[l, pl.ds(0, 7)], tcs.at[l])
+        departed(codes.at[l, pl.ds(0, 7)], us.at[l])
+        departed(cscale.at[l, pl.ds(0, 7)], ucs.at[l])
+    departed(pall_ref.at[pl.ds(0, modes - 1)], ps.at[0])
+    departed(pxb, p0s.at[0])
+    departed(pyb, p1s.at[0])
+    departed(pzb, p2s.at[0])
+    departed(pg_ref.at[pl.ds(0, 7)], p3s.at[0])
 
 
 def gradients(tile_owner, block_tiles, positions, tiles, probe, counts, tables, modes, scale):
@@ -649,10 +641,10 @@
         pltpu.VMEM((5, RING, side), jnp.int32),
         pltpu.SMEM((5, RING, side), jnp.int32),
     ]
-    sizes = [(6,)] + [(slices, 2, 4)] * 2 + [(slices, 7, RING)] * 2 + [(slices, modes - 1, npos)] * 2
-    sizes += [(modes - 1,)] * 2 + [(slices, modes - 1, npos)] * 2
-    sizes += [(slices, 7, RING)] * 2 + [(slices, 7)] * 2 + [(slices, 2, 4)] * 4
-    sizes += [(modes - 1,)] * 2 + [(7,)] * 2 + [(RING - 1,)] * 2 + [(7,)] * 2
+    sizes = [(6,), (slices,), (slices, 2, 4), (slices,), (slices,), (slices,), (slices, npos)]
+    sizes += [(1,), (1,), (slices,), (slices,)]
+    sizes += [(slices,), (slices, RING), (slices,), (slices,), (slices,), (slices, 2, 4), (slices,), (slices, 2, 4)]
+    sizes += [(1,)] * 8
     scratch += [dma(size) for size in sizes]
     return pl.pallas_call(
         functools.partial(kernel_body, scale=scale),
@@ -667,7 +659,7 @@
             collective_id=0, has_side_effects=True, vmem_limit_bytes=60 * MIB
         ),
         name="gradients",
-    )(tile_owner, block_tiles, positions, tile_owner.reshape(-1, side), tiles, probe, counts, tables)
+    )(tile_owner, block_tiles, positions.T, tile_owner.reshape(-1, side), tiles, probe, counts, tables)
 
 
 def shards(object_tiles, tile_owner, block_tiles, positions, counts, probe):

time: 108 us -> 100 us (0.926)
  Pallas kernels: 103 us -> 96.9 us
  local copies, waits for them, and re-layouts: 3.93 us -> 2.58 us
    pallas_call x1, Pallas kernels: 103 us -> 96.9 us  [gradients(): pl.pallas_call(functools.partial(kernel_body, scale=scale), in_specs=[sme...]
    unnamed x7 -> x4, local copies, waits for them, and re-layouts: 3.93 us -> 2.58 us
where the time goes in v6:
time: 100 us
  Pallas kernels  96.9 us (97%)
  local copies, waits for them, and re-layouts  2.58 us (3%)
    pallas_call x1, Pallas kernels, gradients(): pl.pallas_call(functools.partial(kernel_body, scale=scale), in_specs=[sme...  96.9 us
    unnamed x4, local copies, waits for them, and re-layouts  2.58 us

profile of v6, /device:TPU:1, one launch (start us, length us, event | category | flops | bytes accessed | tf_op | source)
XLA Modules:
  0.0 100.1 jit_solution(15018609874965948178)
XLA Ops:
  0.6 96.9 %gradients.1 = (f32[8,2,2,32,128]{4,3,2,1,0:T(8,128)}, f32[8,32,128]{2,1,0:T(8,128)}) custom-call(s32[512]{0:T(512)} %owner_ref.1, s32[64,64]{1,0:T(8,128)} %first_ref.1, s32[2,16]{1,0:T(2,128)} %bitcast.5, s32[4,128]{1,0:T(4,128)} %bitcast.4, bf16[8,2,2,128,128]{4,3,2,1,0:T(8,128)(2,1)} %obj_ref.1, f32[1,2,128,128]{3,2,1,0:T(8,128)} %probe_ref.1, ...), custom_call_target="tpu_custom_call" | custom-call | tf_op jit(solution)/shard_map/gradients/pallas_call | solution.py:649
  97.5 0.0 copy-start
  97.5 1.9 %copy.11 = f32[8,2,2,32,128]{4,3,2,1,0:T(8,128)} copy(f32[8,2,2,32,128]{4,3,2,1,0:T(8,128)} %get-tuple-element.8) | data formatting | bytes 1048576
  99.4 0.0 copy-done
  99.4 0.7 copy.12
Async XLA Ops:
  97.5 1.9 %copy-start = (f32[8,32,128]{2,1,0:T(8,128)S(1)}, f32[8,32,128]{2,1,0:T(8,128)}, u32[]{:S(2)}) copy-start(f32[8,32,128]{2,1,0:T(8,128)} %get-tuple-element.5) | copy-start | bytes 393220

commit v7 on v6

--- a/solution.py
+++ b/solution.py
@@ -116,8 +116,8 @@
     chunk = [several(8) for _ in range(2)]
     win = several(2)
     ybuf, xbuf, x_ref, pall_ref, counts_ref, tab_ref, ebuf = several(7)
-    eq_ref = several(2)
-    pp_ref = next(names)
+    eq_ref, e_steps = several(2), several(2)
+    e_out, pp_ref = several(2)
     a_hi, a_lo, b_hi, b_lo, c_hi, c_lo, planes_ref, xroll, wave_ref, sum_ref = several(10)
     left_sum, right_sum = several(2), several(2)
     rbuf = [several(8) for _ in range(2)]
@@ -125,7 +125,7 @@
     out_of = [[several(4) for _ in range(2)] for _ in range(2)]
     into = [[several(4) for _ in range(2)] for _ in range(2)]
     codes, cscale, sscale, zscale, given, pxb, pxs, pyb, pzs, pzb, table_ref, pick_ref = several(12)
-    local_sem, zs, zr, ys, yr, xs, xr, ps, pr, es, er = several(11)
+    local_sem, zs, zr, ys, yr, xs, xr, ps, pr, es, er, ess, esr = several(13)
     ts, tr, tcs, tcr, us, ur, ucs, ucr, p0s, p0r, p1s, p1r, p2s, p2r, p3s, p3r = several(16)
 
     here, q = lax.axis_index("scan"), lax.axis_index("mode")
@@ -274,15 +274,30 @@
 
     for l in range(2):
         offer(l, 0)
-    for step in range(1, 4):
-        for l in range(2):
-            step_on(l, step)
-            offer(l, 2 * step - 1)
-            offer(l, 2 * step)
-    for l in range(2):
-        for direction in (0, 1):
-            moving[l, direction].wait_recv()
-        offer(l, 7)
+    step_on(0, 1)
+    offer(0, 1)
+    offer(0, 2)
+    step_on(1, 1)
+    offer(1, 1)
+    offer(1, 2)
+    step_on(0, 2)
+    offer(0, 3)
+    offer(0, 4)
+    step_on(1, 2)
+    offer(1, 3)
+    step_on(0, 3)
+    offer(0, 5)
+    offer(0, 6)
+    step_on(1, 3)
+    offer(1, 4)
+    for direction in (0, 1):
+        moving[0, direction].wait_recv()
+    offer(0, 7)
+    offer(1, 5)
+    for direction in (0, 1):
+        moving[1, direction].wait_recv()
+    offer(1, 6)
+    offer(1, 7)
     for l in range(2):
         arrive(ybuf.at[l], yr.at[l])
         share(l)
@@ -290,6 +305,9 @@
         copy.wait()
     arrive(pall_ref.at[pl.ds(0, modes - 1)], pr.at[0])
 
+
+    pair = 2
+    count = pair * modes
 
     def block(m):
         return slice(m * side, (m + 1) * side)
@@ -304,7 +322,7 @@
             lo_ref[block(m), side : 2 * side] = il
 
     def two_sided(right_table, left_table, hi_ref, lo_ref):
-        for m in range(modes):
+        for m in range(count):
             bh, bl = tab_ref[2 * right_table], tab_ref[2 * right_table + 1]
             whole = dot(hi_ref[block(m)], bh) + dot(lo_ref[block(m)], bh) + dot(hi_ref[block(m)], bl)
             hi, lo = split_parts(whole)
@@ -314,20 +332,29 @@
             c_lo[side : 2 * side, block(m)] = lo[:, side : 2 * side]
         lh, ll = tab_ref[2 * left_table], tab_ref[2 * left_table + 1]
         out = []
-        for h in range(modes // 2):
+        for h in range(count // 2):
             cut = slice(h * 2 * side, (h + 1) * 2 * side)
             whole = dot(lh, c_hi[:, cut]) + dot(lh, c_lo[:, cut]) + dot(ll, c_hi[:, cut])
             for k in range(2):
                 out.append((whole[0:side, block(k)], whole[side : 2 * side, block(k)]))
         return out
 
-    def patch(l, p):
+    def patch(l, p, n):
         arrive(x_ref.at[l, pl.ds(0, modes - 1), p], xr.at[l, p])
         row, col = pos_ref[0, q * npos + p], pos_ref[1, q * npos + p]
         for part in range(2):
             whole = jnp.concatenate([x_ref[l, k, p, part].astype(jnp.float32) for k in range(modes)], axis=0)
             whole = pltpu.roll(whole, (side - row) & (side - 1), 0)
-            planes_ref[part] = pltpu.roll(whole, (side - (col & (side - 1))) & (side - 1), 1)
+            planes_ref[n, part] = pltpu.roll(whole, (side - (col & (side - 1))) & (side - 1), 1)
+
+    def plane(n):
+        return planes_ref[n, 0], planes_ref[n, 1]
+
+    def wave(p, m):
+        return wave_ref[p, m, 0], wave_ref[p, m, 1]
+
+    def shone(m):
+        return pall_ref[m, 0], pall_ref[m, 1]
 
     def times(wave, field):
         (wr, wi), (fr, fi) = wave, field
@@ -340,63 +367,85 @@
     def e_copy(l, k, p, mode, target):
         return send(ebuf.at[l, k, p], eq_ref[l].at[target, p], es.at[l], er.at[l], here, mode)
 
-    def hand_out(l, p, total):
+    def hand_out(l, p, n, total):
         row, col = pos_ref[0, q * npos + p], pos_ref[1, q * npos + p]
         for part in range(2):
-            sum_ref[part] = pltpu.roll(pltpu.roll(total[part], row & (side - 1), 0), col & (side - 1), 1)
+            sum_ref[n, part] = pltpu.roll(pltpu.roll(total[part], row & (side - 1), 0), col & (side - 1), 1)
+        def coded(mode):
+            value = sum_ref[n, :, pl.ds(pl.multiple_of(mode * quarter, quarter), quarter)]
+            step = column_scale(value)
+            return encode(value, step), step
+
         for k in range(modes - 1):
-            cut = pl.ds(pl.multiple_of(others[k] * quarter, quarter), quarter)
+            ebuf[l, k, p], e_out[l, k, pl.ds(p, 1)] = coded(others[k])
+            e_copy(l, k, p, others[k], q).start()
+        eq_ref[l][q, p], e_steps[l][q, pl.ds(p, 1)] = coded(q)
+
+    def hand_out_steps(l):
+        for k, m in enumerate(others):
+            go(send(e_out.at[l, k], e_steps[l].at[q], ess.at[l], esr.at[l], here, m))
+
+    def each(i):
+        return [(n, i * pair + n, m) for n in range(pair) for m in range(modes)]
+
+    def enter(i, carry):
+        for n in range(pair):
+            patch(0, i * pair + n, n)
             for part in range(2):
-                ebuf[l, k, p, part] = sum_ref[part, cut]
-            e_copy(l, k, p, others[k], q).start()
-        cut = pl.ds(pl.multiple_of(q * quarter, quarter), quarter)
-        for part in range(2):
-            eq_ref[l][q, p, part] = sum_ref[part, cut]
-
-    def enter(p, carry):
-        patch(0, p)
-        for part in range(2):
-            xroll[p, part] = planes_ref[part]
-        load(a_hi, a_lo, [times((pall_ref[m, 0], pall_ref[m, 1]), (planes_ref[0], planes_ref[1])) for m in range(modes)])
-        for m, (re, im) in enumerate(two_sided(2, 3, a_hi, a_lo)):
+                xroll[i * pair + n, part] = planes_ref[n, part]
+        load(a_hi, a_lo, [times(shone(m), plane(n)) for n, p, m in each(i)])
+        for (n, p, m), (re, im) in zip(each(i), two_sided(2, 3, a_hi, a_lo)):
             wave_ref[p, m, 0] = re
             wave_ref[p, m, 1] = im
         return carry
 
-    lax.fori_loop(0, npos, enter, 0)
-
-    def detect(p, carry):
-        patch(1, p)
-        load(a_hi, a_lo, [times((wave_ref[p, m, 0], wave_ref[p, m, 1]), (planes_ref[0], planes_ref[1])) for m in range(modes)])
+    def summed(terms):
+        return [functools.reduce(jnp.add, part) for part in zip(*terms)]
+
+    def detect(i, carry):
+        for n in range(pair):
+            patch(1, i * pair + n, n)
+        load(a_hi, a_lo, [times(wave(p, m), plane(n)) for n, p, m in each(i)])
         far = two_sided(0, 1, a_hi, a_lo)
-        intensity = background
-        for re, im in far:
-            intensity = intensity + (re * re + im * im)
-        weight = 1.0 - counts_ref[p].astype(jnp.float32) / intensity
-        load(a_hi, a_lo, [(weight * re, weight * im) for re, im in far])
+        weighted = []
+        for n in range(pair):
+            mine_far = far[n * modes : (n + 1) * modes]
+            intensity = background
+            for re, im in mine_far:
+                intensity = intensity + (re * re + im * im)
+            weight = 1.0 - counts_ref[i * pair + n].astype(jnp.float32) / intensity
+            weighted.extend((weight * re, weight * im) for re, im in mine_far)
+        load(a_hi, a_lo, weighted)
         grads = two_sided(1, 0, a_hi, a_lo)
-        load(b_hi.at[p], b_lo.at[p], [conj_times((planes_ref[0], planes_ref[1]), grad) for grad in grads])
-        terms = [conj_times((wave_ref[p, m, 0], wave_ref[p, m, 1]), grad) for m, grad in enumerate(grads)]
-        hand_out(1, p, [functools.reduce(jnp.add, part) for part in zip(*terms)])
+        load(b_hi.at[i], b_lo.at[i], [conj_times(plane(n), grad) for (n, p, m), grad in zip(each(i), grads)])
+        terms = [conj_times(wave(p, m), grad) for (n, p, m), grad in zip(each(i), grads)]
+        for n in range(pair):
+            hand_out(1, i * pair + n, n, summed(terms[n * modes : (n + 1) * modes]))
         return carry
 
-    lax.fori_loop(0, npos, detect, 0)
+    def leave(i, carry):
+        grads = two_sided(3, 2, b_hi.at[i], b_lo.at[i])
+        for m in range(modes):
+            terms = [conj_times((xroll[p, 0], xroll[p, 1]), grad) for (n, p, k), grad in zip(each(i), grads) if k == m]
+            for part, term in enumerate(summed(terms)):
+                pp_ref[m, part * side : (part + 1) * side] += term
+        terms = [conj_times(shone(m), grad) for (n, p, m), grad in zip(each(i), grads)]
+        for n in range(pair):
+            hand_out(0, i * pair + n, n, summed(terms[n * modes : (n + 1) * modes]))
+        return carry
+
+    lax.fori_loop(0, npos // pair, enter, 0)
+    e_out[...] = jnp.zeros_like(e_out)
+    lax.fori_loop(0, npos // pair, detect, 0)
+    hand_out_steps(1)
     pp_ref[...] = jnp.zeros_like(pp_ref)
-
-    def leave(p, carry):
-        grads = two_sided(3, 2, b_hi.at[p], b_lo.at[p])
-        for m, grad in enumerate(grads):
-            for part, term in enumerate(conj_times((xroll[p, 0], xroll[p, 1]), grad)):
-                pp_ref[m, part * side : (part + 1) * side] += term
-        terms = [conj_times((pall_ref[m, 0], pall_ref[m, 1]), grad) for m, grad in enumerate(grads)]
-        hand_out(0, p, [functools.reduce(jnp.add, part) for part in zip(*terms)])
-        return carry
-
-    lax.fori_loop(0, npos, leave, 0)
+    lax.fori_loop(0, npos // pair, leave, 0)
+    hand_out_steps(0)
 
 
     def gather_e(l):
         arrive(eq_ref[l].at[pl.ds(0, modes - 1)], er.at[l])
+        arrive(e_steps[l].at[pl.ds(0, modes - 1)], esr.at[l])
 
     def lay(l):
         blank = jnp.zeros(shape, jnp.float32)
@@ -408,7 +457,7 @@
             j = pick_ref[4, 0, n]
             kept = cols >= (pos_ref[1, j] & (side - 1))
             upper = rows >= pos_ref[0, j]
-            term = eq_ref[l][j // npos, j % npos]
+            term = decode(eq_ref[l][j // npos, j % npos]) * e_steps[l][j // npos, pl.ds(j % npos, 1)]
             lefts, rights = jnp.where(kept, term, 0.0), jnp.where(kept, 0.0, term)
             for sums, part in ((left_sum[l], lefts), (right_sum[l], rights)):
                 sums[0, n + 1] = sums[0, n] + jnp.where(upper, part, 0.0)
@@ -459,108 +508,126 @@
             giver = pick_ref[1, place, n]
             total = total + decode(rbuf[l][r][giver]) * rscale[l][giver, pl.ds(place, 1)]
             given[n + 1] = total
+        received = received()
         start = 0
         for k in range(tile_dev):
             end = pick_ref[2, place, k]
             value = given[end] - given[start]
-            for ref, ref_scale in received:
-                value = value + decode(ref[k]) * ref_scale[k : k + 1]
+            for ref, ref_scale, held in received:
+                if k in held:
+                    value = value + decode(ref[k]) * ref_scale[k : k + 1]
             use(k, value)
             start = end
 
-    def ship(l, direction, step, r, received):
+    def ship(l, direction, step, tiles):
         at = (l, direction, step)
-        buf, to = out_of[l][direction][step], into[l][direction][step]
-
-        def pack(k, value):
-            step_size = column_scale(value)
-            sscale[l, direction, step, k : k + 1] = step_size
-            buf[k] = encode(value, step_size)
-
-        combine(l, r, received, pack)
+        buf, to = out_of[l][direction][step].at[tiles], into[l][direction][step].at[tiles]
         scan = (right, left)[direction]
         return (
             go(send(sscale.at[at], zscale.at[at], ucs.at[l], ucr.at[at], scan, q)),
             go(send(buf, to, us.at[l], ur.at[at], scan, q)),
         )
 
+    def packer(l, direction, step):
+        def pack(k, value):
+            side_of = (k // half_dev) if direction is None else direction
+            step_size = column_scale(value)
+            sscale[l, side_of, step, k : k + 1] = step_size
+            out_of[l][side_of][step][k] = encode(value, step_size)
+
+        return pack
+
     flying = {}
+    half_dev = tile_dev // 2
+    halves = (pl.ds(0, half_dev), pl.ds(half_dev, half_dev))
 
     def arrived(l, direction, step):
-        if (l, direction) not in flying:
-            return []
         for copy in flying[l, direction]:
             copy.wait_recv()
-        return [(into[l][direction][step - 1], zscale.at[l, direction, step - 1])]
+        held = range(direction * half_dev, (direction + 1) * half_dev) if step == 1 else range(tile_dev)
+        return [(into[l][direction][step - 1], zscale.at[l, direction, step - 1], held)]
 
     def turn(l, step):
         if step == 0:
             await_scales(l)
             await_up(l, 0)
-            flying[l, l] = ship(l, l, 0, 0, [])
+            for scan_side in range(2):
+                sscale[l, scan_side, 0] = jnp.zeros_like(sscale[l, scan_side, 0])
+            combine(l, 0, lambda: [], packer(l, None, 0))
+            for direction in (0, 1):
+                flying[l, direction] = ship(l, direction, 0, halves[direction])
             return
-        for direction in (l, 1 - l):
+        for direction in (0, 1):
             r = 2 * step - 1 + direction
             await_up(l, r)
-            flying[l, direction] = ship(l, direction, step, r, arrived(l, direction, step))
+            combine(l, r, lambda: arrived(l, direction, step), packer(l, direction, step))
+            flying[l, direction] = ship(l, direction, step, pl.ds(0, tile_dev))
+
+    def probe_over_modes():
+        arrive(pxb, p0r.at[0])
+        total = pp_ref[q]
+        for k in range(modes - 1):
+            total = total + pxb[k]
+        pxs[...] = total.reshape(pxs.shape)
+        for n, scan, d in peers:
+            go(send(pxs.at[d], pyb.at[n], p1s.at[0], p1r.at[0], scan, q))
+
+    def probe_over_plane():
+        arrive(pyb, p1r.at[0])
+        total = pxs[mine]
+        for n in range(7):
+            total = total + pyb[n]
+        pzs[...] = total
+        for k, scan in enumerate(column):
+            go(send(pzs, pzb.at[k], p2s.at[0], p2r.at[0], scan, q))
+
+    def probe_over_ring():
+        arrive(pzb, p2r.at[0])
+        total = pzs[...]
+        for k in range(RING - 1):
+            total = total + pzb[k]
+        pg_ref[mine] = total * scale
+        for n, scan, d in peers:
+            go(send(pg_ref.at[mine], pg_ref.at[mine], p3s.at[0], p3r.at[0], scan, q))
+
+    def keep(l):
+        def put(k, value):
+            out_ref[k, l] = value
+
+        return put
 
     gather_e(1)
     lay(1)
     code(1)
-    for r in range(3):
+    for r in range(5):
         yield_up(1, r)
     for k, m in enumerate(others):
         go(send(pp_ref.at[m], pxb.at[k], p0s.at[0], p0r.at[0], here, m))
     gather_e(0)
     lay(0)
+    turn(1, 0)
     code(0)
-    for r in range(3):
+    for r in range(5):
         yield_up(0, r)
-    turn(1, 0)
-    yield_up(1, 3)
-    yield_up(1, 4)
+    turn(1, 1)
     turn(0, 0)
-    yield_up(0, 3)
-    yield_up(0, 4)
-    turn(1, 1)
     yield_up(1, 5)
     yield_up(1, 6)
+    probe_over_modes()
     turn(0, 1)
     yield_up(0, 5)
     yield_up(0, 6)
-    total = pp_ref[q]
-    arrive(pxb, p0r.at[0])
-    for k in range(modes - 1):
-        total = total + pxb[k]
-    pxs[...] = total.reshape(pxs.shape)
-    for n, scan, d in peers:
-        go(send(pxs.at[d], pyb.at[n], p1s.at[0], p1r.at[0], scan, q))
     turn(1, 2)
     yield_up(1, 7)
+    probe_over_plane()
     turn(0, 2)
     yield_up(0, 7)
-    total = pxs[mine]
-    arrive(pyb, p1r.at[0])
-    for n in range(7):
-        total = total + pyb[n]
-    pzs[...] = total
-    for k, scan in enumerate(column):
-        go(send(pzs, pzb.at[k], p2s.at[0], p2r.at[0], scan, q))
     turn(1, 3)
+    probe_over_ring()
     turn(0, 3)
-    arrive(pzb, p2r.at[0])
-    for k in range(RING - 1):
-        total = total + pzb[k]
-    pg_ref[mine] = total * scale
-    for n, scan, d in peers:
-        go(send(pg_ref.at[mine], pg_ref.at[mine], p3s.at[0], p3r.at[0], scan, q))
     for l in (1, 0):
         await_up(l, 7)
-
-        def keep(k, value, l=l):
-            out_ref[k, l] = value
-
-        combine(l, 7, arrived(l, 0, 4) + arrived(l, 1, 4), keep)
+        combine(l, 7, lambda: arrived(l, 0, 4) + arrived(l, 1, 4), keep(l))
     arrive(pg_ref.at[pl.ds(0, 7)], p3r.at[0])
 
     def departed(ref, sem):
@@ -571,10 +638,11 @@
         departed(ybuf.at[l], ys.at[l])
         departed(xbuf.at[l], xs.at[l])
         departed(ebuf.at[l], es.at[l])
+        departed(e_out.at[l], ess.at[l])
         departed(codes.at[l, pl.ds(0, 7)], ts.at[l])
         departed(cscale.at[l, pl.ds(0, 7)], tcs.at[l])
         departed(codes.at[l, pl.ds(0, 7)], us.at[l])
-        departed(cscale.at[l, pl.ds(0, 7)], ucs.at[l])
+        departed(cscale.at[l], ucs.at[l])
     departed(pall_ref.at[pl.ds(0, modes - 1)], ps.at[0])
     departed(pxb, p0s.at[0])
     departed(pyb, p1s.at[0])
@@ -609,20 +677,23 @@
         wide(modes, parts, side, side),
         pltpu.VMEM((npos, side, side), counts.dtype),
         half(*tables.shape),
-        wide(slices, modes - 1, npos, *tile),
-        wide(modes, npos, *tile),
-        wide(modes, npos, *tile),
+        short(slices, modes - 1, npos, *tile),
+        short(modes, npos, *tile),
+        short(modes, npos, *tile),
+        wide(modes, 8, side),
+        wide(modes, 8, side),
+        wide(slices, modes - 1, 8, side),
         wide(modes, parts * side, side),
-        half(modes * side, 2 * side),
-        half(modes * side, 2 * side),
-        half(npos, modes * side, 2 * side),
-        half(npos, modes * side, 2 * side),
-        half(2 * side, modes * side),
-        half(2 * side, modes * side),
-        wide(parts, side, side),
+        half(2 * modes * side, 2 * side),
+        half(2 * modes * side, 2 * side),
+        half(npos // 2, 2 * modes * side, 2 * side),
+        half(npos // 2, 2 * modes * side, 2 * side),
+        half(2 * side, 2 * modes * side),
+        half(2 * side, 2 * modes * side),
+        wide(2, parts, side, side),
         wide(npos, parts, side, side),
         wide(npos, modes, parts, side, side),
-        wide(parts, side, side),
+        wide(2, parts, side, side),
     ]
     scratch += [wide(2, batch + 1, *tile)] * 4
     scratch += [short(8, *tile)] * 16 + [wide(8, RING, side)] * 2
@@ -642,7 +713,7 @@
         pltpu.SMEM((5, RING, side), jnp.int32),
     ]
     sizes = [(6,), (slices,), (slices, 2, 4), (slices,), (slices,), (slices,), (slices, npos)]
-    sizes += [(1,), (1,), (slices,), (slices,)]
+    sizes += [(1,), (1,), (slices,), (slices,), (slices,), (slices,)]
     sizes += [(slices,), (slices, RING), (slices,), (slices,), (slices,), (slices, 2, 4), (slices,), (slices, 2, 4)]
     sizes += [(1,)] * 8
     scratch += [dma(size) for size in sizes]

time: 100 us -> 96.5 us (0.965)
  Pallas kernels: 96.9 us -> 93.1 us
    pallas_call x1, Pallas kernels: 96.9 us -> 93.1 us  [gradients(): pl.pallas_call(functools.partial(kernel_body, scale=scale), in_specs=[sme...]
where the time goes in v7:
time: 96.5 us; the launch traced here: 96.3 us
  Pallas kernels  93.1 us (96%)
  local copies, waits for them, and re-layouts  2.58 us (3%)
    pallas_call x1, Pallas kernels, gradients(): pl.pallas_call(functools.partial(kernel_body, scale=scale), in_specs=[sme...  93.1 us
    unnamed x4, local copies, waits for them, and re-layouts  2.58 us

profile of v7, /device:TPU:1, one launch (start us, length us, event | category | flops | bytes accessed | tf_op | source)
XLA Modules:
  0.0 96.3 jit_solution(1742386912977058051)
XLA Ops:
  0.6 93.1 %gradients.1 = (f32[8,2,2,32,128]{4,3,2,1,0:T(8,128)}, f32[8,32,128]{2,1,0:T(8,128)}) custom-call(s32[512]{0:T(512)} %owner_ref.1, s32[64,64]{1,0:T(8,128)} %first_ref.1, s32[2,16]{1,0:T(2,128)} %bitcast.5, s32[4,128]{1,0:T(4,128)} %bitcast.4, bf16[8,2,2,128,128]{4,3,2,1,0:T(8,128)(2,1)} %obj_ref.1, f32[1,2,128,128]{3,2,1,0:T(8,128)} %probe_ref.1, ...), custom_call_target="tpu_custom_call" | custom-call | tf_op jit(solution)/shard_map/gradients/pallas_call | solution.py:720
  93.7 0.0 copy-start
  93.7 1.9 %copy.11 = f32[8,2,2,32,128]{4,3,2,1,0:T(8,128)} copy(f32[8,2,2,32,128]{4,3,2,1,0:T(8,128)} %get-tuple-element.8) | data formatting | bytes 1048576
  95.6 0.0 copy-done
  95.7 0.7 copy.12
Async XLA Ops:
  93.7 1.9 %copy-start = (f32[8,32,128]{2,1,0:T(8,128)S(1)}, f32[8,32,128]{2,1,0:T(8,128)}, u32[]{:S(2)}) copy-start(f32[8,32,128]{2,1,0:T(8,128)} %get-tuple-element.5) | copy-start | bytes 393220

commit v8 on v7

--- a/solution.py
+++ b/solution.py
@@ -599,7 +599,7 @@
     gather_e(1)
     lay(1)
     code(1)
-    for r in range(5):
+    for r in range(3):
         yield_up(1, r)
     for k, m in enumerate(others):
         go(send(pp_ref.at[m], pxb.at[k], p0s.at[0], p0r.at[0], here, m))
@@ -607,13 +607,17 @@
     lay(0)
     turn(1, 0)
     code(0)
-    for r in range(5):
+    for r in range(3):
         yield_up(0, r)
+    yield_up(1, 3)
+    yield_up(1, 4)
     turn(1, 1)
     turn(0, 0)
+    yield_up(0, 3)
+    yield_up(0, 4)
+    probe_over_modes()
     yield_up(1, 5)
     yield_up(1, 6)
-    probe_over_modes()
     turn(0, 1)
     yield_up(0, 5)
     yield_up(0, 6)

time: 96.5 us -> 95.7 us (level)
  no operation moved by 1% of the time
where the time goes in v8:
time: 95.7 us; the launch traced here: 95.5 us
  Pallas kernels  92.3 us (96%)
  local copies, waits for them, and re-layouts  2.58 us (3%)
    pallas_call x1, Pallas kernels, gradients(): pl.pallas_call(functools.partial(kernel_body, scale=scale), in_specs=[sme...  92.3 us
    unnamed x4, local copies, waits for them, and re-layouts  2.58 us

profile of v8, /device:TPU:1, one launch (start us, length us, event | category | flops | bytes accessed | tf_op | source)
XLA Modules:
  0.0 95.5 jit_solution(15797677411000463664)
XLA Ops:
  0.6 92.3 %gradients.1 = (f32[8,2,2,32,128]{4,3,2,1,0:T(8,128)}, f32[8,32,128]{2,1,0:T(8,128)}) custom-call(s32[512]{0:T(512)} %owner_ref.1, s32[64,64]{1,0:T(8,128)} %first_ref.1, s32[2,16]{1,0:T(2,128)} %bitcast.5, s32[4,128]{1,0:T(4,128)} %bitcast.4, bf16[8,2,2,128,128]{4,3,2,1,0:T(8,128)(2,1)} %obj_ref.1, f32[1,2,128,128]{3,2,1,0:T(8,128)} %probe_ref.1, ...), custom_call_target="tpu_custom_call" | custom-call | tf_op jit(solution)/shard_map/gradients/pallas_call | solution.py:724
  92.9 0.0 copy-start
  92.9 1.9 %copy.11 = f32[8,2,2,32,128]{4,3,2,1,0:T(8,128)} copy(f32[8,2,2,32,128]{4,3,2,1,0:T(8,128)} %get-tuple-element.8) | data formatting | bytes 1048576
  94.8 0.0 copy-done
  94.8 0.7 copy.12
Async XLA Ops:
  92.9 1.9 %copy-start = (f32[8,32,128]{2,1,0:T(8,128)S(1)}, f32[8,32,128]{2,1,0:T(8,128)}, u32[]{:S(2)}) copy-start(f32[8,32,128]{2,1,0:T(8,128)} %get-tuple-element.5) | copy-start | bytes 393220

commit v9 on v8

--- a/solution.py
+++ b/solution.py
@@ -624,10 +624,10 @@
     turn(1, 2)
     yield_up(1, 7)
     probe_over_plane()
+    yield_up(0, 7)
     turn(0, 2)
-    yield_up(0, 7)
+    probe_over_ring()
     turn(1, 3)
-    probe_over_ring()
     turn(0, 3)
     for l in (1, 0):
         await_up(l, 7)

time: 95.7 us -> 95.1 us (level)
  no operation moved by 1% of the time
where the time goes in v9:
time: 95.1 us; the launch traced here: 94.9 us
  Pallas kernels  91.7 us (96%)
  local copies, waits for them, and re-layouts  2.58 us (3%)
    pallas_call x1, Pallas kernels, gradients(): pl.pallas_call(functools.partial(kernel_body, scale=scale), in_specs=[sme...  91.7 us
    unnamed x4, local copies, waits for them, and re-layouts  2.58 us

profile of v9, /device:TPU:1, one launch (start us, length us, event | category | flops | bytes accessed | tf_op | source)
XLA Modules:
  0.0 94.9 jit_solution(11971469701518280597)
XLA Ops:
  0.6 91.7 %gradients.1 = (f32[8,2,2,32,128]{4,3,2,1,0:T(8,128)}, f32[8,32,128]{2,1,0:T(8,128)}) custom-call(s32[512]{0:T(512)} %owner_ref.1, s32[64,64]{1,0:T(8,128)} %first_ref.1, s32[2,16]{1,0:T(2,128)} %bitcast.5, s32[4,128]{1,0:T(4,128)} %bitcast.4, bf16[8,2,2,128,128]{4,3,2,1,0:T(8,128)(2,1)} %obj_ref.1, f32[1,2,128,128]{3,2,1,0:T(8,128)} %probe_ref.1, ...), custom_call_target="tpu_custom_call" | custom-call | tf_op jit(solution)/shard_map/gradients/pallas_call | solution.py:724
  92.3 0.0 copy-start
  92.3 1.9 %copy.11 = f32[8,2,2,32,128]{4,3,2,1,0:T(8,128)} copy(f32[8,2,2,32,128]{4,3,2,1,0:T(8,128)} %get-tuple-element.8) | data formatting | bytes 1048576
  94.3 0.0 copy-done
  94.3 0.7 copy.12
Async XLA Ops:
  92.3 1.9 %copy-start = (f32[8,32,128]{2,1,0:T(8,128)S(1)}, f32[8,32,128]{2,1,0:T(8,128)}, u32[]{:S(2)}) copy-start(f32[8,32,128]{2,1,0:T(8,128)} %get-tuple-element.5) | copy-start | bytes 393220
